TPU v7x, 256 devices: a whole 4x4x8 slice. The times are simulated.
256 devices in a mesh: grp: 4 (over z_lo), tile: 32 (over x, y, z_hi), cores: 2 (over core).
Axes of the slice: x: 4, y: 4, z: 8 (z_hi: 2, z_lo: 4; z = z_hi * 4 + z_lo), core: 2. Of those that a mesh axis runs over, the one named last changes fastest.
Arguments:
- trial_collection: float32 [32, 3, 1024, 1024], P('grp', None, 'tile', 'cores'), may hold values from -6 to 6
- seabed_profile: float32 [1024, 1024], P('tile', 'cores'), may hold values from 0.4 to 1.8
- observed: float32 [4096], P(('grp', 'tile', 'cores')), may hold values from -6 to 6
- variances: float32 [4096], P(('grp', 'tile', 'cores')), may hold values from 4 to 40
- perturbations: float32 [4096, 32], P(('grp', 'tile', 'cores')), may hold values from -6 to 6
- stencil_cells: int32 [4096, 4], P(('grp', 'tile', 'cores')), may hold values from 0 to 4095, as said below
- stencil_weights: float32 [4096, 4], P(('grp', 'tile', 'cores')), may hold values from 0.1 to 0.5
- region_mask: int32 [4096, 8], P(('grp', 'tile', 'cores')), may hold values from 0 to 1, as said below
Outputs:
- propagated_trials: float32 [32, 3, 1024, 1024], P('grp', None, 'tile', 'cores')
- analysis_updates: float32 [32, 3, 1024, 1024], P('grp', None, 'tile', 'cores')
Inputs may be any that keep to these rules, and one draw needn't show every extreme that they name: `stencil_cells`: each observation's four entries are s, s + 1, s + 512, s + 513 for a cell s of its block in a row below 7 and a column below 511; in every block the first observation has s = 3582 and the second s = 0. `region_mask`: an observation counts in the region that holds its block's rows, in each region next to that one or not, and in no other.
All inputs are finite; a program needn't handle non-finite values.
Results may differ from a plain program's by a relative error of at most 0.00018.
Values sent between devices are 32-bit elements; how exact they have to be, the bound alone decides.
No kernel may reach another device: no remote copies, remote signals or barrier semaphores. Data moves between devices by JAX's collectives and lax.ppermute only.
A program may use at most 64 MiB of HBM per device.

v0:
```python
import jax
import jax.numpy as jnp
from jax import lax
from jax.sharding import PartitionSpec as P

STEPS = 3
REG = 8


FRICTION = 0.02
HIGHEST = lax.Precision.HIGHEST


def extended(block, sides, width):
    for axis, dim in sides:
        count = lax.axis_size(axis)
        forward = [(i, i + 1) for i in range(count - 1)]
        backward = [(target, source) for source, target in forward]
        low = lax.ppermute(
            lax.slice_in_dim(block, block.shape[dim] - width, None, axis=dim), axis, forward
        )
        high = lax.ppermute(lax.slice_in_dim(block, 0, width, axis=dim), axis, backward)
        block = jnp.concatenate([low, block, high], axis=dim)
    return block


def edge_rims(field):
    return extended(field, (("tile", 1), ("cores", 2)), 1)


def advance_block(free_elevation, zonal_speed, meridional_speed, seabed_profile, widen):
    members = free_elevation.shape[0]
    fluxes = widen(
        jnp.concatenate(
            [seabed_profile[None] * zonal_speed, seabed_profile[None] * meridional_speed], axis=0
        )
    )
    flux_east = fluxes[:members]
    flux_north = fluxes[members:]
    spread = 0.5 * (flux_east[:, 2:, 1:-1] - flux_east[:, :-2, 1:-1]) + 0.5 * (
        flux_north[:, 1:-1, 2:] - flux_north[:, 1:-1, :-2]
    )
    free_elevation = free_elevation - spread
    padded = widen(free_elevation)
    zonal_speed = (1.0 - FRICTION) * zonal_speed - 0.5 * (
        padded[:, 2:, 1:-1] - padded[:, :-2, 1:-1]
    )
    meridional_speed = (1.0 - FRICTION) * meridional_speed - 0.5 * (
        padded[:, 1:-1, 2:] - padded[:, 1:-1, :-2]
    )
    return (free_elevation, zonal_speed, meridional_speed)


def sense(block, stencil_cells, stencil_weights):
    flat = block.reshape(block.shape[0], -1)
    picked_components = jnp.take(flat, stencil_cells, axis=1)
    return jnp.sum(picked_components * stencil_weights[None], axis=2)


def local_products(observed_state, observed, variances, perturbations, region_mask):
    centre = jnp.mean(observed_state, axis=0)
    anomaly_obs = observed_state - centre[None]
    innovation = observed[None] + jnp.sqrt(variances)[None] * perturbations.T - observed_state
    scaled = anomaly_obs / variances[None]
    paired = jnp.concatenate([anomaly_obs, innovation], axis=0)
    return jnp.einsum(
        "or,eo,go->reg", region_mask.astype(jnp.float32), scaled, paired, precision=HIGHEST
    )


def solve_one(triangle, target):
    return jax.scipy.linalg.cho_solve((triangle, True), target)


def transform(products):
    members = products.shape[1]
    system = products[:, :, :members] + (members - 1.0) * jnp.eye(members, dtype=jnp.float32)[None]
    factor = jnp.linalg.cholesky(system)
    return jax.vmap(solve_one)(factor, products[:, :, members:])


def on_device(
    trial_collection,
    seabed_profile,
    observed,
    variances,
    perturbations,
    stencil_cells,
    stencil_weights,
    region_mask,
):
    rows_here = trial_collection.shape[2]
    free_elevation = trial_collection[:, 0]
    zonal_speed = trial_collection[:, 1]
    meridional_speed = trial_collection[:, 2]
    for repeat in range(STEPS):
        free_elevation, zonal_speed, meridional_speed = advance_block(
            free_elevation, zonal_speed, meridional_speed, seabed_profile, edge_rims
        )
    propagated_trials = jnp.stack([free_elevation, zonal_speed, meridional_speed], axis=1)
    group_id = lax.axis_index("grp")
    tile_id = lax.axis_index("tile")
    block_rows = rows_here // lax.axis_size("grp")
    region_rows = rows_here * lax.axis_size("tile") // REG
    propagated_quantities = lax.all_to_all(
        propagated_trials, "grp", split_axis=2, concat_axis=0, tiled=True
    )
    observed_state = sense(propagated_quantities[:, 0], stencil_cells, stencil_weights)
    products = lax.psum(
        local_products(observed_state, observed, variances, perturbations, region_mask),
        ("grp", "tile", "cores"),
    )
    weights = transform(products)
    region_id = (tile_id * rows_here + group_id * block_rows) // region_rows
    chosen = lax.dynamic_index_in_dim(weights, region_id, 0, keepdims=False)
    trial_anomalies = propagated_quantities - jnp.mean(propagated_quantities, axis=0, keepdims=True)
    block_increments = jnp.einsum("fkxy,fe->ekxy", trial_anomalies, chosen, precision=HIGHEST)
    analysis_updates = lax.all_to_all(
        block_increments, "grp", split_axis=0, concat_axis=2, tiled=True
    )
    return (propagated_trials, analysis_updates)


def solution(mesh):
    in_specs = (
        P("grp", None, "tile", "cores"),
        P("tile", "cores"),
        P(("grp", "tile", "cores")),
        P(("grp", "tile", "cores")),
        P(("grp", "tile", "cores"), None),
        P(("grp", "tile", "cores"), None),
        P(("grp", "tile", "cores"), None),
        P(("grp", "tile", "cores"), None),
    )
    out_specs = (P("grp", None, "tile", "cores"), P("grp", None, "tile", "cores"))
    return jax.shard_map(
        on_device, mesh=mesh, in_specs=in_specs, out_specs=out_specs, check_vma=False
    )
```

profile of v0, /device:TPU:38, one launch (start us, length us, event | category | flops | bytes accessed | tf_op | source)
XLA Modules:
  0.0 541.3 jit_solution(17866130877956921308)
XLA Ops:
  7.2 1.5 fusion.59
  9.3 10.9 %collective-permute-start = (f32[16,1,512]{2,0,1:T(8,128)S(1)}, f32[16,1,512]{2,0,1:T(8,128)S(1)}, u32[]{:S(2)}, u32[]{:S(2)}) collective-permute-start(f32[16,1,512]{2,0,1:T(8,128)S(1)} %get-tuple-element.30), channel_id=1, source_target_pairs={{2,0},{4,2},{6,4},{8,6},{10,8},{12,10},{14,12},{16,14},{18,16},{20... | collective-permute-start | bytes 98312 | tf_op jit(solution)/shard_map/ppermute | solution.py:22
  20.3 1.9 collective-permute-start.1
  22.2 10.8 %collective-permute-done.1 = f32[16,1,512]{2,0,1:T(8,128)S(1)} collective-permute-done((f32[16,1,512]{2,0,1:T(8,128)S(1)}, f32[16,1,512]{2,0,1:T(8,128)S(1)}, u32[]{:S(2)}, u32[]{:S(2)}) %collective-permute-start.1) | collective-permute-done | bytes 32800 | tf_op jit(solution)/shard_map/ppermute | solution.py:19
  33.1 1.3 collective-permute-start.2
  34.4 3.1 collective-permute-start.3
  37.5 1.1 collective-permute-done.3
  39.1 1.9 collective-permute-start.4
  41.1 7.8 %collective-permute-start.5 = (f32[8,1,512]{2,0,1:T(8,128)S(1)}, f32[8,1,512]{2,0,1:T(8,128)S(1)}, u32[]{:S(2)}, u32[]{:S(2)}) collective-permute-start(f32[8,1,512]{2,0,1:T(8,128)S(1)} %get-tuple-element.45), channel_id=1, source_target_pairs={{0,2},{2,4},{4,6},{6,8},{8,10},{10,12},{12,14},{14,16},{16,18},{18... | collective-permute-start | bytes 49160 | tf_op jit(solution)/shard_map/ppermute | solution.py:19
  48.9 4.7 collective-permute-done.5
  53.7 1.3 collective-permute-start.6
  55.0 3.0 collective-permute-start.7
  59.9 3.1 collective-permute-start.8
  63.0 6.7 %collective-permute-start.9 = (f32[16,1,512]{2,0,1:T(8,128)S(1)}, f32[16,1,512]{2,0,1:T(8,128)S(1)}, u32[]{:S(2)}, u32[]{:S(2)}) collective-permute-start(f32[16,1,512]{2,0,1:T(8,128)S(1)} %get-tuple-element.27), channel_id=1, source_target_pairs={{0,2},{2,4},{4,6},{6,8},{8,10},{10,12},{12,14},{14,16},{16,18},{18... | collective-permute-start | bytes 98312 | tf_op jit(solution)/shard_map/ppermute | solution.py:19
  69.7 6.2 %collective-permute-done.9 = f32[16,1,512]{2,0,1:T(8,128)S(1)} collective-permute-done((f32[16,1,512]{2,0,1:T(8,128)S(1)}, f32[16,1,512]{2,0,1:T(8,128)S(1)}, u32[]{:S(2)}, u32[]{:S(2)}) %collective-permute-start.9) | collective-permute-done | bytes 32800 | tf_op jit(solution)/shard_map/ppermute | solution.py:19
  76.1 1.3 collective-permute-start.10
  77.4 3.1 collective-permute-start.11
  82.0 1.9 collective-permute-start.12
  83.9 7.8 %collective-permute-start.13 = (f32[8,1,512]{2,0,1:T(8,128)S(1)}, f32[8,1,512]{2,0,1:T(8,128)S(1)}, u32[]{:S(2)}, u32[]{:S(2)}) collective-permute-start(f32[8,1,512]{2,0,1:T(8,128)S(1)} %get-tuple-element.43), channel_id=1, source_target_pairs={{0,2},{2,4},{4,6},{6,8},{8,10},{10,12},{12,14},{14,16},{16,18},{18... | collective-permute-start | bytes 49160 | tf_op jit(solution)/shard_map/ppermute | solution.py:19
  91.8 4.8 collective-permute-done.13
  96.7 1.3 collective-permute-start.14
  98.0 3.0 collective-permute-start.15
  102.4 2.5 collective-permute-start.16
  104.9 7.3 %collective-permute-start.17 = (f32[16,1,512]{2,0,1:T(8,128)S(1)}, f32[16,1,512]{2,0,1:T(8,128)S(1)}, u32[]{:S(2)}, u32[]{:S(2)}) collective-permute-start(f32[16,1,512]{2,0,1:T(8,128)S(1)} %get-tuple-element.25), channel_id=1, source_target_pairs={{0,2},{2,4},{4,6},{6,8},{8,10},{10,12},{12,14},{14,16},{16,18},{18... | collective-permute-start | bytes 98312 | tf_op jit(solution)/shard_map/ppermute | solution.py:19
  112.3 5.3 collective-permute-done.17
  117.8 1.3 collective-permute-start.18
  119.1 3.1 collective-permute-start.19
  123.7 1.9 collective-permute-start.20
  125.7 7.8 %collective-permute-start.21 = (f32[8,1,512]{2,0,1:T(8,128)S(1)}, f32[8,1,512]{2,0,1:T(8,128)S(1)}, u32[]{:S(2)}, u32[]{:S(2)}) collective-permute-start(f32[8,1,512]{2,0,1:T(8,128)S(1)} %get-tuple-element.41), channel_id=1, source_target_pairs={{0,2},{2,4},{4,6},{6,8},{8,10},{10,12},{12,14},{14,16},{16,18},{18... | collective-permute-start | bytes 49160 | tf_op jit(solution)/shard_map/ppermute | solution.py:19
  133.5 4.9 collective-permute-done.21
  138.5 1.3 collective-permute-start.22
  139.8 3.0 collective-permute-start.23
  144.5 1.3 pad_maximum_fusion
  145.7 4.2 all-to-all-start
  150.5 33.9 %all-to-all-done = f32[8,3,32,512]{3,0,1,2:T(8,128)S(1)} async-done(((f32[8,3,32,512]{3,0,1,2:T(8,128)}), f32[8,3,32,512]{3,0,1,2:T(8,128)S(1)}, u32[]{:S(2)}, u32[]{:S(2)}) %all-to-all-start) | async-done | bytes 1572896 | tf_op jit(solution)/shard_map/all_to_all | solution.py:105
  185.4 2.0 copy.127
  187.4 2.2 gather_fusion
  190.1 1.2 convolution_bitcast_fusion
  193.2 247.6 %all-reduce.2.cloned.1.call-done = f32[8,32,64]{1,2,0:T(8,128)} async-done(((f32[8,32,64]{1,2,0:T(8,128)}), f32[8,32,64]{1,2,0:T(8,128)}) %all-reduce.2.cloned.1.call-update) | async-done | bytes 65552 | tf_op jit(solution)/shard_map/psum | solution.py:109
  442.8 23.4 %custom-call.11 = f32[8,32,32]{2,1,0:T(8,128)S(1)} custom-call(f32[8,32,32]{2,1,0:T(8,128)S(1)} %fusion.44), custom_call_target="Cholesky" | custom-call | tf_op jit(solution)/shard_map/jit(cholesky)/cholesky | solution.py:78
  466.5 19.7 %custom-call.12 = f32[8,1,32,32]{2,3,1,0:T(8,128)S(1)} custom-call(f32[8,1,32,32]{3,2,1,0:T(8,128)S(1)} %select_bitcast_fusion), custom_call_target="InvertDiagBlocksLowerTriangular" | custom-call | tf_op jit(solution)/shard_map/vmap(jit(_cho_solve))/triangular_solve | solution.py:72
  486.2 1.3 fusion.39
  487.8 2.3 fusion
  490.1 2.1 copy.138
  492.2 6.3 %all-to-all-start.1 = ((f32[32,3,8,512]{3,2,1,0:T(8,128)}), f32[32,3,8,512]{3,2,1,0:T(8,128)S(1)}, u32[]{:S(2)}, u32[]{:S(2)}) async-start(f32[32,3,8,512]{3,2,1,0:T(8,128)} %copy.138), calls=%async_computation.1 | async-start | bytes 3145728 | tf_op jit(solution)/shard_map/all_to_all | solution.py:118
  498.4 3.5 copy.140
  501.9 31.2 %all-to-all-done.1 = f32[32,3,8,512]{3,2,1,0:T(8,128)S(1)} async-done(((f32[32,3,8,512]{3,2,1,0:T(8,128)}), f32[32,3,8,512]{3,2,1,0:T(8,128)S(1)}, u32[]{:S(2)}, u32[]{:S(2)}) %all-to-all-start.1) | async-done | bytes 1572896 | tf_op jit(solution)/shard_map/all_to_all | solution.py:118
  533.2 1.3 copy.170
  (83 shorter events, 16.1 us)
Async XLA Ops:
  7.2 1.5 copy-start
  9.3 12.9 %collective-permute-start = (f32[16,1,512]{2,0,1:T(8,128)S(1)}, f32[16,1,512]{2,0,1:T(8,128)S(1)}, u32[]{:S(2)}, u32[]{:S(2)}) collective-permute-start(f32[16,1,512]{2,0,1:T(8,128)S(1)} %get-tuple-element.30), channel_id=1, source_target_pairs={{2,0},{4,2},{6,4},{8,6},{10,8},{12,10},{14,12},{16,14},{18,16},{20... | collective-permute-start | bytes 98312 | tf_op jit(solution)/shard_map/ppermute | solution.py:22
  20.3 12.7 %collective-permute-start.1 = (f32[16,1,512]{2,0,1:T(8,128)S(1)}, f32[16,1,512]{2,0,1:T(8,128)S(1)}, u32[]{:S(2)}, u32[]{:S(2)}) collective-permute-start(f32[16,1,512]{2,0,1:T(8,128)S(1)} %get-tuple-element.29), channel_id=1, source_target_pairs={{0,2},{2,4},{4,6},{6,8},{8,10},{10,12},{12,14},{14,16},{16,18},{18... | collective-permute-start | bytes 98312 | tf_op jit(solution)/shard_map/ppermute | solution.py:19
  33.1 4.4 collective-permute-start.2
  34.4 4.2 collective-permute-start.3
  39.1 9.8 %collective-permute-start.4 = (f32[8,1,512]{2,0,1:T(8,128)S(1)}, f32[8,1,512]{2,0,1:T(8,128)S(1)}, u32[]{:S(2)}, u32[]{:S(2)}) collective-permute-start(f32[8,1,512]{2,0,1:T(8,128)S(1)} %get-tuple-element.46), channel_id=1, source_target_pairs={{2,0},{4,2},{6,4},{8,6},{10,8},{12,10},{14,12},{16,14},{18,16},{20... | collective-permute-start | bytes 49160 | tf_op jit(solution)/shard_map/ppermute | solution.py:22
  41.1 12.6 %collective-permute-start.5 = (f32[8,1,512]{2,0,1:T(8,128)S(1)}, f32[8,1,512]{2,0,1:T(8,128)S(1)}, u32[]{:S(2)}, u32[]{:S(2)}) collective-permute-start(f32[8,1,512]{2,0,1:T(8,128)S(1)} %get-tuple-element.45), channel_id=1, source_target_pairs={{0,2},{2,4},{4,6},{6,8},{8,10},{10,12},{12,14},{14,16},{16,18},{18... | collective-permute-start | bytes 49160 | tf_op jit(solution)/shard_map/ppermute | solution.py:19
  53.7 4.4 collective-permute-start.6
  55.0 4.0 collective-permute-start.7
  59.9 9.8 %collective-permute-start.8 = (f32[16,1,512]{2,0,1:T(8,128)S(1)}, f32[16,1,512]{2,0,1:T(8,128)S(1)}, u32[]{:S(2)}, u32[]{:S(2)}) collective-permute-start(f32[16,1,512]{2,0,1:T(8,128)S(1)} %get-tuple-element.28), channel_id=1, source_target_pairs={{2,0},{4,2},{6,4},{8,6},{10,8},{12,10},{14,12},{16,14},{18,16},{20... | collective-permute-start | bytes 98312 | tf_op jit(solution)/shard_map/ppermute | solution.py:22
  63.0 12.9 %collective-permute-start.9 = (f32[16,1,512]{2,0,1:T(8,128)S(1)}, f32[16,1,512]{2,0,1:T(8,128)S(1)}, u32[]{:S(2)}, u32[]{:S(2)}) collective-permute-start(f32[16,1,512]{2,0,1:T(8,128)S(1)} %get-tuple-element.27), channel_id=1, source_target_pairs={{0,2},{2,4},{4,6},{6,8},{8,10},{10,12},{12,14},{14,16},{16,18},{18... | collective-permute-start | bytes 98312 | tf_op jit(solution)/shard_map/ppermute | solution.py:19
  76.1 4.4 collective-permute-start.10
  77.4 4.2 collective-permute-start.11
  82.0 9.8 %collective-permute-start.12 = (f32[8,1,512]{2,0,1:T(8,128)S(1)}, f32[8,1,512]{2,0,1:T(8,128)S(1)}, u32[]{:S(2)}, u32[]{:S(2)}) collective-permute-start(f32[8,1,512]{2,0,1:T(8,128)S(1)} %get-tuple-element.44), channel_id=1, source_target_pairs={{2,0},{4,2},{6,4},{8,6},{10,8},{12,10},{14,12},{16,14},{18,16},{20... | collective-permute-start | bytes 49160 | tf_op jit(solution)/shard_map/ppermute | solution.py:22
  83.9 12.7 %collective-permute-start.13 = (f32[8,1,512]{2,0,1:T(8,128)S(1)}, f32[8,1,512]{2,0,1:T(8,128)S(1)}, u32[]{:S(2)}, u32[]{:S(2)}) collective-permute-start(f32[8,1,512]{2,0,1:T(8,128)S(1)} %get-tuple-element.43), channel_id=1, source_target_pairs={{0,2},{2,4},{4,6},{6,8},{8,10},{10,12},{12,14},{14,16},{16,18},{18... | collective-permute-start | bytes 49160 | tf_op jit(solution)/shard_map/ppermute | solution.py:19
  96.7 4.4 collective-permute-start.14
  98.0 4.0 collective-permute-start.15
  102.4 9.9 %collective-permute-start.16 = (f32[16,1,512]{2,0,1:T(8,128)S(1)}, f32[16,1,512]{2,0,1:T(8,128)S(1)}, u32[]{:S(2)}, u32[]{:S(2)}) collective-permute-start(f32[16,1,512]{2,0,1:T(8,128)S(1)} %get-tuple-element.26), channel_id=1, source_target_pairs={{2,0},{4,2},{6,4},{8,6},{10,8},{12,10},{14,12},{16,14},{18,16},{20... | collective-permute-start | bytes 98312 | tf_op jit(solution)/shard_map/ppermute | solution.py:22
  104.9 12.7 %collective-permute-start.17 = (f32[16,1,512]{2,0,1:T(8,128)S(1)}, f32[16,1,512]{2,0,1:T(8,128)S(1)}, u32[]{:S(2)}, u32[]{:S(2)}) collective-permute-start(f32[16,1,512]{2,0,1:T(8,128)S(1)} %get-tuple-element.25), channel_id=1, source_target_pairs={{0,2},{2,4},{4,6},{6,8},{8,10},{10,12},{12,14},{14,16},{16,18},{18... | collective-permute-start | bytes 98312 | tf_op jit(solution)/shard_map/ppermute | solution.py:19
  117.8 4.4 collective-permute-start.18
  119.1 4.2 collective-permute-start.19
  123.7 9.8 %collective-permute-start.20 = (f32[8,1,512]{2,0,1:T(8,128)S(1)}, f32[8,1,512]{2,0,1:T(8,128)S(1)}, u32[]{:S(2)}, u32[]{:S(2)}) collective-permute-start(f32[8,1,512]{2,0,1:T(8,128)S(1)} %get-tuple-element.42), channel_id=1, source_target_pairs={{2,0},{4,2},{6,4},{8,6},{10,8},{12,10},{14,12},{16,14},{18,16},{20... | collective-permute-start | bytes 49160 | tf_op jit(solution)/shard_map/ppermute | solution.py:22
  125.7 12.7 %collective-permute-start.21 = (f32[8,1,512]{2,0,1:T(8,128)S(1)}, f32[8,1,512]{2,0,1:T(8,128)S(1)}, u32[]{:S(2)}, u32[]{:S(2)}) collective-permute-start(f32[8,1,512]{2,0,1:T(8,128)S(1)} %get-tuple-element.41), channel_id=1, source_target_pairs={{0,2},{2,4},{4,6},{6,8},{8,10},{10,12},{12,14},{14,16},{16,18},{18... | collective-permute-start | bytes 49160 | tf_op jit(solution)/shard_map/ppermute | solution.py:19
  138.5 4.6 collective-permute-start.22
  139.8 4.0 collective-permute-start.23
  145.7 4.2 copy-start.2
  145.7 4.4 copy-start.4
  145.7 4.6 copy-start.5
  145.7 4.6 copy-start.3
  145.7 38.7 %all-to-all-start = ((f32[8,3,32,512]{3,0,1,2:T(8,128)}), f32[8,3,32,512]{3,0,1,2:T(8,128)S(1)}, u32[]{:S(2)}, u32[]{:S(2)}) async-start(f32[8,3,32,512]{3,0,1,2:T(8,128)} %pad_maximum_fusion), calls=%async_computation | async-start | bytes 3145728 | tf_op jit(solution)/shard_map/all_to_all | solution.py:105
  149.9 290.9 %all-reduce.2.cloned.1.call-start = ((), (), s32[]{:S(2)}) async-start(), calls=%async_computation.2 | async-start | bytes 524288 | tf_op jit(solution)/shard_map/psum | solution.py:109
  187.4 2.6 copy-start.1
  187.4 2.6 copy-start.6
  492.2 41.0 %all-to-all-start.1 = ((f32[32,3,8,512]{3,2,1,0:T(8,128)}), f32[32,3,8,512]{3,2,1,0:T(8,128)S(1)}, u32[]{:S(2)}, u32[]{:S(2)}) async-start(f32[32,3,8,512]{3,2,1,0:T(8,128)} %copy.138), calls=%async_computation.1 | async-start | bytes 3145728 | tf_op jit(solution)/shard_map/all_to_all | solution.py:118
Sparse Core Ops, SparseCore 0:
  191.4 249.3 all-reduce.1
where the time goes:
time: 547 us; the launch traced here: 541 us
  waiting for transfers between devices  356 us (65%)
  starting transfers between devices  98.2 us (18%)
  other arithmetic  53.4 us (10%)
  between operations  14.6 us (3%)
  local copies, waits for them, and re-layouts  14.3 us (3%)
    psum x1, waiting for transfers between devices, on_device(): lax.psum(local_products(observed_state, observed, variances, perturbation...  248 us
    ppermute x12, starting transfers between devices, extended(): lax.ppermute(lax.slice_in_dim(block, block.shape[dim] - width, None, axis...  57.7 us
    ppermute x12, waiting for transfers between devices, extended(): lax.ppermute(lax.slice_in_dim(block, block.shape[dim] - width, None, axis...  42.8 us
    all_to_all x1, waiting for transfers between devices, on_device(): lax.all_to_all(propagated_trials, 'grp', split_axis=2, concat_axis=0, til...  33.9 us
    all_to_all x1, waiting for transfers between devices, on_device(): lax.all_to_all(block_increments, 'grp', split_axis=0, concat_axis=2, tile...  31.2 us
    ppermute x12, starting transfers between devices, extended(): lax.ppermute(lax.slice_in_dim(block, 0, width, axis=dim), axis, backward)  30 us
    another operation x4, other arithmetic, transform(): factor = jnp.linalg.cholesky(system)  23.6 us
    another operation x3, other arithmetic, solve_one(): return jax.scipy.linalg.cho_solve((triangle, True), target)  19.8 us
  transfers between devices with their start and end apart: 27, of which 16 were waited for; matrix products, arithmetic and copies ran while one was open for 1% of the time, Pallas kernels for 0%

commit v1 on v0

v1 whole, which is shorter than its diff:
```python
import functools

import jax
import jax.numpy as jnp
from jax import lax
from jax.experimental import pallas as pl
from jax.experimental.pallas import tpu as pltpu
from jax.sharding import Mesh, PartitionSpec as P

STEPS = 3
REG = 8
GRP = 4
SUB = 4
MEM = 8
E = 32
CX = 32
CY = 512
LANE = 128
PARTS = CY // LANE
WIDE = CY + LANE
PAD = 8
ROWS = CX + 2 * PAD
OBS = 16
DU, DV, DL = 6, 5, 5
STRIP = DU + DV + DL + 1
FRICTION = 0.02
HIGHEST = lax.Precision.HIGHEST
F32 = jnp.float32
BF16 = jnp.bfloat16
SIDE = ("grp", "sub", "cores")
TILE = ("reg", "sub")


def vmem(n):
    return [pl.BlockSpec(memory_space=pltpu.VMEM)] * n


SMEM = pl.BlockSpec(memory_space=pltpu.SMEM)
PARAMS = pltpu.CompilerParams(vmem_limit_bytes=48 * 1024 * 1024)


def call(body, outs, args, scratch=(), flops=0):
    moved = sum(a.size * 4 for a in args) + sum(4 * o.size for o in outs)
    return pl.pallas_call(
        body,
        out_shape=list(outs),
        in_specs=[SMEM] + vmem(len(args) - 1),
        out_specs=vmem(len(outs)),
        scratch_shapes=list(scratch),
        compiler_params=PARAMS,
        cost_estimate=pl.CostEstimate(flops=flops, bytes_accessed=moved, transcendentals=0),
    )(*args)


def shaped(*shape, dtype=F32):
    return jax.ShapeDtypeStruct(shape, dtype)


def aligned(value, unit):
    return pl.multiple_of(value * unit, unit)


def pack_body(where, trial, seabed, down, up, beside):
    for out, first in ((down, CX), (up, 0)):
        for part in range(PARTS):
            lanes = slice(part * LANE, (part + 1) * LANE)
            for member in range(MEM):
                at = 0
                for field, depth in ((1, DU), (2, DV), (0, DL)):
                    low = first - depth if first else 0
                    out[part, pl.ds(at * MEM + member, depth, stride=MEM), :] = trial[
                        member, field, low : low + depth, lanes
                    ]
                    at += depth
            low = first - DU if first else 0
            out[part, (STRIP - 1) * MEM : STRIP * MEM, :] = jnp.zeros((MEM, LANE), F32)
            out[part, (STRIP - 1) * MEM : (STRIP - 1) * MEM + DU, :] = seabed[low : low + DU, lanes]
    edge = pl.ds(pl.multiple_of(jnp.where(where[1] == 0, CY - LANE, 0), LANE), LANE)
    for member in range(MEM):
        for field in range(3):
            beside[member * 3 + field] = trial[member, field, :, edge]
    beside[MEM * 3] = seabed[:, edge]


def pack(where, trial, seabed):
    strip = shaped(PARTS, STRIP * MEM, LANE)
    return call(
        pack_body, (strip, strip, shaped(MEM * 3 + 1, CX, LANE)), (where, trial, seabed)
    )


def forecast_body(
    where, trial, seabed, above, below, beside, corner, columns, rows_of, *rest
):
    blocks, state, (level, east, north, depth) = rest[:GRP], rest[GRP], rest[GRP + 1 :]
    group, core = where[0], where[1]
    fields = (level, east, north)
    lane = lax.broadcasted_iota(jnp.int32, (1, LANE), 1)
    keep = jnp.where((lane < LANE // 2) == (core == 0), 1.0, 0.0).astype(F32)

    for field in range(3):
        for member in range(MEM):
            at = pl.ds(PAD * MEM + member, CX, stride=MEM)
            for part in range(PARTS):
                fields[field][part, at, :] = trial[
                    member, field, :, part * LANE : (part + 1) * LANE
                ]
            fields[field][PARTS, at, :] = beside[member * 3 + field] * keep
    for strip, side, top in ((above, 0, True), (below, 1, False)):
        for part in range(PARTS + 1):
            def piece(low, count):
                if part < PARTS:
                    return strip[part, low : low + count, :]
                return corner[side, low : low + count, :] * keep

            at = 0
            for ref, count in ((east, DU), (north, DV), (level, DL)):
                to = (PAD - count if top else PAD + CX) * MEM
                ref[part, to : to + count * MEM, :] = piece(at * MEM, count * MEM)
                at += count
            for row in range(DU):
                to = ((PAD - DU if top else PAD + CX) + row) * MEM
                depth[part, to : to + MEM, :] = jnp.broadcast_to(
                    piece((STRIP - 1) * MEM + row, 1), (MEM, LANE)
                )
    for row in range(CX):
        to = (PAD + row) * MEM
        for part in range(PARTS):
            depth[part, to : to + MEM, :] = jnp.broadcast_to(
                seabed[row : row + 1, part * LANE : (part + 1) * LANE], (MEM, LANE)
            )
        depth[PARTS, to : to + MEM, :] = jnp.broadcast_to(
            beside[MEM * 3, row : row + 1, :] * keep, (MEM, LANE)
        )

    wide_lane = lax.broadcasted_iota(jnp.int32, (1, WIDE), 1)
    inside = jnp.where(
        (wide_lane < CY) | ((wide_lane < CY + LANE // 2) == (core == 0)), 1.0, 0.0
    ).astype(F32)
    has_above = where[2].astype(F32)
    has_below = where[3].astype(F32)

    def get(ref, row):
        at = pl.ds(aligned(row, MEM), MEM)
        return jnp.concatenate([ref[part, at, :] for part in range(PARTS + 1)], axis=1)

    def put(ref, row, value):
        at = pl.ds(aligned(row, MEM), MEM)
        for part in range(PARTS + 1):
            ref[part, at, :] = value[:, part * LANE : (part + 1) * LANE]

    def across(value):
        return pltpu.roll(value, WIDE - 1, 1) - pltpu.roll(value, 1, 1)

    def move_level(row, carry):
        flag = jnp.where(row < PAD, has_above, jnp.where(row >= PAD + CX, has_below, 1.0))
        along = get(depth, row + 1) * get(east, row + 1) - get(depth, row - 1) * get(east, row - 1)
        spread = 0.5 * along + 0.5 * across(get(depth, row) * get(north, row))
        put(level, row, (get(level, row) - spread) * (inside * flag))
        return carry

    def move_flow(row, carry):
        slope = get(level, row + 1) - get(level, row - 1)
        put(east, row, (1.0 - FRICTION) * get(east, row) - 0.5 * slope)
        slope = across(get(level, row))
        put(north, row, (1.0 - FRICTION) * get(north, row) - 0.5 * slope)
        return carry

    for step in range(STEPS):
        reach = 2 * (STEPS - 1 - step)
        lax.fori_loop(PAD - reach - 1, PAD + CX + reach + 1, move_level, 0, unroll=2)
        lax.fori_loop(PAD - reach, PAD + CX + reach, move_flow, 0, unroll=2)

    inner = slice(PAD * MEM, (PAD + CX) * MEM)
    own = jnp.concatenate([level[part, inner, :] for part in range(PARTS)], axis=1)
    first = own.astype(BF16)
    left = own - first.astype(F32)
    second = left.astype(BF16)
    third = (left - second.astype(F32)).astype(BF16)
    pick = columns[...].astype(BF16)
    dot = functools.partial(jnp.dot, preferred_element_type=F32)
    picked = dot(first, pick) + dot(second, pick) + dot(third, pick)
    total = jnp.zeros((MEM, LANE), F32)
    for row in range(CX):
        total += picked[row * MEM : (row + 1) * MEM, :] * rows_of[row : row + 1, :]
    total = total + pltpu.roll(total, LANE // 2, 1)
    for to in range(GRP * SUB * 2):
        state[to] = total

    for other in range(GRP):
        for field in range(3):
            blocks[other][field * CX * MEM : (field + 1) * CX * MEM, :] = fields[field][
                jnp.bitwise_xor(group, other), inner, :
            ]


def forecast(where, trial, seabed, above, below, beside, corner, columns, rows_of):
    block = shaped(3 * CX * MEM, LANE)
    return call(
        forecast_body,
        (block,) * GRP + (shaped(GRP * SUB * 2, MEM, LANE),),
        (where, trial, seabed, above, below, beside, corner, columns, rows_of),
        [pltpu.VMEM((PARTS + 1, ROWS * MEM, LANE), F32)] * 4,
        flops=12_000_000,
    )


def unpack_body(where, *refs):
    blocks, out = refs[:GRP], refs[GRP]
    for other in range(GRP):
        at = pl.ds(aligned(jnp.bitwise_xor(where[0], other), LANE), LANE)
        for field in range(3):
            for member in range(MEM):
                out[member, field, :, at] = blocks[other][
                    pl.ds(field * CX * MEM + member, CX, stride=MEM), :
                ]


def unpack(where, blocks):
    return call(unpack_body, (shaped(MEM, 3, CX, CY),), (where, *blocks))[0]


def products_body(where, states, noisy, variances, masks, out):
    group = where[0]
    left, right = [], []
    for block in range(SUB * 2):
        seen = jnp.concatenate(
            [states[jnp.bitwise_xor(group, s) * (SUB * 2) + block] for s in range(GRP)], axis=0
        )
        wanted = jnp.concatenate(
            [
                noisy[block, pl.ds(aligned(jnp.bitwise_xor(group, s), MEM), MEM), :]
                for s in range(GRP)
            ],
            axis=0,
        )
        anomaly = seen - jnp.mean(seen, axis=0, keepdims=True)
        scaled = anomaly / variances[block : block + 1, :]
        left.append(
            jnp.concatenate([scaled * masks[block, r : r + 1, :] for r in range(3)], axis=0)
        )
        right.append(jnp.concatenate([anomaly, wanted - seen], axis=0))
    out[...] = lax.dot_general(
        jnp.concatenate(left, axis=1),
        jnp.concatenate(right, axis=1),
        (((1,), (1,)), ((), ())),
        precision=HIGHEST,
        preferred_element_type=F32,
    )


def region_products(where, states, noisy, variances, masks):
    return call(
        products_body, (shaped(3 * E, 2 * E),), (where, states, noisy, variances, masks)
    )[0]


def solve_body(where, own, low, high, out):
    total = own[E : 2 * E, :] + low[...] + high[...]
    row = lax.broadcasted_iota(jnp.int32, (E, 2 * E), 0)
    lane = lax.broadcasted_iota(jnp.int32, (E, 2 * E), 1)
    system = total + jnp.where(row == lane, E - 1.0, 0.0)
    for k in range(E):
        pivot = system[k : k + 1, :] / system[k : k + 1, k : k + 1]
        system = jnp.where(row == k, pivot, system - system[:, k : k + 1] * pivot)
    out[...] = system[:, E:]


def solve(where, own, low, high):
    return call(solve_body, (shaped(E, E),), (where, own, low, high))[0]


def increments_body(where, *refs):
    weights, blocks, outs = refs[0], refs[1 : 1 + GRP], refs[1 + GRP :]
    turned = weights[...].T
    coarse = turned.astype(BF16)
    fine = (turned - coarse.astype(F32)).astype(BF16)
    left = jnp.concatenate([coarse, coarse, fine], axis=1)
    group = 8

    def some(part, carry):
        pieces = []
        for inner in range(group):
            at = pl.ds(aligned(part * group + inner, MEM), MEM)
            pieces.append(jnp.concatenate([block[at, :] for block in blocks], axis=0))
        state = jnp.concatenate(pieces, axis=1)
        state = state - jnp.mean(state, axis=0, keepdims=True)
        high = state.astype(BF16)
        low = (state - high.astype(F32)).astype(BF16)
        right = jnp.concatenate([high, low, high], axis=0)
        result = jnp.dot(left, right, preferred_element_type=F32)
        for inner in range(group):
            at = pl.ds(aligned(part * group + inner, MEM), MEM)
            for other in range(GRP):
                outs[other][at, :] = result[
                    other * MEM : (other + 1) * MEM, inner * LANE : (inner + 1) * LANE
                ]
        return carry

    lax.fori_loop(0, 3 * CX // group, some, 0)


def increments(where, weights, blocks):
    return call(
        increments_body,
        (shaped(3 * CX * MEM, LANE),) * GRP,
        (where, weights, *blocks),
        flops=80_000_000,
    )


def exchange(blocks):
    return [blocks[0]] + [
        lax.ppermute(blocks[s], "grp", [(i, i ^ s) for i in range(GRP)]) for s in range(1, GRP)
    ]


def on_device(
    trial, seabed, observed, variances, perturbations, stencil_cells, stencil_weights, region_mask
):
    group, region = lax.axis_index("grp"), lax.axis_index("reg")
    sub, core = lax.axis_index("sub"), lax.axis_index("cores")
    tile = region * SUB + sub
    where = jnp.stack(
        [group, core, (tile > 0).astype(jnp.int32), (tile < REG * SUB - 1).astype(jnp.int32)]
    ).astype(jnp.int32)
    forward = [(i, i + 1) for i in range(REG * SUB - 1)]
    backward = [(i + 1, i) for i in range(REG * SUB - 1)]

    down, up, beside = pack(where, trial, seabed)
    above = lax.ppermute(down, TILE, forward)
    below = lax.ppermute(up, TILE, backward)
    beside = lax.ppermute(beside, "cores", [(0, 1), (1, 0)])

    noisy = observed[:, None] + jnp.sqrt(variances)[:, None] * perturbations
    three = lax.dynamic_slice_in_dim(
        jnp.pad(region_mask.astype(F32), ((0, 0), (1, 1))), region, 3, axis=1
    )
    known = jnp.concatenate(
        [noisy, three, variances[:, None], stencil_cells[:, :1].astype(F32), stencil_weights],
        axis=1,
    )
    fields = known.shape[1]
    known = jnp.pad(known.reshape(-1), (0, MEM * LANE - OBS * fields)).reshape(1, MEM, LANE)
    known = lax.all_to_all(
        jnp.broadcast_to(known, (GRP * SUB * 2, MEM, LANE)), SIDE, 0, 0, tiled=True
    )
    known = known.reshape(GRP, SUB * 2, MEM * LANE)[:, :, : OBS * fields]
    known = known.reshape(GRP, SUB * 2, OBS, fields).transpose(1, 3, 0, 2)
    known = known.reshape(SUB * 2, fields, GRP * OBS)
    mine = lax.dynamic_index_in_dim(known, sub * 2 + core, 0, keepdims=False)[E + 4 :]
    known = jnp.pad(known[:, : E + 4], ((0, 0), (0, 0), (0, LANE - GRP * OBS)))
    noisy, masks, scale = known[:, :E], known[:, E : E + 3], known[:, E + 3]
    scale = jnp.where(jnp.arange(LANE)[None] < GRP * OBS, scale, 1.0)
    anchor = mine[0].astype(jnp.int32)
    first_row = anchor // CY + (jnp.arange(GRP * OBS) // OBS) * (CX // GRP)
    first_column = anchor % CY
    column = jnp.arange(CY)[:, None]
    columns = jnp.concatenate(
        [column == first_column[None], column == first_column[None] + 1], axis=1
    ).astype(F32)
    row = jnp.arange(CX)[:, None]
    at_row, next_row = (row == first_row[None]).astype(F32), (row == first_row[None] + 1).astype(F32)
    rows_of = jnp.concatenate(
        [
            at_row * mine[1][None] + next_row * mine[3][None],
            at_row * mine[2][None] + next_row * mine[4][None],
        ],
        axis=1,
    )

    edge = jnp.where(core == 0, PARTS - 1, 0)
    corner = lax.ppermute(
        jnp.stack([lax.dynamic_index_in_dim(s, edge, 0, keepdims=False) for s in (above, below)]),
        "cores",
        [(0, 1), (1, 0)],
    )
    *blocks, state = forecast(
        where, trial, seabed, above, below, beside, corner, columns, rows_of
    )
    members = exchange(blocks)
    propagated_trials = unpack(where, blocks)

    states = lax.all_to_all(state, SIDE, 0, 0, tiled=True)
    products = region_products(where, states, noisy, scale, masks)
    up_region = [(i + 1, i) for i in range(REG - 1)]
    down_region = [(i, i + 1) for i in range(REG - 1)]
    from_above = lax.ppermute(products[2 * E :], "reg", down_region)
    from_below = lax.ppermute(products[:E], "reg", up_region)
    weights = solve(where, products, from_above, from_below)
    analysis_updates = unpack(where, exchange(increments(where, weights, members)))
    return (propagated_trials, analysis_updates)


def solution(mesh):
    fine = Mesh(
        mesh.devices.reshape(GRP, REG, SUB, 2), ("grp", "reg", "sub", "cores")
    )
    every = ("grp", "reg", "sub", "cores")
    state = P("grp", None, TILE, "cores")
    in_specs = (
        state,
        P(TILE, "cores"),
        P(every),
        P(every),
        P(every, None),
        P(every, None),
        P(every, None),
        P(every, None),
    )
    return jax.shard_map(
        on_device, mesh=fine, in_specs=in_specs, out_specs=(state, state), check_vma=False
    )
```

time: 547 us -> 158 us (0.29)
  waiting for transfers between devices: 356 us -> 71.1 us
  starting transfers between devices: 98.2 us -> 44.6 us
  other arithmetic: 53.4 us -> 2.74 us
  Pallas kernels: 0 us -> 25.5 us
  between operations: 14.6 us -> 0.94 us
    psum x1 -> x0, waiting for transfers between devices: 248 us -> none  [on_device(): lax.psum(local_products(observed_state, observed, variances, perturbation...]
    ppermute x24 -> x12, starting transfers between devices: 87.7 us -> 27.4 us  [the longest x1 8.97 us: on_device(): below = lax.ppermute(up, TILE, backward)]
    all_to_all x2, waiting for transfers between devices: 65.2 us -> 11.8 us  [the longest x1 11.8 us: on_device(): states = lax.all_to_all(state, SIDE, 0, 0, tiled=True)]
    another operation x10 -> x2, other arithmetic: 45.5 us -> 0.09 us  [the longest x1 0.08 us: on_device(): jnp.stack([group, core, (tile > 0).astype(jnp.int32), (tile < REG * SUB -...]
    pallas_call x0 -> x7, Pallas kernels: none -> 25.5 us  [call(): pl.pallas_call(body, out_shape=list(outs), in_specs=[SMEM] + vmem(len(arg...]
    ppermute x24 -> x12, waiting for transfers between devices: 42.9 us -> 59.3 us  [the longest x6 36.6 us: exchange(): lax.ppermute(blocks[s], 'grp', [(i, i ^ s) for i in range(GRP)])]
    all_to_all x2, starting transfers between devices: 10.5 us -> 17.2 us  [the longest x1 9.74 us: on_device(): lax.all_to_all(jnp.broadcast_to(known, (GRP * SUB * 2, MEM, LANE)), SIDE,...]
  transfers between devices with their start and end apart: 27 -> 14, of which waited for: 16 -> 8; matrix products, arithmetic and copies ran while one was open for 1% -> 4% of each run, Pallas kernels for 0% -> 5%
where the time goes in v1:
time: 158 us; the launch traced here: 157 us
  waiting for transfers between devices  71.1 us (45%)
  starting transfers between devices  44.6 us (28%)
  Pallas kernels  25.5 us (16%)
  local copies, waits for them, and re-layouts  12 us (8%)
  other arithmetic  2.74 us (2%)
    ppermute x6, waiting for transfers between devices, exchange(): lax.ppermute(blocks[s], 'grp', [(i, i ^ s) for i in range(GRP)])  36.6 us
    pallas_call x7, Pallas kernels, call(): pl.pallas_call(body, out_shape=list(outs), in_specs=[SMEM] + vmem(len(arg...  25.5 us
    ppermute x1, waiting for transfers between devices, on_device(): below = lax.ppermute(up, TILE, backward)  12.5 us
    all_to_all x1, waiting for transfers between devices, on_device(): states = lax.all_to_all(state, SIDE, 0, 0, tiled=True)  11.8 us
    all_to_all x1, starting transfers between devices, on_device(): lax.all_to_all(jnp.broadcast_to(known, (GRP * SUB * 2, MEM, LANE)), SIDE,...  9.74 us
    ppermute x1, starting transfers between devices, on_device(): below = lax.ppermute(up, TILE, backward)  8.97 us
    ppermute x6, starting transfers between devices, exchange(): lax.ppermute(blocks[s], 'grp', [(i, i ^ s) for i in range(GRP)])  8.04 us
    ppermute x1, waiting for transfers between devices, on_device(): above = lax.ppermute(down, TILE, forward)  7.65 us
  transfers between devices with their start and end apart: 14, of which 8 were waited for; matrix products, arithmetic and copies ran while one was open for 4% of the time, Pallas kernels for 5%

profile of v1, /device:TPU:38, one launch (start us, length us, event | category | flops | bytes accessed | tf_op | source)
XLA Modules:
  0.0 157.0 jit_solution(17535869556789753367)
XLA Ops:
  0.6 0.7 convert_element_type.38
  1.4 0.7 slice_convert_fusion
  2.2 0.7 sqrt.3
  2.9 0.7 copy.21
  3.6 0.8 copy.23
  4.3 0.8 multiply_add_fusion
  5.3 0.7 broadcast_in_dim.20
  6.0 9.7 %all-to-all-start = ((f32[32,8,128]{2,1,0:T(8,128)}), f32[32,8,128]{2,1,0:T(8,128)S(1)}, u32[]{:S(2)}, u32[]{:S(2)}) async-start(f32[32,8,128]{2,1,0:T(8,128)} %broadcast_in_dim.20), calls=%async_computation | async-start | bytes 262144 | tf_op jit(solution)/shard_map/all_to_all | solution.py:345
  15.8 1.4 copy-done
  17.2 0.8 copy-done.6
  18.1 1.5 shard_map.95
  19.5 9.0 %collective-permute-start.1 = (f32[4,136,128]{2,1,0:T(8,128)S(1)}, f32[4,136,128]{2,1,0:T(8,128)S(1)}, u32[]{:S(2)}, u32[]{:S(2)}) collective-permute-start(f32[4,136,128]{2,1,0:T(8,128)S(1)} %get-tuple-element.15), channel_id=1, source_target_pairs={{2,0},{4,2},{6,4},{8,6},{10,8},{12,10},{14,12},{16,14},{18,16},{20... | collective-permute-start | bytes 835592 | tf_op jit(solution)/shard_map/ppermute | solution.py:332
  28.5 1.9 %collective-permute-start = (f32[4,136,128]{2,1,0:T(8,128)S(1)}, f32[4,136,128]{2,1,0:T(8,128)S(1)}, u32[]{:S(2)}, u32[]{:S(2)}) collective-permute-start(f32[4,136,128]{2,1,0:T(8,128)S(1)} %get-tuple-element.14), channel_id=1, source_target_pairs={{0,2},{2,4},{4,6},{6,8},{8,10},{10,12},{12,14},{14,16},{16,18},{18... | collective-permute-start | bytes 835592 | tf_op jit(solution)/shard_map/ppermute | solution.py:331
  30.7 0.9 reshape.100
  31.6 1.0 copy.24
  32.5 0.2 fusion
  32.8 0.2 dynamic-slice_reduce_fusion.3
  33.1 0.1 copy-done.9
  33.2 1.1 copy.26
  34.4 12.5 %collective-permute-done.1.below = f32[4,136,128]{2,1,0:T(8,128)S(1)} collective-permute-done((f32[4,136,128]{2,1,0:T(8,128)S(1)}, f32[4,136,128]{2,1,0:T(8,128)S(1)}, u32[]{:S(2)}, u32[]{:S(2)}) %collective-permute-start.1) | collective-permute-done | bytes 278560 | tf_op jit(solution)/shard_map/ppermute | solution.py:332
  46.9 7.6 %collective-permute-done.above = f32[4,136,128]{2,1,0:T(8,128)S(1)} collective-permute-done((f32[4,136,128]{2,1,0:T(8,128)S(1)}, f32[4,136,128]{2,1,0:T(8,128)S(1)}, u32[]{:S(2)}, u32[]{:S(2)}) %collective-permute-start) | collective-permute-done | bytes 278560 | tf_op jit(solution)/shard_map/ppermute | solution.py:331
  54.6 0.1 collective-permute-start.3
  54.7 0.1 add_convert_fusion.columns
  54.9 1.2 collective-permute-done.3.corner
  56.0 13.1 %shard_map.96 = (f32[768,128]{1,0:T(8,128)S(1)}, f32[768,128]{1,0:T(8,128)S(1)}, f32[768,128]{1,0:T(8,128)S(1)}, f32[768,128]{1,0:T(8,128)S(1)}, f32[32,8,128]{2,1,0:T(8,128)}) custom-call(s32[4]{0:T(128)S(1)} %pad_add_fusion.where, f32[8,3,32,512]{3,2,1,0:T(8,128)S(1)} %copy-done.1, f32[32,512]{1,0:T(8,128)S(1)} %copy-done.7, ...), custom_call_target="tpu_custom_call" | custom-call | flops 12000000 | bytes 4726800 | tf_op jit(solution)/shard_map/pallas_call | solution.py:44
  69.2 0.7 copy-done.2
  69.9 0.7 copy-done.4
  70.6 7.5 %all-to-all-start.1 = ((f32[32,8,128]{2,1,0:T(8,128)}), f32[32,8,128]{2,1,0:T(8,128)S(1)}, u32[]{:S(2)}, u32[]{:S(2)}) async-start(f32[32,8,128]{2,1,0:T(8,128)} %get-tuple-element.21), calls=%async_computation.1 | async-start | bytes 262144 | tf_op jit(solution)/shard_map/all_to_all | solution.py:384
  78.2 0.3 collective-permute-start.6
  78.5 2.7 %collective-permute-start.7 = (f32[768,128]{1,0:T(8,128)}, f32[768,128]{1,0:T(8,128)S(1)}, u32[]{:S(2)}, u32[]{:S(2)}) collective-permute-start(f32[768,128]{1,0:T(8,128)} %copy-done.2), channel_id=1, source_target_pairs={{0,128},{64,192},{128,0},{192,64},{1,129},{65,193},{129,1},{193,65... | collective-permute-start | bytes 1179656 | tf_op jit(solution)/shard_map/ppermute | solution.py:314
  81.2 0.6 collective-permute-start.8
  81.7 0.8 pad_slice_fusion.masks
  82.5 0.9 pad_slice_fusion.2.noisy
  83.4 11.8 %all-to-all-done.1.states = f32[32,8,128]{2,1,0:T(8,128)S(1)} async-done(((f32[32,8,128]{2,1,0:T(8,128)}), f32[32,8,128]{2,1,0:T(8,128)S(1)}, u32[]{:S(2)}, u32[]{:S(2)}) %all-to-all-start.1) | async-done | bytes 131104 | tf_op jit(solution)/shard_map/all_to_all | solution.py:384
  95.2 1.0 shard_map.98.own
  96.3 2.3 %collective-permute-start.4 = (f32[32,64]{1,0:T(8,128)S(1)}, f32[32,64]{1,0:T(8,128)S(1)}, u32[]{:S(2)}, u32[]{:S(2)}) collective-permute-start(f32[32,64]{1,0:T(8,128)S(1)} %get-tuple-element.35), channel_id=1, source_target_pairs={{0,8},{8,16},{16,24},{24,32},{32,40},{40,48},{48,56},{1,9},{9,17},... | collective-permute-start | bytes 24584 | tf_op jit(solution)/shard_map/ppermute | solution.py:388
  98.6 5.9 %collective-permute-start.5 = (f32[32,64]{1,0:T(8,128)S(1)}, f32[32,64]{1,0:T(8,128)S(1)}, u32[]{:S(2)}, u32[]{:S(2)}) collective-permute-start(f32[32,64]{1,0:T(8,128)S(1)} %get-tuple-element.34), channel_id=1, source_target_pairs={{8,0},{16,8},{24,16},{32,24},{40,32},{48,40},{56,48},{9,1},{17,9},... | collective-permute-start | bytes 24584 | tf_op jit(solution)/shard_map/ppermute | solution.py:389
  104.5 1.4 collective-permute-done.5.high
  106.0 3.2 %shard_map.99.refs_0_ = f32[32,32]{1,0:T(8,128)S(1)} custom-call(s32[4]{0:T(128)S(1)} %pad_add_fusion.where, f32[96,64]{1,0:T(8,128)S(1)} %shard_map.98.own, f32[32,64]{1,0:T(8,128)S(1)} %collective-permute-done.4.low, f32[32,64]{1,0:T(8,128)S(1)} %collective-permute-done.5.high), custom_call_target="tpu_custom_call" | custom-call | bytes 45072 | tf_op jit(solution)/shard_map/pallas_call | solution.py:44
  109.2 8.2 %collective-permute-done.8.refs_4_ = f32[768,128]{1,0:T(8,128)S(1)} collective-permute-done((f32[768,128]{1,0:T(8,128)}, f32[768,128]{1,0:T(8,128)S(1)}, u32[]{:S(2)}, u32[]{:S(2)}) %collective-permute-start.8) | collective-permute-done | bytes 393248 | tf_op jit(solution)/shard_map/ppermute | solution.py:314
  117.4 2.7 %shard_map.100 = (f32[768,128]{1,0:T(8,128)S(1)}, f32[768,128]{1,0:T(8,128)S(1)}, f32[768,128]{1,0:T(8,128)S(1)}, f32[768,128]{1,0:T(8,128)S(1)}) custom-call(s32[4]{0:T(128)S(1)} %pad_add_fusion.where, f32[32,32]{1,0:T(8,128)S(1)} %shard_map.99.refs_0_, f32[768,128]{1,0:T(8,128)S(1)} %get-tuple-element.17.refs_0_.refs_1_, ...), custom_call_target="tpu_custom_call" | custom-call | flops 80000000 | bytes 3149840 | tf_op jit(solution)/shard_map/pallas_call | solution.py:44
  120.1 0.1 collective-permute-start.10
  120.2 0.9 collective-permute-start.11
  121.1 3.5 %collective-permute-start.9 = (f32[768,128]{1,0:T(8,128)S(1)}, f32[768,128]{1,0:T(8,128)S(1)}, u32[]{:S(2)}, u32[]{:S(2)}) collective-permute-start(f32[768,128]{1,0:T(8,128)S(1)} %get-tuple-element.23), channel_id=1, source_target_pairs={{0,64},{64,0},{128,192},{192,128},{1,65},{65,1},{129,193},{193,129... | collective-permute-start | bytes 1179656 | tf_op jit(solution)/shard_map/ppermute | solution.py:314
  124.6 2.0 %shard_map.97 = f32[8,3,32,512]{3,2,1,0:T(8,128)} custom-call(s32[4]{0:T(128)S(1)} %pad_add_fusion.where, f32[768,128]{1,0:T(8,128)S(1)} %get-tuple-element.17.refs_0_.refs_1_, f32[768,128]{1,0:T(8,128)S(1)} %get-tuple-element.18.refs_1_, f32[768,128]{1,0:T(8,128)S(1)} %copy-done.3, f32[768,128]{1,0:T(8,128)S(1)} %copy-done.5), custom_call_target="tpu_custom_call" | custom-call | bytes 3145744 | tf_op jit(solution)/shard_map/pallas_call | solution.py:44
  126.5 20.1 %collective-permute-done.10.refs_2_ = f32[768,128]{1,0:T(8,128)S(1)} collective-permute-done((f32[768,128]{1,0:T(8,128)S(1)}, f32[768,128]{1,0:T(8,128)S(1)}, u32[]{:S(2)}, u32[]{:S(2)}) %collective-permute-start.10) | collective-permute-done | bytes 393248 | tf_op jit(solution)/shard_map/ppermute | solution.py:314
  146.6 8.4 %collective-permute-done.11.refs_3_ = f32[768,128]{1,0:T(8,128)S(1)} collective-permute-done((f32[768,128]{1,0:T(8,128)S(1)}, f32[768,128]{1,0:T(8,128)S(1)}, u32[]{:S(2)}, u32[]{:S(2)}) %collective-permute-start.11) | collective-permute-done | bytes 393248 | tf_op jit(solution)/shard_map/ppermute | solution.py:314
  155.0 2.0 %shard_map.101 = f32[8,3,32,512]{3,2,1,0:T(8,128)} custom-call(s32[4]{0:T(128)S(1)} %pad_add_fusion.where, f32[768,128]{1,0:T(8,128)S(1)} %get-tuple-element.22.refs_0_, f32[768,128]{1,0:T(8,128)S(1)} %collective-permute-done.9.refs_1_, f32[768,128]{1,0:T(8,128)S(1)} %collective-permute-done.10.refs_2_, f32[768,128]{1,0:T(8,128)S(1)} %collective-permute-done.11.refs_3_), custom_call_target="tpu_custom_call" | custom-call | bytes 3145744 | tf_op jit(solution)/shard_map/pallas_call | solution.py:44
  (42 shorter events, 0.9 us)
Async XLA Ops:
  6.0 24.6 %all-to-all-start = ((f32[32,8,128]{2,1,0:T(8,128)}), f32[32,8,128]{2,1,0:T(8,128)S(1)}, u32[]{:S(2)}, u32[]{:S(2)}) async-start(f32[32,8,128]{2,1,0:T(8,128)} %broadcast_in_dim.20), calls=%async_computation | async-start | bytes 262144 | tf_op jit(solution)/shard_map/all_to_all | solution.py:345
  15.8 1.4 copy-start
  17.2 0.8 copy-start.6
  19.5 27.4 %collective-permute-start.1 = (f32[4,136,128]{2,1,0:T(8,128)S(1)}, f32[4,136,128]{2,1,0:T(8,128)S(1)}, u32[]{:S(2)}, u32[]{:S(2)}) collective-permute-start(f32[4,136,128]{2,1,0:T(8,128)S(1)} %get-tuple-element.15), channel_id=1, source_target_pairs={{2,0},{4,2},{6,4},{8,6},{10,8},{12,10},{14,12},{16,14},{18,16},{20... | collective-permute-start | bytes 835592 | tf_op jit(solution)/shard_map/ppermute | solution.py:332
  28.5 26.0 %collective-permute-start = (f32[4,136,128]{2,1,0:T(8,128)S(1)}, f32[4,136,128]{2,1,0:T(8,128)S(1)}, u32[]{:S(2)}, u32[]{:S(2)}) collective-permute-start(f32[4,136,128]{2,1,0:T(8,128)S(1)} %get-tuple-element.14), channel_id=1, source_target_pairs={{0,2},{2,4},{4,6},{6,8},{8,10},{10,12},{12,14},{14,16},{16,18},{18... | collective-permute-start | bytes 835592 | tf_op jit(solution)/shard_map/ppermute | solution.py:331
  30.5 24.4 %collective-permute-start.2 = (f32[25,32,128]{2,1,0:T(8,128)}, f32[25,32,128]{2,1,0:T(8,128)S(1)}, u32[]{:S(2)}, u32[]{:S(2)}) collective-permute-start(f32[25,32,128]{2,1,0:T(8,128)} %get-tuple-element.16), channel_id=1, source_target_pairs={{0,1},{1,0},{2,3},{3,2},{4,5},{5,4},{6,7},{7,6},{8,9},{9,8},{10,11... | collective-permute-start | bytes 1228808 | tf_op jit(solution)/shard_map/ppermute | solution.py:333
  30.6 25.4 %copy-start.1 = (f32[8,3,32,512]{3,2,1,0:T(8,128)S(1)}, f32[8,3,32,512]{3,2,1,0:T(8,128)}, u32[]{:S(2)}) copy-start(f32[8,3,32,512]{3,2,1,0:T(8,128)} %trial.3) | copy-start | bytes 4718596
  30.6 25.4 %copy-start.7 = (f32[32,512]{1,0:T(8,128)S(1)}, f32[32,512]{1,0:T(8,128)}, u32[]{:S(2)}) copy-start(f32[32,512]{1,0:T(8,128)} %seabed.3) | copy-start | bytes 196612
  32.5 0.7 copy-start.9
  34.3 20.5 %copy-start.8 = (f32[8,36,64]{2,1,0:T(8,128)}, f32[8,36,64]{2,1,0:T(8,128)S(1)}, u32[]{:S(2)}) copy-start(f32[8,36,64]{2,1,0:T(8,128)S(1)} %copy.26) | copy-start | bytes 221188
  54.6 1.4 collective-permute-start.3
  69.2 0.7 copy-start.2
  69.9 0.7 copy-start.4
  70.6 53.9 %copy-start.3 = (f32[768,128]{1,0:T(8,128)S(1)}, f32[768,128]{1,0:T(8,128)}, u32[]{:S(2)}) copy-start(f32[768,128]{1,0:T(8,128)} %copy-done.2) | copy-start | bytes 1179652
  70.6 53.9 %copy-start.5 = (f32[768,128]{1,0:T(8,128)S(1)}, f32[768,128]{1,0:T(8,128)}, u32[]{:S(2)}) copy-start(f32[768,128]{1,0:T(8,128)} %copy-done.4) | copy-start | bytes 1179652
  70.6 24.6 %all-to-all-start.1 = ((f32[32,8,128]{2,1,0:T(8,128)}), f32[32,8,128]{2,1,0:T(8,128)S(1)}, u32[]{:S(2)}, u32[]{:S(2)}) async-start(f32[32,8,128]{2,1,0:T(8,128)} %get-tuple-element.21), calls=%async_computation.1 | async-start | bytes 262144 | tf_op jit(solution)/shard_map/all_to_all | solution.py:384
  78.2 31.0 %collective-permute-start.6 = (f32[768,128]{1,0:T(8,128)S(1)}, f32[768,128]{1,0:T(8,128)S(1)}, u32[]{:S(2)}, u32[]{:S(2)}) collective-permute-start(f32[768,128]{1,0:T(8,128)S(1)} %get-tuple-element.18.refs_1_), channel_id=1, source_target_pairs={{0,64},{64,0},{128,192},{192,128},{1,65},{65,1},{129,193},{193,129... | collective-permute-start | bytes 1179656 | tf_op jit(solution)/shard_map/ppermute | solution.py:314
  78.5 30.7 %collective-permute-start.7 = (f32[768,128]{1,0:T(8,128)}, f32[768,128]{1,0:T(8,128)S(1)}, u32[]{:S(2)}, u32[]{:S(2)}) collective-permute-start(f32[768,128]{1,0:T(8,128)} %copy-done.2), channel_id=1, source_target_pairs={{0,128},{64,192},{128,0},{192,64},{1,129},{65,193},{129,1},{193,65... | collective-permute-start | bytes 1179656 | tf_op jit(solution)/shard_map/ppermute | solution.py:314
  81.2 36.2 %collective-permute-start.8 = (f32[768,128]{1,0:T(8,128)}, f32[768,128]{1,0:T(8,128)S(1)}, u32[]{:S(2)}, u32[]{:S(2)}) collective-permute-start(f32[768,128]{1,0:T(8,128)} %copy-done.4), channel_id=1, source_target_pairs={{0,192},{64,128},{128,64},{192,0},{1,193},{65,129},{129,65},{193,1... | collective-permute-start | bytes 1179656 | tf_op jit(solution)/shard_map/ppermute | solution.py:314
  96.3 8.3 %collective-permute-start.4 = (f32[32,64]{1,0:T(8,128)S(1)}, f32[32,64]{1,0:T(8,128)S(1)}, u32[]{:S(2)}, u32[]{:S(2)}) collective-permute-start(f32[32,64]{1,0:T(8,128)S(1)} %get-tuple-element.35), channel_id=1, source_target_pairs={{0,8},{8,16},{16,24},{24,32},{32,40},{40,48},{48,56},{1,9},{9,17},... | collective-permute-start | bytes 24584 | tf_op jit(solution)/shard_map/ppermute | solution.py:388
  98.6 7.4 %collective-permute-start.5 = (f32[32,64]{1,0:T(8,128)S(1)}, f32[32,64]{1,0:T(8,128)S(1)}, u32[]{:S(2)}, u32[]{:S(2)}) collective-permute-start(f32[32,64]{1,0:T(8,128)S(1)} %get-tuple-element.34), channel_id=1, source_target_pairs={{8,0},{16,8},{24,16},{32,24},{40,32},{48,40},{56,48},{9,1},{17,9},... | collective-permute-start | bytes 24584 | tf_op jit(solution)/shard_map/ppermute | solution.py:389
  120.1 26.5 %collective-permute-start.10 = (f32[768,128]{1,0:T(8,128)S(1)}, f32[768,128]{1,0:T(8,128)S(1)}, u32[]{:S(2)}, u32[]{:S(2)}) collective-permute-start(f32[768,128]{1,0:T(8,128)S(1)} %get-tuple-element.24), channel_id=1, source_target_pairs={{0,128},{64,192},{128,0},{192,64},{1,129},{65,193},{129,1},{193,65... | collective-permute-start | bytes 1179656 | tf_op jit(solution)/shard_map/ppermute | solution.py:314
  120.2 34.8 %collective-permute-start.11 = (f32[768,128]{1,0:T(8,128)S(1)}, f32[768,128]{1,0:T(8,128)S(1)}, u32[]{:S(2)}, u32[]{:S(2)}) collective-permute-start(f32[768,128]{1,0:T(8,128)S(1)} %get-tuple-element.25), channel_id=1, source_target_pairs={{0,192},{64,128},{128,64},{192,0},{1,193},{65,129},{129,65},{193,1... | collective-permute-start | bytes 1179656 | tf_op jit(solution)/shard_map/ppermute | solution.py:314
  121.1 33.9 %collective-permute-start.9 = (f32[768,128]{1,0:T(8,128)S(1)}, f32[768,128]{1,0:T(8,128)S(1)}, u32[]{:S(2)}, u32[]{:S(2)}) collective-permute-start(f32[768,128]{1,0:T(8,128)S(1)} %get-tuple-element.23), channel_id=1, source_target_pairs={{0,64},{64,0},{128,192},{192,128},{1,65},{65,1},{129,193},{193,129... | collective-permute-start | bytes 1179656 | tf_op jit(solution)/shard_map/ppermute | solution.py:314

commit v2 on v1

v2 whole, which is shorter than its diff:
```python
import functools

import jax
import jax.numpy as jnp
from jax import lax
from jax.experimental import pallas as pl
from jax.experimental.pallas import tpu as pltpu
from jax.sharding import Mesh, PartitionSpec as P

STEPS = 3
REG = 8
GRP = 4
SUB = 4
MEM = 8
E = 32
CX = 32
CY = 512
LANE = 128
PARTS = CY // LANE
WIDE = CY + LANE
PAD = 8
OBS = 16
HALF = PAD * MEM
MIDDLE = CX * MEM - 2 * HALF
DU, DV, DL = 6, 5, 5
STRIP = DU + DV + DL + 1
FRICTION = 0.02
HIGHEST = lax.Precision.HIGHEST
F32 = jnp.float32
BF16 = jnp.bfloat16
SIDE = ("grp", "sub", "cores")
TILE = ("reg", "sub")


VMEM = pl.BlockSpec(memory_space=pltpu.VMEM)
SMEM = pl.BlockSpec(memory_space=pltpu.SMEM)


def call(body, outs, args, scratch=(), mib=16, flops=0, moved=0):
    return pl.pallas_call(
        body,
        out_shape=list(outs),
        in_specs=[SMEM] + [VMEM] * (len(args) - 1),
        out_specs=[VMEM] * len(outs),
        scratch_shapes=list(scratch),
        compiler_params=pltpu.CompilerParams(vmem_limit_bytes=mib * 1024 * 1024),
        cost_estimate=pl.CostEstimate(flops=flops, bytes_accessed=moved, transcendentals=0),
    )(*args)


def shaped(*shape, dtype=F32):
    return jax.ShapeDtypeStruct(shape, dtype)


def aligned(value, unit):
    return pl.multiple_of(value * unit, unit)


def pack_body(where, trial, seabed, down, up, beside):
    for out, first in ((down, CX), (up, 0)):
        for part in range(PARTS):
            lanes = slice(part * LANE, (part + 1) * LANE)
            for member in range(MEM):
                at = 0
                for field, depth in ((1, DU), (2, DV), (0, DL)):
                    low = first - depth if first else 0
                    out[part, pl.ds(at * MEM + member, depth, stride=MEM), :] = trial[
                        member, field, low : low + depth, lanes
                    ]
                    at += depth
            low = first - DU if first else 0
            out[part, (STRIP - 1) * MEM : STRIP * MEM, :] = jnp.zeros((MEM, LANE), F32)
            out[part, (STRIP - 1) * MEM : (STRIP - 1) * MEM + DU, :] = seabed[low : low + DU, lanes]
    edge = pl.ds(pl.multiple_of(jnp.where(where[1] == 0, CY - LANE, 0), LANE), LANE)
    for member in range(MEM):
        for field in range(3):
            beside[member * 3 + field] = trial[member, field, :, edge]
    beside[MEM * 3] = seabed[:, edge]


def pack(where, trial, seabed):
    strip = shaped(PARTS, STRIP * MEM, LANE)
    return call(
        pack_body, (strip, strip, shaped(MEM * 3 + 1, CX, LANE)), (where, trial, seabed)
    )


def row_at(row):
    return pl.ds(aligned(row, MEM), MEM)


def get(ref, row):
    at = row_at(row)
    return jnp.concatenate([ref[part, at, :] for part in range(PARTS + 1)], axis=1)


def put(ref, row, value):
    at = row_at(row)
    for part in range(PARTS + 1):
        ref[part, at, :] = value[:, part * LANE : (part + 1) * LANE]


def across(value):
    return pltpu.roll(value, WIDE - 1, 1) - pltpu.roll(value, 1, 1)


def move_level(fields, row, inside):
    level, east, north, depth = fields
    along = get(depth, row + 1) * get(east, row + 1) - get(depth, row - 1) * get(east, row - 1)
    spread = 0.5 * along + 0.5 * across(get(depth, row) * get(north, row))
    put(level, row, (get(level, row) - spread) * inside)


def move_flow(fields, row):
    level, east, north, _ = fields
    slope = get(level, row + 1) - get(level, row - 1)
    put(east, row, (1.0 - FRICTION) * get(east, row) - 0.5 * slope)
    slope = across(get(level, row))
    put(north, row, (1.0 - FRICTION) * get(north, row) - 0.5 * slope)


def kept_half(core):
    lane = lax.broadcasted_iota(jnp.int32, (1, LANE), 1)
    return jnp.where((lane < LANE // 2) == (core == 0), 1.0, 0.0).astype(F32)


def inside_of(core):
    lane = lax.broadcasted_iota(jnp.int32, (1, WIDE), 1)
    inside = (lane < CY) | ((lane < CY + LANE // 2) == (core == 0))
    return jnp.where(inside, 1.0, 0.0).astype(F32)


def inner_body(where, trial, seabed, beside, *outs):
    blocks, fields = outs[:GRP], [outs[GRP].at[f] for f in range(4)]
    keep, inside = kept_half(where[1]), inside_of(where[1])
    for field in range(3):
        for member in range(MEM):
            at = pl.ds(member, CX, stride=MEM)
            for part in range(PARTS):
                fields[field][part, at, :] = trial[
                    member, field, :, part * LANE : (part + 1) * LANE
                ]
            fields[field][PARTS, at, :] = beside[member * 3 + field] * keep
    depth = fields[3]
    for row in range(CX):
        at = slice(row * MEM, (row + 1) * MEM)
        for part in range(PARTS):
            depth[part, at, :] = jnp.broadcast_to(
                seabed[row : row + 1, part * LANE : (part + 1) * LANE], (MEM, LANE)
            )
        depth[PARTS, at, :] = jnp.broadcast_to(
            beside[MEM * 3, row : row + 1, :] * keep, (MEM, LANE)
        )

    def level_row(row, carry):
        move_level(fields, row, inside)
        return carry

    def flow_row(row, carry):
        move_flow(fields, row)
        return carry

    for step in range(STEPS):
        lax.fori_loop(2 * step + 1, CX - 2 * step - 1, level_row, 0, unroll=2)
        lax.fori_loop(2 * step + 2, CX - 2 * step - 2, flow_row, 0, unroll=2)
    for other in range(GRP):
        for field in range(3):
            blocks[other][field * MIDDLE : (field + 1) * MIDDLE, :] = fields[field][
                jnp.bitwise_xor(where[0], other), HALF : CX * MEM - HALF, :
            ]


def inner_forecast(where, trial, seabed, beside):
    fields = shaped(4, PARTS + 1, CX * MEM, LANE)
    block = shaped(3 * MIDDLE, LANE)
    return call(
        inner_body,
        (block,) * GRP + (fields,),
        (where, trial, seabed, beside),
        flops=10_000_000,
        moved=32_000_000,
    )


def sense(levels, stencils):
    anchor = stencils[0:1, :].astype(jnp.int32)
    lane = lax.broadcasted_iota(jnp.int32, (1, LANE), 1)
    of_group = (lane % (GRP * OBS)) // OBS
    row = anchor // CY + of_group * (CX // GRP)
    pick = lax.broadcasted_iota(jnp.int32, (CY, LANE), 0) == anchor % CY
    pick = jnp.where(pick, 1.0, 0.0).astype(BF16)
    first = levels.astype(BF16)
    left = levels - first.astype(F32)
    second = left.astype(BF16)
    third = (left - second.astype(F32)).astype(BF16)
    dot = functools.partial(jnp.dot, preferred_element_type=F32)
    picked = dot(first, pick) + dot(second, pick) + dot(third, pick)
    total = jnp.zeros((MEM, LANE), F32)
    for at in range(CX):
        here = jnp.where(row == at, stencils[1:2, :], 0.0)
        here += jnp.where(row + 1 == at, stencils[2:3, :], 0.0)
        total += picked[at * MEM : (at + 1) * MEM, :] * here
    return total + pltpu.roll(total, LANE // 2, 1)


def outer_body(where, inner, above, below, corner, known, *rest):
    stencils, rest = rest[:GRP], rest[GRP:]
    blocks, state, whole, scratch = rest[:GRP], rest[GRP], rest[GRP + 1], rest[GRP + 2 :]
    group, core = where[0], where[1]
    keep, inside = kept_half(core), inside_of(core)
    given = [inner.at[f] for f in range(4)]
    half = HALF
    top, bottom = scratch[:4], scratch[4:]
    for field in range(4):
        for part in range(PARTS + 1):
            top[field][part, half:, :] = given[field][part, :half, :]
            bottom[field][part, :half, :] = given[field][part, CX * MEM - half :, :]
    for strip, side, fields in ((above, 0, top), (below, 1, bottom)):
        for part in range(PARTS + 1):

            def piece(low, count):
                if part < PARTS:
                    return strip[part, low : low + count, :]
                return corner[side, low : low + count, :] * keep

            at = 0
            for field, count in ((1, DU), (2, DV), (0, DL)):
                to = half if side else (PAD - count) * MEM
                fields[field][part, to : to + count * MEM, :] = piece(at * MEM, count * MEM)
                at += count
            for row in range(DU):
                to = half + row * MEM if side else (PAD - DU + row) * MEM
                fields[3][part, to : to + MEM, :] = jnp.broadcast_to(
                    piece((STRIP - 1) * MEM + row, 1), (MEM, LANE)
                )
    has_above = inside * where[2].astype(F32)
    has_below = inside * where[3].astype(F32)
    for step in range(STEPS):
        shift = 2 * step
        for row in range(-5 + shift, 1 + shift):
            move_level(top, PAD + row, has_above if row < 0 else inside)
            move_level(bottom, PAD - 1 - row, has_below if row < 0 else inside)
        for row in range(-4 + shift, 2 + shift):
            move_flow(top, PAD + row)
            move_flow(bottom, PAD - 1 - row)

    levels = jnp.concatenate(
        [
            jnp.concatenate(
                [
                    top[0][part, half:, :],
                    given[0][part, half : CX * MEM - half, :],
                    bottom[0][part, :half, :],
                ],
                axis=0,
            )
            for part in range(PARTS)
        ],
        axis=1,
    )
    total = sense(levels, sum(s[...] for s in stencils))
    for to in range(GRP * SUB * 2):
        state[to, :MEM, :] = total
        state[to, MEM:, :] = known[...]

    for field in range(3):
        for part in range(PARTS):
            whole[field, part, :half, :] = top[field][part, half:, :]
            whole[field, part, half:, :] = bottom[field][part, :half, :]
        for other in range(GRP):
            blocks[other][field * MIDDLE : (field + 1) * MIDDLE, :] = whole[
                field, jnp.bitwise_xor(group, other)
            ]


def outer_forecast(where, inner, above, below, corner, known, stencils):
    block = shaped(3 * MIDDLE, LANE)
    return call(
        outer_body,
        (block,) * GRP
        + (shaped(GRP * SUB * 2, 2 * MEM, LANE), shaped(3, PARTS, 2 * HALF, LANE)),
        (where, inner, above, below, corner, known, *stencils),
        [pltpu.VMEM((PARTS + 1, 2 * PAD * MEM, LANE), F32)] * 8,
    )


def unpack_body(where, *refs):
    blocks, out = refs[:GRP], refs[GRP]
    for other in range(GRP):
        at = pl.ds(aligned(jnp.bitwise_xor(where[0], other), LANE), LANE)
        for field in range(3):
            for member in range(MEM):
                out[member, field, :, at] = blocks[other][
                    pl.ds(field * CX * MEM + member, CX, stride=MEM), :
                ]


def unpack(where, blocks):
    return call(unpack_body, (shaped(MEM, 3, CX, CY),), (where, *blocks))[0]


def spread_out_body(where, inner, outer, out):
    for part in range(PARTS):
        lanes = slice(part * LANE, (part + 1) * LANE)
        for field in range(3):
            for member in range(MEM):
                out[member, field, PAD : CX - PAD, lanes] = inner[
                    field, part, pl.ds(HALF + member, CX - 2 * PAD, stride=MEM), :
                ]
                out[member, field, :PAD, lanes] = outer[
                    field, part, pl.ds(member, PAD, stride=MEM), :
                ]
                out[member, field, CX - PAD :, lanes] = outer[
                    field, part, pl.ds(HALF + member, PAD, stride=MEM), :
                ]


def spread_out(where, inner, outer):
    return call(spread_out_body, (shaped(MEM, 3, CX, CY),), (where, inner, outer))[0]


def products_body(where, states, out, wanted_at):
    group = where[0]
    lane = lax.broadcasted_iota(jnp.int32, (1, LANE), 1)
    left, right = [], []
    for block in range(SUB * 2):
        noisy, other = [jnp.zeros((MEM, LANE), F32)] * GRP, jnp.zeros((MEM, LANE), F32)
        for source in range(GRP):
            held = states[source * (SUB * 2) + block, MEM:, :]
            here = lane // OBS == source
            for part in range(GRP):
                turned = pltpu.roll(held, (source - part) * OBS % LANE, 1)
                noisy[part] = jnp.where(here, turned, noisy[part])
            turned = pltpu.roll(held, (source - GRP) * OBS % LANE, 1)
            other = jnp.where(here, turned, other)
        for part in range(GRP):
            wanted_at[block, part] = noisy[part]
        seen = jnp.concatenate(
            [
                states[jnp.bitwise_xor(group, s) * (SUB * 2) + block, :MEM, :]
                for s in range(GRP)
            ],
            axis=0,
        )
        wanted = jnp.concatenate(
            [wanted_at[block, jnp.bitwise_xor(group, s)] for s in range(GRP)], axis=0
        )
        anomaly = seen - jnp.mean(seen, axis=0, keepdims=True)
        scaled = anomaly / jnp.where(lane < GRP * OBS, other[3:4, :], 1.0)
        left.append(jnp.concatenate([scaled * other[r : r + 1, :] for r in range(3)], axis=0))
        right.append(jnp.concatenate([anomaly, wanted - seen], axis=0))
    out[...] = lax.dot_general(
        jnp.concatenate(left, axis=1),
        jnp.concatenate(right, axis=1),
        (((1,), (1,)), ((), ())),
        precision=HIGHEST,
        preferred_element_type=F32,
    )


def region_products(where, states):
    return call(
        products_body,
        (shaped(3 * E, 2 * E),),
        (where, states),
        [pltpu.VMEM((SUB * 2, GRP, MEM, LANE), F32)],
    )[0]


def solve_body(where, own, low, high, out):
    total = own[E : 2 * E, :] + low[...] + high[...]
    row = lax.broadcasted_iota(jnp.int32, (E, 2 * E), 0)
    lane = lax.broadcasted_iota(jnp.int32, (E, 2 * E), 1)
    system = total + jnp.where(row == lane, E - 1.0, 0.0)
    for k in range(E):
        pivot = system[k : k + 1, :] / system[k : k + 1, k : k + 1]
        system = jnp.where(row == k, pivot, system - system[:, k : k + 1] * pivot)
    out[...] = system[:, E:]


def solve(where, own, low, high):
    return call(solve_body, (shaped(E, E),), (where, own, low, high))[0]


def increments_body(where, *refs):
    weights, middle, edge, outs = refs[0], refs[1 : 1 + GRP], refs[1 + GRP : 1 + 2 * GRP], refs[1 + 2 * GRP :]
    turned = weights[...].T
    coarse = turned.astype(BF16)
    fine = (turned - coarse.astype(F32)).astype(BF16)
    left = jnp.concatenate([coarse, coarse, fine], axis=1)

    def some(blocks, low, to):
        pieces = []
        for row in range(PAD):
            at = slice(low + row * MEM, low + (row + 1) * MEM)
            pieces.append(jnp.concatenate([block[at, :] for block in blocks], axis=0))
        state = jnp.concatenate(pieces, axis=1)
        state = state - jnp.mean(state, axis=0, keepdims=True)
        high = state.astype(BF16)
        low_part = (state - high.astype(F32)).astype(BF16)
        right = jnp.concatenate([high, low_part, high], axis=0)
        result = jnp.dot(left, right, preferred_element_type=F32)
        for row in range(PAD):
            for other in range(GRP):
                outs[other][to + row * MEM : to + (row + 1) * MEM, :] = result[
                    other * MEM : (other + 1) * MEM, row * LANE : (row + 1) * LANE
                ]

    for field in range(3):
        at, to = field * MIDDLE, field * CX * MEM
        some(edge, at, to)
        some(middle, at, to + HALF)
        some(middle, at + HALF, to + 2 * HALF)
        some(edge, at + HALF, to + 3 * HALF)


def increments(where, weights, middle, edge):
    return call(
        increments_body,
        (shaped(3 * CX * MEM, LANE),) * GRP,
        (where, weights, *middle, *edge),
    )


def exchange(blocks):
    return [blocks[0]] + [
        lax.ppermute(blocks[s], "grp", [(i, i ^ s) for i in range(GRP)]) for s in range(1, GRP)
    ]


def on_device(
    trial, seabed, observed, variances, perturbations, stencil_cells, stencil_weights, region_mask
):
    group, region = lax.axis_index("grp"), lax.axis_index("reg")
    sub, core = lax.axis_index("sub"), lax.axis_index("cores")
    tile = region * SUB + sub
    where = jnp.stack(
        [group, core, (tile > 0).astype(jnp.int32), (tile < REG * SUB - 1).astype(jnp.int32)]
    ).astype(jnp.int32)
    forward = [(i, i + 1) for i in range(REG * SUB - 1)]
    backward = [(i + 1, i) for i in range(REG * SUB - 1)]

    down, up, beside = pack(where, trial, seabed)
    above = lax.ppermute(down, TILE, forward)
    below = lax.ppermute(up, TILE, backward)
    beside = lax.ppermute(beside, "cores", [(0, 1), (1, 0)])

    count, wide = GRP * OBS, LANE // 2
    anchor = stencil_cells[:, 0].astype(F32)
    pair = jnp.stack([anchor, anchor + 1.0])
    uses = stencil_weights.T
    stencil = jnp.stack([pair, uses[:2], uses[2:]])
    slot = (jnp.arange(GRP) == group).astype(F32)
    stencil = (stencil[:, :, None, :] * slot[None, None, :, None]).reshape(3, 2 * count)
    stencil = jnp.pad(stencil, ((0, MEM - 3), (0, 0)))
    noisy = observed[:, None] + jnp.sqrt(variances)[:, None] * perturbations
    noisy = noisy.T.reshape(GRP, MEM, OBS).transpose(1, 0, 2).reshape(MEM, count)
    three = lax.dynamic_slice_in_dim(
        jnp.pad(region_mask.astype(F32), ((0, 0), (1, 1))), region, 3, axis=1
    )
    three = jnp.concatenate([three.T, variances[None]], axis=0)
    known = jnp.concatenate(
        [noisy, jnp.pad(three, ((0, MEM - 4), (0, wide - OBS)))], axis=1
    )

    *middle, inner = inner_forecast(where, trial, seabed, beside)
    stencil, inner = lax.optimization_barrier((stencil, inner))
    stencils = exchange([stencil] * GRP)
    above, below, _ = lax.optimization_barrier((above, below, stencils[1:]))
    edge = jnp.where(core == 0, PARTS - 1, 0)

    def outer_rows(above, below, inner, known, stencils):
        ends = [lax.dynamic_index_in_dim(s, edge, 0, keepdims=False) for s in (above, below)]
        corner = lax.ppermute(jnp.stack(ends), "cores", [(0, 1), (1, 0)])
        *outer, state, rest = outer_forecast(where, inner, above, below, corner, known, stencils)
        return outer, rest, lax.all_to_all(state, SIDE, 0, 0, tiled=True)

    def nothing(*args):
        block = jnp.zeros((3 * MIDDLE, LANE), F32)
        rest = jnp.zeros((3, PARTS, 2 * HALF, LANE), F32)
        return [block] * GRP, rest, jnp.zeros((GRP * SUB * 2, 2 * MEM, LANE), F32)

    middle, *_ = lax.optimization_barrier((middle, stencils[1:]))
    middle = exchange(middle)
    outer, rest, states = lax.cond(
        group < GRP, outer_rows, nothing, above, below, inner, known, stencils
    )
    outer = exchange(outer)
    propagated_trials = spread_out(where, inner, rest)

    up_region = [(i + 1, i) for i in range(REG - 1)]
    down_region = [(i, i + 1) for i in range(REG - 1)]
    products = region_products(where, states)
    products, _ = lax.optimization_barrier((products, middle[1:]))
    from_above = lax.ppermute(products[2 * E :], "reg", down_region)
    from_below = lax.ppermute(products[:E], "reg", up_region)
    weights = solve(where, products, from_above, from_below)
    analysis_updates = unpack(where, exchange(increments(where, weights, middle, outer)))
    return (propagated_trials, analysis_updates)


def solution(mesh):
    fine = Mesh(
        mesh.devices.reshape(GRP, REG, SUB, 2), ("grp", "reg", "sub", "cores")
    )
    every = ("grp", "reg", "sub", "cores")
    state = P("grp", None, TILE, "cores")
    in_specs = (
        state,
        P(TILE, "cores"),
        P(every),
        P(every),
        P(every, None),
        P(every, None),
        P(every, None),
        P(every, None),
    )
    return jax.shard_map(
        on_device, mesh=fine, in_specs=in_specs, out_specs=(state, state), check_vma=False
    )
```

time: 158 us -> 131 us (0.83); the launches traced: 157 us -> 128 us
  waiting for transfers between devices: 71.1 us -> 42.9 us
  blocking collectives: 0 us -> 18.6 us
  local copies, waits for them, and re-layouts: 12 us -> 3.65 us
  starting transfers between devices: 44.6 us -> 37.2 us
  other arithmetic: 2.74 us -> 0.3 us
    all_to_all x0 -> x1, blocking collectives: none -> 18.6 us  [outer_rows(): return (outer, rest, lax.all_to_all(state, SIDE, 0, 0, tiled=True))]
    all_to_all x2 -> x0, starting transfers between devices: 17.2 us -> none  [the longest x1 9.74 us: on_device(): lax.all_to_all(jnp.broadcast_to(known, (GRP * SUB * 2, MEM, LANE)), SIDE,...]
    ppermute x1, waiting for transfers between devices: 12.5 us -> 0.01 us  [on_device(): below = lax.ppermute(up, TILE, backward)]
    all_to_all x2 -> x0, waiting for transfers between devices: 11.8 us -> none  [the longest x1 11.8 us: on_device(): states = lax.all_to_all(state, SIDE, 0, 0, tiled=True)]
    ppermute x6 -> x12, starting transfers between devices: 8.04 us -> 16.3 us  [exchange(): lax.ppermute(blocks[s], 'grp', [(i, i ^ s) for i in range(GRP)])]
    ppermute x1, waiting for transfers between devices: 7.65 us -> 0.01 us  [on_device(): above = lax.ppermute(down, TILE, forward)]
    ppermute x1, starting transfers between devices: 1.92 us -> 8.2 us  [on_device(): above = lax.ppermute(down, TILE, forward)]
    ppermute x1, waiting for transfers between devices: 0.01 us -> 5.49 us  [on_device(): from_above = lax.ppermute(products[2 * E:], 'reg', down_region)]
  transfers between devices with their start and end apart: 14 -> 18, of which waited for: 8 -> 9; matrix products, arithmetic and copies ran while one was open for 4% -> 1% of each run, Pallas kernels for 5% -> 16%
where the time goes in v2:
time: 131 us; the launch traced here: 128 us
  waiting for transfers between devices  42.9 us (33%)
  starting transfers between devices  37.2 us (28%)
  Pallas kernels  24.8 us (19%)
  blocking collectives  18.6 us (14%)
  local copies, waits for them, and re-layouts  3.65 us (3%)
    ppermute x12, waiting for transfers between devices, exchange(): lax.ppermute(blocks[s], 'grp', [(i, i ^ s) for i in range(GRP)])  34.8 us
    pallas_call x8, Pallas kernels, call(): pl.pallas_call(body, out_shape=list(outs), in_specs=[SMEM] + [VMEM] * (le...  24.8 us
    all_to_all x1, blocking collectives, outer_rows(): return (outer, rest, lax.all_to_all(state, SIDE, 0, 0, tiled=True))  18.6 us
    ppermute x12, starting transfers between devices, exchange(): lax.ppermute(blocks[s], 'grp', [(i, i ^ s) for i in range(GRP)])  16.3 us
    ppermute x1, starting transfers between devices, on_device(): above = lax.ppermute(down, TILE, forward)  8.2 us
    ppermute x1, waiting for transfers between devices, on_device(): from_above = lax.ppermute(products[2 * E:], 'reg', down_region)  5.49 us
    ppermute x1, starting transfers between devices, on_device(): from_below = lax.ppermute(products[:E], 'reg', up_region)  5.33 us
    ppermute x1, starting transfers between devices, on_device(): below = lax.ppermute(up, TILE, backward)  4.64 us
  transfers between devices with their start and end apart: 18, of which 9 were waited for; matrix products, arithmetic and copies ran while one was open for 1% of the time, Pallas kernels for 16%

profile of v2, /device:TPU:38, one launch (start us, length us, event | category | flops | bytes accessed | tf_op | source)
XLA Modules:
  0.0 128.3 jit_solution(3846152730631348536)
XLA Ops:
  0.7 0.1 pad_add_fusion.where
  0.8 1.4 %copy-done = f32[8,3,32,512]{3,2,1,0:T(8,128)S(1)} copy-done((f32[8,3,32,512]{3,2,1,0:T(8,128)S(1)}, f32[8,3,32,512]{3,2,1,0:T(8,128)}, u32[]{:S(2)}) %copy-start) | copy-done | bytes 1572888
  2.2 0.8 copy-done.2
  3.0 0.7 shard_map.95
  3.8 8.2 %collective-permute-start.2 = (f32[4,136,128]{2,1,0:T(8,128)S(1)}, f32[4,136,128]{2,1,0:T(8,128)}, u32[]{:S(2)}, u32[]{:S(2)}) collective-permute-start(f32[4,136,128]{2,1,0:T(8,128)S(1)} %get-tuple-element.73), channel_id=1, source_target_pairs={{0,2},{2,4},{4,6},{6,8},{8,10},{10,12},{12,14},{14,16},{16,18},{18... | collective-permute-start | bytes 835592 | tf_op jit(solution)/shard_map/ppermute | solution.py:444
  12.0 4.6 %collective-permute-start.3 = (f32[4,136,128]{2,1,0:T(8,128)S(1)}, f32[4,136,128]{2,1,0:T(8,128)}, u32[]{:S(2)}, u32[]{:S(2)}) collective-permute-start(f32[4,136,128]{2,1,0:T(8,128)S(1)} %get-tuple-element.74), channel_id=1, source_target_pairs={{2,0},{4,2},{6,4},{8,6},{10,8},{12,10},{14,12},{16,14},{18,16},{20... | collective-permute-start | bytes 835592 | tf_op jit(solution)/shard_map/ppermute | solution.py:445
  16.6 0.1 collective-permute-start.1
  16.8 0.1 mul.34
  16.9 0.1 mul.35
  17.0 0.1 mul.33
  17.2 0.1 add_bitcast_fusion
  17.2 1.2 collective-permute-done.1.beside
  18.5 9.7 %shard_map.96 = (f32[384,128]{1,0:T(8,128)S(1)}, f32[384,128]{1,0:T(8,128)S(1)}, f32[384,128]{1,0:T(8,128)S(1)}, f32[384,128]{1,0:T(8,128)S(1)}, f32[4,5,256,128]{3,2,1,0:T(8,128)}) custom-call(s32[4]{0:T(128)S(1)} %pad_add_fusion.where, f32[8,3,32,512]{3,2,1,0:T(8,128)S(1)} %copy-done.1, f32[32,512]{1,0:T(8,128)S(1)} %copy-done.3, ...), custom_call_target="tpu_custom_call" | custom-call | flops 10000000 | bytes 32000000 | tf_op jit(solution)/shard_map/pallas_call | solution.py:40
  28.2 1.8 %collective-permute-start.6 = (f32[8,128]{1,0:T(8,128)S(1)}, f32[8,128]{1,0:T(8,128)S(1)}, u32[]{:S(2)}, u32[]{:S(2)}) collective-permute-start(f32[8,128]{1,0:T(8,128)S(1)} %pad.12), channel_id=1, source_target_pairs={{0,192},{64,128},{128,64},{192,0},{1,193},{65,129},{129,65},{193,1... | collective-permute-start | bytes 12296 | tf_op jit(solution)/shard_map/ppermute | solution.py:427
  30.0 1.5 %collective-permute-start.5 = (f32[8,128]{1,0:T(8,128)S(1)}, f32[8,128]{1,0:T(8,128)S(1)}, u32[]{:S(2)}, u32[]{:S(2)}) collective-permute-start(f32[8,128]{1,0:T(8,128)S(1)} %pad.12), channel_id=1, source_target_pairs={{0,128},{64,192},{128,0},{192,64},{1,129},{65,193},{129,1},{193,65... | collective-permute-start | bytes 12296 | tf_op jit(solution)/shard_map/ppermute | solution.py:427
  31.6 1.3 %collective-permute-start.4 = (f32[8,128]{1,0:T(8,128)S(1)}, f32[8,128]{1,0:T(8,128)S(1)}, u32[]{:S(2)}, u32[]{:S(2)}) collective-permute-start(f32[8,128]{1,0:T(8,128)S(1)} %pad.12), channel_id=1, source_target_pairs={{0,64},{64,0},{128,192},{192,128},{1,65},{65,1},{129,193},{193,129... | collective-permute-start | bytes 12296 | tf_op jit(solution)/shard_map/ppermute | solution.py:427
  32.9 0.1 copy.14
  33.0 0.1 reshape.40
  33.0 4.3 %collective-permute-done.5 = f32[8,128]{1,0:T(8,128)S(1)} collective-permute-done((f32[8,128]{1,0:T(8,128)S(1)}, f32[8,128]{1,0:T(8,128)S(1)}, u32[]{:S(2)}, u32[]{:S(2)}) %collective-permute-start.5) | collective-permute-done | bytes 4128 | tf_op jit(solution)/shard_map/ppermute | solution.py:427
  37.4 0.2 collective-permute-done.4
  37.6 1.3 %collective-permute-start.7 = (f32[384,128]{1,0:T(8,128)S(1)}, f32[384,128]{1,0:T(8,128)S(1)}, u32[]{:S(2)}, u32[]{:S(2)}) collective-permute-start(f32[384,128]{1,0:T(8,128)S(1)} %get-tuple-element.84), channel_id=1, source_target_pairs={{0,64},{64,0},{128,192},{192,128},{1,65},{65,1},{129,193},{193,129... | collective-permute-start | bytes 589832 | tf_op jit(solution)/shard_map/ppermute | solution.py:427
  38.9 1.6 %collective-permute-start.8 = (f32[384,128]{1,0:T(8,128)S(1)}, f32[384,128]{1,0:T(8,128)S(1)}, u32[]{:S(2)}, u32[]{:S(2)}) collective-permute-start(f32[384,128]{1,0:T(8,128)S(1)} %get-tuple-element.85), channel_id=1, source_target_pairs={{0,128},{64,192},{128,0},{192,64},{1,129},{65,193},{129,1},{193,65... | collective-permute-start | bytes 589832 | tf_op jit(solution)/shard_map/ppermute | solution.py:427
  40.5 0.6 collective-permute-start.9
  41.1 0.1 pad_maximum_fusion.1
  41.2 24.6 %conditional.1 = (f32[384,128]{1,0:T(8,128)S(1)}, f32[384,128]{1,0:T(8,128)}, f32[384,128]{1,0:T(8,128)S(1)}, f32[384,128]{1,0:T(8,128)S(1)}, f32[3,4,128,128]{3...) conditional(s32[]{:T(128)} %convert_element_type.41, () %tuple.22, (s32[]{:T(128)}, f32[4,136,128]{2,1,0:T(8,128)}, ...), branch_computations={%region_0.1_spmd, %region_1.2_spmd} | conditional | flops 34818 | bytes 1835080 | solution.py:485
  41.2 0.9 constant_dynamic-slice_fusion
  42.1 0.1 collective-permute-start
  42.2 1.3 %collective-permute-done.corner = f32[2,136,128]{2,1,0:T(8,128)S(1)} collective-permute-done((f32[2,136,128]{2,1,0:T(8,128)S(1)}, f32[2,136,128]{2,1,0:T(8,128)S(1)}, u32[]{:S(2)}, u32[]{:S(2)}) %collective-permute-start) | collective-permute-done | bytes 139296 | tf_op jit(solution)/shard_map/cond/branch_1_fun/ppermute | solution.py:474
  43.6 3.6 %branch_1_fun.1 = (f32[384,128]{1,0:T(8,128)S(1)}, f32[384,128]{1,0:T(8,128)}, f32[384,128]{1,0:T(8,128)S(1)}, f32[384,128]{1,0:T(8,128)S(1)}, f32[32,16,128]{2,...) custom-call(s32[4]{0:T(128)S(1)} %get-tuple-element.25.where, f32[4,5,256,128]{3,2,1,0:T(8,128)} %get-tuple-element.26.inner, ...), custom_call_target="tpu_custom_call" | custom-call | tf_op jit(solution)/shard_map/cond/branch_1_fun/pallas_call | solution.py:40
  47.2 18.6 %all_to_all.4 = f32[32,16,128]{2,1,0:T(8,128)S(1)} all-to-all(f32[32,16,128]{2,1,0:T(8,128)S(1)} %get-tuple-element.40), channel_id=1, replica_groups=mesh['grp'=4,'reg'=8,'sub'=4,'cores'=2] {'grp','sub','cores'}, dimensions={0} | all-to-all | bytes 524288 | tf_op jit(solution)/shard_map/cond/branch_1_fun/all_to_all | solution.py:476
  65.8 1.2 shard_map.98.own
  67.0 2.7 %collective-permute-start.12 = (f32[384,128]{1,0:T(8,128)}, f32[384,128]{1,0:T(8,128)S(1)}, u32[]{:S(2)}, u32[]{:S(2)}) collective-permute-start(f32[384,128]{1,0:T(8,128)} %get-tuple-element.90), channel_id=1, source_target_pairs={{0,64},{64,0},{128,192},{192,128},{1,65},{65,1},{129,193},{193,129... | collective-permute-start | bytes 589832 | tf_op jit(solution)/shard_map/ppermute | solution.py:427
  69.7 0.2 collective-permute-start.13
  69.9 1.3 %collective-permute-start.14 = (f32[384,128]{1,0:T(8,128)S(1)}, f32[384,128]{1,0:T(8,128)S(1)}, u32[]{:S(2)}, u32[]{:S(2)}) collective-permute-start(f32[384,128]{1,0:T(8,128)S(1)} %get-tuple-element.92), channel_id=1, source_target_pairs={{0,192},{64,128},{128,64},{192,0},{1,193},{65,129},{129,65},{193,1... | collective-permute-start | bytes 589832 | tf_op jit(solution)/shard_map/ppermute | solution.py:427
  71.3 5.3 %collective-permute-start.11 = (f32[32,64]{1,0:T(8,128)S(1)}, f32[32,64]{1,0:T(8,128)S(1)}, u32[]{:S(2)}, u32[]{:S(2)}) collective-permute-start(f32[32,64]{1,0:T(8,128)S(1)} %get-tuple-element.99), channel_id=1, source_target_pairs={{8,0},{16,8},{24,16},{32,24},{40,32},{48,40},{56,48},{9,1},{17,9},... | collective-permute-start | bytes 24584 | tf_op jit(solution)/shard_map/ppermute | solution.py:496
  76.6 2.5 %collective-permute-start.10 = (f32[32,64]{1,0:T(8,128)S(1)}, f32[32,64]{1,0:T(8,128)S(1)}, u32[]{:S(2)}, u32[]{:S(2)}) collective-permute-start(f32[32,64]{1,0:T(8,128)S(1)} %get-tuple-element.100), channel_id=1, source_target_pairs={{0,8},{8,16},{16,24},{24,32},{32,40},{40,48},{48,56},{1,9},{9,17},... | collective-permute-start | bytes 24584 | tf_op jit(solution)/shard_map/ppermute | solution.py:495
  79.2 5.5 %collective-permute-done.10.low = f32[32,64]{1,0:T(8,128)S(1)} collective-permute-done((f32[32,64]{1,0:T(8,128)S(1)}, f32[32,64]{1,0:T(8,128)S(1)}, u32[]{:S(2)}, u32[]{:S(2)}) %collective-permute-start.10) | collective-permute-done | bytes 8224 | tf_op jit(solution)/shard_map/ppermute | solution.py:495
  84.7 3.2 %shard_map.99.refs_0_ = f32[32,32]{1,0:T(8,128)S(1)} custom-call(s32[4]{0:T(128)S(1)} %pad_add_fusion.where, f32[96,64]{1,0:T(8,128)S(1)} %shard_map.98.own, f32[32,64]{1,0:T(8,128)S(1)} %collective-permute-done.10.low, f32[32,64]{1,0:T(8,128)S(1)} %collective-permute-done.11.high), custom_call_target="tpu_custom_call" | custom-call | tf_op jit(solution)/shard_map/pallas_call | solution.py:40
  87.9 0.6 collective-permute-done.14.refs_8_
  88.6 1.1 shard_map.100
  89.7 2.3 %collective-permute-start.15 = (f32[768,128]{1,0:T(8,128)S(1)}, f32[768,128]{1,0:T(8,128)S(1)}, u32[]{:S(2)}, u32[]{:S(2)}) collective-permute-start(f32[768,128]{1,0:T(8,128)S(1)} %get-tuple-element.94), channel_id=1, source_target_pairs={{0,64},{64,0},{128,192},{192,128},{1,65},{65,1},{129,193},{193,129... | collective-permute-start | bytes 1179656 | tf_op jit(solution)/shard_map/ppermute | solution.py:427
  92.0 0.2 collective-permute-start.16
  92.2 1.3 %collective-permute-start.17 = (f32[768,128]{1,0:T(8,128)S(1)}, f32[768,128]{1,0:T(8,128)S(1)}, u32[]{:S(2)}, u32[]{:S(2)}) collective-permute-start(f32[768,128]{1,0:T(8,128)S(1)} %get-tuple-element.96), channel_id=1, source_target_pairs={{0,192},{64,128},{128,64},{192,0},{1,193},{65,129},{129,65},{193,1... | collective-permute-start | bytes 1179656 | tf_op jit(solution)/shard_map/ppermute | solution.py:427
  93.6 3.2 %shard_map.97 = f32[8,3,32,512]{3,2,1,0:T(8,128)} custom-call(s32[4]{0:T(128)S(1)} %pad_add_fusion.where, f32[4,5,256,128]{3,2,1,0:T(8,128)} %get-tuple-element.72.inner, f32[3,4,128,128]{3,2,1,0:T(8,128)S(1)} %get-tuple-element.78.outer), custom_call_target="tpu_custom_call" | custom-call | tf_op jit(solution)/shard_map/pallas_call | solution.py:40
  96.7 7.8 %collective-permute-done.15.refs_1_ = f32[768,128]{1,0:T(8,128)S(1)} collective-permute-done((f32[768,128]{1,0:T(8,128)S(1)}, f32[768,128]{1,0:T(8,128)S(1)}, u32[]{:S(2)}, u32[]{:S(2)}) %collective-permute-start.15) | collective-permute-done | bytes 393248 | tf_op jit(solution)/shard_map/ppermute | solution.py:427
  104.5 14.1 %collective-permute-done.16.refs_2_ = f32[768,128]{1,0:T(8,128)S(1)} collective-permute-done((f32[768,128]{1,0:T(8,128)S(1)}, f32[768,128]{1,0:T(8,128)S(1)}, u32[]{:S(2)}, u32[]{:S(2)}) %collective-permute-start.16) | collective-permute-done | bytes 393248 | tf_op jit(solution)/shard_map/ppermute | solution.py:427
  118.7 7.6 %collective-permute-done.17.refs_3_ = f32[768,128]{1,0:T(8,128)S(1)} collective-permute-done((f32[768,128]{1,0:T(8,128)S(1)}, f32[768,128]{1,0:T(8,128)S(1)}, u32[]{:S(2)}, u32[]{:S(2)}) %collective-permute-start.17) | collective-permute-done | bytes 393248 | tf_op jit(solution)/shard_map/ppermute | solution.py:427
  126.3 2.0 %shard_map.101 = f32[8,3,32,512]{3,2,1,0:T(8,128)} custom-call(s32[4]{0:T(128)S(1)} %pad_add_fusion.where, f32[768,128]{1,0:T(8,128)S(1)} %get-tuple-element.93.refs_0_, f32[768,128]{1,0:T(8,128)S(1)} %collective-permute-done.15.refs_1_, f32[768,128]{1,0:T(8,128)S(1)} %collective-permute-done.16.refs_2_, f32[768,128]{1,0:T(8,128)S(1)} %collective-permute-done.17.refs_3_), custom_call_target="tpu_custom_call" | custom-call | tf_op jit(solution)/shard_map/pallas_call | solution.py:40
  (42 shorter events, 0.2 us)
Async XLA Ops:
  0.6 16.1 %copy-start.9 = (s32[16,4]{0,1:T(4,128)S(1)}, s32[16,4]{0,1:T(4,128)}, u32[]{:S(2)}) copy-start(s32[16,4]{0,1:T(4,128)} %param.15) | copy-start | bytes 772
  0.6 16.1 %copy-start.8 = (f32[16]{0:T(128)S(1)}, f32[16]{0:T(128)}, u32[]{:S(2)}) copy-start(f32[16]{0:T(128)} %param.13) | copy-start | bytes 196
  0.7 16.3 %copy-start.5 = (s32[16,8]{0,1:T(8,128)S(1)}, s32[16,8]{0,1:T(8,128)}, u32[]{:S(2)}) copy-start(s32[16,8]{0,1:T(8,128)} %param.17) | copy-start | bytes 1540
  0.7 16.3 %copy-start.6 = (f32[16,4]{0,1:T(4,128)S(1)}, f32[16,4]{0,1:T(4,128)}, u32[]{:S(2)}) copy-start(f32[16,4]{0,1:T(4,128)} %param.16) | copy-start | bytes 772
  0.7 16.5 %copy-start.4 = (f32[16,32]{1,0:T(8,128)S(1)}, f32[16,32]{1,0:T(8,128)}, u32[]{:S(2)}) copy-start(f32[16,32]{1,0:T(8,128)} %param.14) | copy-start | bytes 6148
  0.7 16.5 %copy-start.7 = (f32[16]{0:T(128)S(1)}, f32[16]{0:T(128)}, u32[]{:S(2)}) copy-start(f32[16]{0:T(128)} %param.12) | copy-start | bytes 196
  0.8 1.4 %copy-start = (f32[8,3,32,512]{3,2,1,0:T(8,128)S(1)}, f32[8,3,32,512]{3,2,1,0:T(8,128)}, u32[]{:S(2)}) copy-start(f32[8,3,32,512]{3,2,1,0:T(8,128)} %trial.3) | copy-start | bytes 4718596
  2.2 0.8 copy-start.2
  3.0 15.4 %copy-start.1 = (f32[8,3,32,512]{3,2,1,0:T(8,128)S(1)}, f32[8,3,32,512]{3,2,1,0:T(8,128)}, u32[]{:S(2)}) copy-start(f32[8,3,32,512]{3,2,1,0:T(8,128)} %trial.3) | copy-start | bytes 4718596
  3.0 15.4 %copy-start.3 = (f32[32,512]{1,0:T(8,128)S(1)}, f32[32,512]{1,0:T(8,128)}, u32[]{:S(2)}) copy-start(f32[32,512]{1,0:T(8,128)} %seabed.3) | copy-start | bytes 196612
  3.8 37.4 %collective-permute-start.2 = (f32[4,136,128]{2,1,0:T(8,128)S(1)}, f32[4,136,128]{2,1,0:T(8,128)}, u32[]{:S(2)}, u32[]{:S(2)}) collective-permute-start(f32[4,136,128]{2,1,0:T(8,128)S(1)} %get-tuple-element.73), channel_id=1, source_target_pairs={{0,2},{2,4},{4,6},{6,8},{8,10},{10,12},{12,14},{14,16},{16,18},{18... | collective-permute-start | bytes 835592 | tf_op jit(solution)/shard_map/ppermute | solution.py:444
  12.0 29.2 %collective-permute-start.3 = (f32[4,136,128]{2,1,0:T(8,128)S(1)}, f32[4,136,128]{2,1,0:T(8,128)}, u32[]{:S(2)}, u32[]{:S(2)}) collective-permute-start(f32[4,136,128]{2,1,0:T(8,128)S(1)} %get-tuple-element.74), channel_id=1, source_target_pairs={{2,0},{4,2},{6,4},{8,6},{10,8},{12,10},{14,12},{16,14},{18,16},{20... | collective-permute-start | bytes 835592 | tf_op jit(solution)/shard_map/ppermute | solution.py:445
  16.6 1.8 %collective-permute-start.1 = (f32[25,32,128]{2,1,0:T(8,128)S(1)}, f32[25,32,128]{2,1,0:T(8,128)S(1)}, u32[]{:S(2)}, u32[]{:S(2)}) collective-permute-start(f32[25,32,128]{2,1,0:T(8,128)S(1)} %get-tuple-element.70), channel_id=1, source_target_pairs={{0,1},{1,0},{2,3},{3,2},{4,5},{5,4},{6,7},{7,6},{8,9},{9,8},{10,11... | collective-permute-start | bytes 1228808 | tf_op jit(solution)/shard_map/ppermute | solution.py:446
  28.2 4.8 %collective-permute-start.6 = (f32[8,128]{1,0:T(8,128)S(1)}, f32[8,128]{1,0:T(8,128)S(1)}, u32[]{:S(2)}, u32[]{:S(2)}) collective-permute-start(f32[8,128]{1,0:T(8,128)S(1)} %pad.12), channel_id=1, source_target_pairs={{0,192},{64,128},{128,64},{192,0},{1,193},{65,129},{129,65},{193,1... | collective-permute-start | bytes 12296 | tf_op jit(solution)/shard_map/ppermute | solution.py:427
  30.0 7.3 %collective-permute-start.5 = (f32[8,128]{1,0:T(8,128)S(1)}, f32[8,128]{1,0:T(8,128)S(1)}, u32[]{:S(2)}, u32[]{:S(2)}) collective-permute-start(f32[8,128]{1,0:T(8,128)S(1)} %pad.12), channel_id=1, source_target_pairs={{0,128},{64,192},{128,0},{192,64},{1,129},{65,193},{129,1},{193,65... | collective-permute-start | bytes 12296 | tf_op jit(solution)/shard_map/ppermute | solution.py:427
  31.6 6.0 %collective-permute-start.4 = (f32[8,128]{1,0:T(8,128)S(1)}, f32[8,128]{1,0:T(8,128)S(1)}, u32[]{:S(2)}, u32[]{:S(2)}) collective-permute-start(f32[8,128]{1,0:T(8,128)S(1)} %pad.12), channel_id=1, source_target_pairs={{0,64},{64,0},{128,192},{192,128},{1,65},{65,1},{129,193},{193,129... | collective-permute-start | bytes 12296 | tf_op jit(solution)/shard_map/ppermute | solution.py:427
  37.6 32.3 %collective-permute-start.7 = (f32[384,128]{1,0:T(8,128)S(1)}, f32[384,128]{1,0:T(8,128)S(1)}, u32[]{:S(2)}, u32[]{:S(2)}) collective-permute-start(f32[384,128]{1,0:T(8,128)S(1)} %get-tuple-element.84), channel_id=1, source_target_pairs={{0,64},{64,0},{128,192},{192,128},{1,65},{65,1},{129,193},{193,129... | collective-permute-start | bytes 589832 | tf_op jit(solution)/shard_map/ppermute | solution.py:427
  38.9 32.4 %collective-permute-start.8 = (f32[384,128]{1,0:T(8,128)S(1)}, f32[384,128]{1,0:T(8,128)S(1)}, u32[]{:S(2)}, u32[]{:S(2)}) collective-permute-start(f32[384,128]{1,0:T(8,128)S(1)} %get-tuple-element.85), channel_id=1, source_target_pairs={{0,128},{64,192},{128,0},{192,64},{1,129},{65,193},{129,1},{193,65... | collective-permute-start | bytes 589832 | tf_op jit(solution)/shard_map/ppermute | solution.py:427
  40.5 30.8 %collective-permute-start.9 = (f32[384,128]{1,0:T(8,128)S(1)}, f32[384,128]{1,0:T(8,128)S(1)}, u32[]{:S(2)}, u32[]{:S(2)}) collective-permute-start(f32[384,128]{1,0:T(8,128)S(1)} %get-tuple-element.86), channel_id=1, source_target_pairs={{0,192},{64,128},{128,64},{192,0},{1,193},{65,129},{129,65},{193,1... | collective-permute-start | bytes 589832 | tf_op jit(solution)/shard_map/ppermute | solution.py:427
  42.1 1.4 %collective-permute-start = (f32[2,136,128]{2,1,0:T(8,128)S(1)}, f32[2,136,128]{2,1,0:T(8,128)S(1)}, u32[]{:S(2)}, u32[]{:S(2)}) collective-permute-start(f32[2,136,128]{2,1,0:T(8,128)S(1)} %pad_maximum_fusion), channel_id=1, source_target_pairs={{0,1},{1,0},{2,3},{3,2},{4,5},{5,4},{6,7},{7,6},{8,9},{9,8},{10,11... | collective-permute-start | bytes 417800 | tf_op jit(solution)/shard_map/cond/branch_1_fun/ppermute | solution.py:474
  67.0 20.9 %collective-permute-start.12 = (f32[384,128]{1,0:T(8,128)}, f32[384,128]{1,0:T(8,128)S(1)}, u32[]{:S(2)}, u32[]{:S(2)}) collective-permute-start(f32[384,128]{1,0:T(8,128)} %get-tuple-element.90), channel_id=1, source_target_pairs={{0,64},{64,0},{128,192},{192,128},{1,65},{65,1},{129,193},{193,129... | collective-permute-start | bytes 589832 | tf_op jit(solution)/shard_map/ppermute | solution.py:427
  69.7 18.2 %collective-permute-start.13 = (f32[384,128]{1,0:T(8,128)S(1)}, f32[384,128]{1,0:T(8,128)S(1)}, u32[]{:S(2)}, u32[]{:S(2)}) collective-permute-start(f32[384,128]{1,0:T(8,128)S(1)} %get-tuple-element.91), channel_id=1, source_target_pairs={{0,128},{64,192},{128,0},{192,64},{1,129},{65,193},{129,1},{193,65... | collective-permute-start | bytes 589832 | tf_op jit(solution)/shard_map/ppermute | solution.py:427
  69.9 18.6 %collective-permute-start.14 = (f32[384,128]{1,0:T(8,128)S(1)}, f32[384,128]{1,0:T(8,128)S(1)}, u32[]{:S(2)}, u32[]{:S(2)}) collective-permute-start(f32[384,128]{1,0:T(8,128)S(1)} %get-tuple-element.92), channel_id=1, source_target_pairs={{0,192},{64,128},{128,64},{192,0},{1,193},{65,129},{129,65},{193,1... | collective-permute-start | bytes 589832 | tf_op jit(solution)/shard_map/ppermute | solution.py:427
  71.3 7.9 %collective-permute-start.11 = (f32[32,64]{1,0:T(8,128)S(1)}, f32[32,64]{1,0:T(8,128)S(1)}, u32[]{:S(2)}, u32[]{:S(2)}) collective-permute-start(f32[32,64]{1,0:T(8,128)S(1)} %get-tuple-element.99), channel_id=1, source_target_pairs={{8,0},{16,8},{24,16},{32,24},{40,32},{48,40},{56,48},{9,1},{17,9},... | collective-permute-start | bytes 24584 | tf_op jit(solution)/shard_map/ppermute | solution.py:496
  76.6 8.0 %collective-permute-start.10 = (f32[32,64]{1,0:T(8,128)S(1)}, f32[32,64]{1,0:T(8,128)S(1)}, u32[]{:S(2)}, u32[]{:S(2)}) collective-permute-start(f32[32,64]{1,0:T(8,128)S(1)} %get-tuple-element.100), channel_id=1, source_target_pairs={{0,8},{8,16},{16,24},{24,32},{32,40},{40,48},{48,56},{1,9},{9,17},... | collective-permute-start | bytes 24584 | tf_op jit(solution)/shard_map/ppermute | solution.py:495
  89.7 14.8 %collective-permute-start.15 = (f32[768,128]{1,0:T(8,128)S(1)}, f32[768,128]{1,0:T(8,128)S(1)}, u32[]{:S(2)}, u32[]{:S(2)}) collective-permute-start(f32[768,128]{1,0:T(8,128)S(1)} %get-tuple-element.94), channel_id=1, source_target_pairs={{0,64},{64,0},{128,192},{192,128},{1,65},{65,1},{129,193},{193,129... | collective-permute-start | bytes 1179656 | tf_op jit(solution)/shard_map/ppermute | solution.py:427
  92.0 26.7 %collective-permute-start.16 = (f32[768,128]{1,0:T(8,128)S(1)}, f32[768,128]{1,0:T(8,128)S(1)}, u32[]{:S(2)}, u32[]{:S(2)}) collective-permute-start(f32[768,128]{1,0:T(8,128)S(1)} %get-tuple-element.95), channel_id=1, source_target_pairs={{0,128},{64,192},{128,0},{192,64},{1,129},{65,193},{129,1},{193,65... | collective-permute-start | bytes 1179656 | tf_op jit(solution)/shard_map/ppermute | solution.py:427
  92.2 34.1 %collective-permute-start.17 = (f32[768,128]{1,0:T(8,128)S(1)}, f32[768,128]{1,0:T(8,128)S(1)}, u32[]{:S(2)}, u32[]{:S(2)}) collective-permute-start(f32[768,128]{1,0:T(8,128)S(1)} %get-tuple-element.96), channel_id=1, source_target_pairs={{0,192},{64,128},{128,64},{192,0},{1,193},{65,129},{129,65},{193,1... | collective-permute-start | bytes 1179656 | tf_op jit(solution)/shard_map/ppermute | solution.py:427

commit v3 on v2

--- a/solution.py
+++ b/solution.py
@@ -34,6 +34,7 @@
 
 VMEM = pl.BlockSpec(memory_space=pltpu.VMEM)
 SMEM = pl.BlockSpec(memory_space=pltpu.SMEM)
+ANY = pl.BlockSpec(memory_space=pl.ANY)
 
 
 def call(body, outs, args, scratch=(), mib=16, flops=0, moved=0):
@@ -56,33 +57,67 @@
     return pl.multiple_of(value * unit, unit)
 
 
-def pack_body(where, trial, seabed, down, up, beside):
-    for out, first in ((down, CX), (up, 0)):
+def pack_body(where, trial, seabed, down, up, beside, last, first, bed, strips, edges, sems):
+    edge = pl.ds(pl.multiple_of(jnp.where(where[1] == 0, CY - LANE, 0), LANE), LANE)
+    moves = [
+        (trial.at[:, :, CX - PAD :, :], last),
+        (seabed, bed),
+        (trial.at[:, :, :PAD, :], first),
+        (trial.at[:, :, :, edge], edges.at[:MEM]),
+        (strips.at[0], down),
+        (strips.at[1], up),
+        (edges, beside),
+    ]
+    copies = [pltpu.make_async_copy(*move, sems.at[i]) for i, move in enumerate(moves)]
+    for copy in copies[:4]:
+        copy.start()
+    for side, (rows, end) in enumerate(((last, True), (first, False))):
+        if end:
+            copies[0].wait()
+            copies[1].wait()
+        else:
+            copies[2].wait()
         for part in range(PARTS):
             lanes = slice(part * LANE, (part + 1) * LANE)
             for member in range(MEM):
                 at = 0
                 for field, depth in ((1, DU), (2, DV), (0, DL)):
-                    low = first - depth if first else 0
-                    out[part, pl.ds(at * MEM + member, depth, stride=MEM), :] = trial[
+                    low = PAD - depth if end else 0
+                    strips[side, part, pl.ds(at * MEM + member, depth, stride=MEM), :] = rows[
                         member, field, low : low + depth, lanes
                     ]
                     at += depth
-            low = first - DU if first else 0
-            out[part, (STRIP - 1) * MEM : STRIP * MEM, :] = jnp.zeros((MEM, LANE), F32)
-            out[part, (STRIP - 1) * MEM : (STRIP - 1) * MEM + DU, :] = seabed[low : low + DU, lanes]
-    edge = pl.ds(pl.multiple_of(jnp.where(where[1] == 0, CY - LANE, 0), LANE), LANE)
-    for member in range(MEM):
-        for field in range(3):
-            beside[member * 3 + field] = trial[member, field, :, edge]
-    beside[MEM * 3] = seabed[:, edge]
+            low, to = CX - DU if end else 0, (STRIP - 1) * MEM
+            strips[side, part, to : to + MEM, :] = jnp.zeros((MEM, LANE), F32)
+            strips[side, part, to : to + DU, :] = bed[low : low + DU, lanes]
+        copies[4 + side].start()
+    for same in range(3):
+        edges[MEM, same] = bed[:, edge]
+    copies[3].wait()
+    for copy in copies[6:]:
+        copy.start()
+    for copy in copies[4:]:
+        copy.wait()
 
 
 def pack(where, trial, seabed):
     strip = shaped(PARTS, STRIP * MEM, LANE)
-    return call(
-        pack_body, (strip, strip, shaped(MEM * 3 + 1, CX, LANE)), (where, trial, seabed)
-    )
+    rows = pltpu.VMEM((MEM, 3, PAD, CY), F32)
+    return pl.pallas_call(
+        pack_body,
+        out_shape=[strip, strip, shaped(MEM + 1, 3, CX, LANE)],
+        in_specs=[SMEM, ANY, ANY],
+        out_specs=[ANY] * 3,
+        scratch_shapes=[
+            rows,
+            rows,
+            pltpu.VMEM((CX, CY), F32),
+            pltpu.VMEM((2,) + strip.shape, F32),
+            pltpu.VMEM((MEM + 1, 3, CX, LANE), F32),
+            pltpu.SemaphoreType.DMA((7,)),
+        ],
+        compiler_params=pltpu.CompilerParams(vmem_limit_bytes=60 * 1024 * 1024),
+    )(where, trial, seabed)
 
 
 def row_at(row):
@@ -140,7 +175,7 @@
                 fields[field][part, at, :] = trial[
                     member, field, :, part * LANE : (part + 1) * LANE
                 ]
-            fields[field][PARTS, at, :] = beside[member * 3 + field] * keep
+            fields[field][PARTS, at, :] = beside[member, field] * keep
     depth = fields[3]
     for row in range(CX):
         at = slice(row * MEM, (row + 1) * MEM)
@@ -149,7 +184,7 @@
                 seabed[row : row + 1, part * LANE : (part + 1) * LANE], (MEM, LANE)
             )
         depth[PARTS, at, :] = jnp.broadcast_to(
-            beside[MEM * 3, row : row + 1, :] * keep, (MEM, LANE)
+            beside[MEM, 0, row : row + 1, :] * keep, (MEM, LANE)
         )
 
     def level_row(row, carry):
@@ -259,9 +294,12 @@
         axis=1,
     )
     total = sense(levels, sum(s[...] for s in stencils))
+    lane = lax.broadcasted_iota(jnp.int32, (1, LANE), 1)
+    total = jnp.where(lane < GRP * OBS, total[: MEM // 2, :], total[MEM // 2 :, :])
     for to in range(GRP * SUB * 2):
-        state[to, :MEM, :] = total
-        state[to, MEM:, :] = known[...]
+        state[3 * to] = total
+        state[3 * to + 1] = known[0]
+        state[3 * to + 2] = known[1]
 
     for field in range(3):
         for part in range(PARTS):
@@ -273,30 +311,52 @@
             ]
 
 
-def outer_forecast(where, inner, above, below, corner, known, stencils):
+def outer_forecast(where, inner, strips, known, stencils):
     block = shaped(3 * MIDDLE, LANE)
     return call(
         outer_body,
         (block,) * GRP
-        + (shaped(GRP * SUB * 2, 2 * MEM, LANE), shaped(3, PARTS, 2 * HALF, LANE)),
-        (where, inner, above, below, corner, known, *stencils),
+        + (shaped(3 * GRP * SUB * 2, MEM // 2, LANE), shaped(3, PARTS, 2 * HALF, LANE)),
+        (where, inner, *strips, known, *stencils),
         [pltpu.VMEM((PARTS + 1, 2 * PAD * MEM, LANE), F32)] * 8,
     )
 
 
+def turned_rows(block, field, member):
+    return block[pl.ds(field * CX * MEM + member, CX, stride=MEM), :]
+
+
 def unpack_body(where, *refs):
-    blocks, out = refs[:GRP], refs[GRP]
-    for other in range(GRP):
+    blocks, out = refs[:-1], refs[-1]
+    for other, block in enumerate(blocks):
         at = pl.ds(aligned(jnp.bitwise_xor(where[0], other), LANE), LANE)
         for field in range(3):
             for member in range(MEM):
-                out[member, field, :, at] = blocks[other][
-                    pl.ds(field * CX * MEM + member, CX, stride=MEM), :
-                ]
+                out[member, field, :, at] = turned_rows(block, field, member)
+
+
+def unpack_last_body(where, block, _, out, held, sem):
+    for field in range(3):
+        for member in range(MEM):
+            held[member, field] = turned_rows(block, field, member)
+    at = pl.ds(aligned(jnp.bitwise_xor(where[0], GRP - 1), LANE), LANE)
+    copy = pltpu.make_async_copy(held, out.at[:, :, :, at], sem)
+    copy.start()
+    copy.wait()
 
 
 def unpack(where, blocks):
-    return call(unpack_body, (shaped(MEM, 3, CX, CY),), (where, *blocks))[0]
+    out = shaped(MEM, 3, CX, CY)
+    early = call(unpack_body, (out,), (where, *blocks[:-1]))[0]
+    return pl.pallas_call(
+        unpack_last_body,
+        out_shape=out,
+        in_specs=[SMEM, VMEM, ANY],
+        out_specs=ANY,
+        scratch_shapes=[pltpu.VMEM((MEM, 3, CX, LANE), F32), pltpu.SemaphoreType.DMA],
+        input_output_aliases={2: 0},
+        compiler_params=pltpu.CompilerParams(vmem_limit_bytes=16 * 1024 * 1024),
+    )(where, blocks[-1], early)
 
 
 def spread_out_body(where, inner, outer, out):
@@ -322,22 +382,27 @@
 def products_body(where, states, out, wanted_at):
     group = where[0]
     lane = lax.broadcasted_iota(jnp.int32, (1, LANE), 1)
+
+    def unfolded(at):
+        value = states[at]
+        return jnp.concatenate([value, pltpu.roll(value, LANE // 2, 1)], axis=0)
+
     left, right = [], []
     for block in range(SUB * 2):
-        noisy, other = [jnp.zeros((MEM, LANE), F32)] * GRP, jnp.zeros((MEM, LANE), F32)
+        noisy = [jnp.zeros((MEM, LANE), F32)] * GRP
+        other = jnp.zeros((MEM // 2, LANE), F32)
         for source in range(GRP):
-            held = states[source * (SUB * 2) + block, MEM:, :]
-            here = lane // OBS == source
+            at = 3 * (source * (SUB * 2) + block)
+            held, here = unfolded(at + 1), lane // OBS == source
             for part in range(GRP):
                 turned = pltpu.roll(held, (source - part) * OBS % LANE, 1)
                 noisy[part] = jnp.where(here, turned, noisy[part])
-            turned = pltpu.roll(held, (source - GRP) * OBS % LANE, 1)
-            other = jnp.where(here, turned, other)
+            other = jnp.where(here, pltpu.roll(states[at + 2], source * OBS, 1), other)
         for part in range(GRP):
             wanted_at[block, part] = noisy[part]
         seen = jnp.concatenate(
             [
-                states[jnp.bitwise_xor(group, s) * (SUB * 2) + block, :MEM, :]
+                unfolded(3 * (jnp.bitwise_xor(group, s) * (SUB * 2) + block))
                 for s in range(GRP)
             ],
             axis=0,
@@ -445,7 +510,7 @@
     below = lax.ppermute(up, TILE, backward)
     beside = lax.ppermute(beside, "cores", [(0, 1), (1, 0)])
 
-    count, wide = GRP * OBS, LANE // 2
+    count = GRP * OBS
     anchor = stencil_cells[:, 0].astype(F32)
     pair = jnp.stack([anchor, anchor + 1.0])
     uses = stencil_weights.T
@@ -454,31 +519,31 @@
     stencil = (stencil[:, :, None, :] * slot[None, None, :, None]).reshape(3, 2 * count)
     stencil = jnp.pad(stencil, ((0, MEM - 3), (0, 0)))
     noisy = observed[:, None] + jnp.sqrt(variances)[:, None] * perturbations
-    noisy = noisy.T.reshape(GRP, MEM, OBS).transpose(1, 0, 2).reshape(MEM, count)
+    noisy = noisy.T.reshape(GRP, 2, MEM // 2, OBS).transpose(2, 1, 0, 3).reshape(MEM // 2, LANE)
     three = lax.dynamic_slice_in_dim(
         jnp.pad(region_mask.astype(F32), ((0, 0), (1, 1))), region, 3, axis=1
     )
     three = jnp.concatenate([three.T, variances[None]], axis=0)
-    known = jnp.concatenate(
-        [noisy, jnp.pad(three, ((0, MEM - 4), (0, wide - OBS)))], axis=1
-    )
-
+    known = jnp.stack([noisy, jnp.pad(three, ((0, 0), (0, LANE - OBS)))])
+
+    stencil, beside = lax.optimization_barrier((stencil, beside))
+    stencils = exchange([stencil] * GRP)
     *middle, inner = inner_forecast(where, trial, seabed, beside)
-    stencil, inner = lax.optimization_barrier((stencil, inner))
-    stencils = exchange([stencil] * GRP)
     above, below, _ = lax.optimization_barrier((above, below, stencils[1:]))
-    edge = jnp.where(core == 0, PARTS - 1, 0)
 
     def outer_rows(above, below, inner, known, stencils):
+        edge = jnp.where(core == 0, PARTS - 1, 0)
         ends = [lax.dynamic_index_in_dim(s, edge, 0, keepdims=False) for s in (above, below)]
         corner = lax.ppermute(jnp.stack(ends), "cores", [(0, 1), (1, 0)])
-        *outer, state, rest = outer_forecast(where, inner, above, below, corner, known, stencils)
+        *outer, state, rest = outer_forecast(
+            where, inner, (above, below, corner), known, stencils
+        )
         return outer, rest, lax.all_to_all(state, SIDE, 0, 0, tiled=True)
 
     def nothing(*args):
         block = jnp.zeros((3 * MIDDLE, LANE), F32)
         rest = jnp.zeros((3, PARTS, 2 * HALF, LANE), F32)
-        return [block] * GRP, rest, jnp.zeros((GRP * SUB * 2, 2 * MEM, LANE), F32)
+        return [block] * GRP, rest, jnp.zeros((3 * GRP * SUB * 2, MEM // 2, LANE), F32)
 
     middle, *_ = lax.optimization_barrier((middle, stencils[1:]))
     middle = exchange(middle)
@@ -488,12 +553,13 @@
     outer = exchange(outer)
     propagated_trials = spread_out(where, inner, rest)
 
-    up_region = [(i + 1, i) for i in range(REG - 1)]
-    down_region = [(i, i + 1) for i in range(REG - 1)]
+    pairs = [
+        (r * SUB + q, (r + 1) * SUB + (q ^ 2)) for r in range(REG - 1) for q in range(SUB)
+    ]
     products = region_products(where, states)
     products, _ = lax.optimization_barrier((products, middle[1:]))
-    from_above = lax.ppermute(products[2 * E :], "reg", down_region)
-    from_below = lax.ppermute(products[:E], "reg", up_region)
+    from_above = lax.ppermute(products[2 * E :], TILE, pairs)
+    from_below = lax.ppermute(products[:E], TILE, [(b, a) for a, b in pairs])
     weights = solve(where, products, from_above, from_below)
     analysis_updates = unpack(where, exchange(increments(where, weights, middle, outer)))
     return (propagated_trials, analysis_updates)

time: 131 us -> 126 us (0.962); the launches traced: 128 us -> 125 us
  Pallas kernels: 24.8 us -> 28 us
  local copies, waits for them, and re-layouts: 3.65 us -> 0.5 us
  starting transfers between devices: 37.2 us -> 35.7 us
    pallas_call x0 -> x2, Pallas kernels: none -> 4.04 us  [the longest x1 2.68 us: pack(): pl.pallas_call(pack_body, out_shape=[strip, strip, shaped(MEM + 1, 3, CX,...]
    unnamed x20 -> x16, local copies, waits for them, and re-layouts: 2.28 us -> 0.04 us
    all_to_all x1, blocking collectives: 18.6 us -> 17.3 us  [outer_rows(): return (outer, rest, lax.all_to_all(state, SIDE, 0, 0, tiled=True))]
    pallas_call x8 -> x7, Pallas kernels: 24.8 us -> 24 us  [call(): pl.pallas_call(body, out_shape=list(outs), in_specs=[SMEM] + [VMEM] * (le...]
  transfers between devices with their start and end apart: 18 -> 18, of which waited for: 9 -> 9; matrix products, arithmetic and copies ran while one was open for 1% -> 0% of each run, Pallas kernels for 16% -> 18%
where the time goes in v3:
time: 126 us; the launch traced here: 125 us
  waiting for transfers between devices  42.6 us (34%)
  starting transfers between devices  35.7 us (28%)
  Pallas kernels  28 us (22%)
  blocking collectives  17.3 us (14%)
    ppermute x12, waiting for transfers between devices, exchange(): lax.ppermute(blocks[s], 'grp', [(i, i ^ s) for i in range(GRP)])  35.5 us
    pallas_call x7, Pallas kernels, call(): pl.pallas_call(body, out_shape=list(outs), in_specs=[SMEM] + [VMEM] * (le...  24 us
    all_to_all x1, blocking collectives, outer_rows(): return (outer, rest, lax.all_to_all(state, SIDE, 0, 0, tiled=True))  17.3 us
    ppermute x12, starting transfers between devices, exchange(): lax.ppermute(blocks[s], 'grp', [(i, i ^ s) for i in range(GRP)])  15.6 us
    ppermute x1, starting transfers between devices, on_device(): above = lax.ppermute(down, TILE, forward)  8.2 us
    ppermute x1, starting transfers between devices, on_device(): below = lax.ppermute(up, TILE, backward)  4.64 us
    ppermute x1, waiting for transfers between devices, on_device(): from_above = lax.ppermute(products[2 * E:], TILE, pairs)  4.29 us
    ppermute x1, starting transfers between devices, on_device(): from_below = lax.ppermute(products[:E], TILE, [(b, a) for a, b in pairs])  3.61 us
  transfers between devices with their start and end apart: 18, of which 9 were waited for; matrix products, arithmetic and copies ran while one was open for 0% of the time, Pallas kernels for 18%

profile of v3, /device:TPU:38, one launch (start us, length us, event | category | flops | bytes accessed | tf_op | source)
XLA Modules:
  0.0 125.3 jit_solution(5830531509522942971)
XLA Ops:
  0.6 0.0 copy-start.1
  0.6 0.0 copy-start
  0.7 0.1 pad_add_fusion.where
  0.8 2.7 %shard_map.95 = (f32[4,136,128]{2,1,0:T(8,128)}, f32[4,136,128]{2,1,0:T(8,128)}, f32[9,3,32,128]{3,2,1,0:T(8,128)}) custom-call(s32[4]{0:T(128)S(1)} %pad_add_fusion.where, f32[8,3,32,512]{3,2,1,0:T(8,128)} %trial.3, f32[32,512]{1,0:T(8,128)} %seabed.3), custom_call_target="tpu_custom_call" | custom-call | tf_op jit(solution)/shard_map/pallas_call | solution.py:106
  3.5 8.2 %collective-permute-start.2 = (f32[4,136,128]{2,1,0:T(8,128)}, f32[4,136,128]{2,1,0:T(8,128)S(1)}, u32[]{:S(2)}, u32[]{:S(2)}) collective-permute-start(f32[4,136,128]{2,1,0:T(8,128)} %get-tuple-element.68), channel_id=1, source_target_pairs={{0,2},{2,4},{4,6},{6,8},{8,10},{10,12},{12,14},{14,16},{16,18},{18... | collective-permute-start | bytes 835592 | tf_op jit(solution)/shard_map/ppermute | solution.py:509
  11.7 4.6 %collective-permute-start.3 = (f32[4,136,128]{2,1,0:T(8,128)}, f32[4,136,128]{2,1,0:T(8,128)S(1)}, u32[]{:S(2)}, u32[]{:S(2)}) collective-permute-start(f32[4,136,128]{2,1,0:T(8,128)} %get-tuple-element.69), channel_id=1, source_target_pairs={{2,0},{4,2},{6,4},{8,6},{10,8},{12,10},{14,12},{16,14},{18,16},{20... | collective-permute-start | bytes 835592 | tf_op jit(solution)/shard_map/ppermute | solution.py:510
  16.3 0.1 collective-permute-start.1
  16.5 0.1 mul.34
  16.6 0.1 mul.35
  16.7 0.1 mul.33
  16.9 0.1 add_bitcast_fusion
  16.9 1.5 %collective-permute-done.1.beside = f32[9,3,32,128]{3,2,1,0:T(8,128)S(1)} collective-permute-done((f32[9,3,32,128]{3,2,1,0:T(8,128)}, f32[9,3,32,128]{3,2,1,0:T(8,128)S(1)}, u32[]{:S(2)}, u32[]{:S(2)}) %collective-permute-start.1) | collective-permute-done | bytes 442400 | tf_op jit(solution)/shard_map/ppermute | solution.py:511
  18.4 1.8 %collective-permute-start.6 = (f32[8,128]{1,0:T(8,128)S(1)}, f32[8,128]{1,0:T(8,128)S(1)}, u32[]{:S(2)}, u32[]{:S(2)}) collective-permute-start(f32[8,128]{1,0:T(8,128)S(1)} %pad.12), channel_id=1, source_target_pairs={{0,192},{64,128},{128,64},{192,0},{1,193},{65,129},{129,65},{193,1... | collective-permute-start | bytes 12296 | tf_op jit(solution)/shard_map/ppermute | solution.py:492
  20.3 1.5 %collective-permute-start.5 = (f32[8,128]{1,0:T(8,128)S(1)}, f32[8,128]{1,0:T(8,128)S(1)}, u32[]{:S(2)}, u32[]{:S(2)}) collective-permute-start(f32[8,128]{1,0:T(8,128)S(1)} %pad.12), channel_id=1, source_target_pairs={{0,128},{64,192},{128,0},{192,64},{1,129},{65,193},{129,1},{193,65... | collective-permute-start | bytes 12296 | tf_op jit(solution)/shard_map/ppermute | solution.py:492
  21.8 1.3 %collective-permute-start.4 = (f32[8,128]{1,0:T(8,128)S(1)}, f32[8,128]{1,0:T(8,128)S(1)}, u32[]{:S(2)}, u32[]{:S(2)}) collective-permute-start(f32[8,128]{1,0:T(8,128)S(1)} %pad.12), channel_id=1, source_target_pairs={{0,64},{64,0},{128,192},{192,128},{1,65},{65,1},{129,193},{193,129... | collective-permute-start | bytes 12296 | tf_op jit(solution)/shard_map/ppermute | solution.py:492
  23.1 0.1 copy.15
  23.2 0.1 stack_reshape.3
  23.3 9.7 %shard_map.96 = (f32[384,128]{1,0:T(8,128)S(1)}, f32[384,128]{1,0:T(8,128)S(1)}, f32[384,128]{1,0:T(8,128)S(1)}, f32[384,128]{1,0:T(8,128)S(1)}, f32[4,5,256,128]{3,2,1,0:T(8,128)}) custom-call(s32[4]{0:T(128)S(1)} %pad_add_fusion.where, f32[8,3,32,512]{3,2,1,0:T(8,128)S(1)} %copy-done, f32[32,512]{1,0:T(8,128)S(1)} %copy-done.1, ...), custom_call_target="tpu_custom_call" | custom-call | flops 10000000 | bytes 32000000 | tf_op jit(solution)/shard_map/pallas_call | solution.py:41
  33.0 4.1 %collective-permute-done.5 = f32[8,128]{1,0:T(8,128)S(1)} collective-permute-done((f32[8,128]{1,0:T(8,128)S(1)}, f32[8,128]{1,0:T(8,128)S(1)}, u32[]{:S(2)}, u32[]{:S(2)}) %collective-permute-start.5) | collective-permute-done | bytes 4128 | tf_op jit(solution)/shard_map/ppermute | solution.py:492
  37.2 0.4 collective-permute-done.4
  37.5 1.2 collective-permute-start.7
  38.7 1.7 %collective-permute-start.8 = (f32[384,128]{1,0:T(8,128)S(1)}, f32[384,128]{1,0:T(8,128)S(1)}, u32[]{:S(2)}, u32[]{:S(2)}) collective-permute-start(f32[384,128]{1,0:T(8,128)S(1)} %get-tuple-element.80), channel_id=1, source_target_pairs={{0,128},{64,192},{128,0},{192,64},{1,129},{65,193},{129,1},{193,65... | collective-permute-start | bytes 589832 | tf_op jit(solution)/shard_map/ppermute | solution.py:492
  40.4 0.6 collective-permute-start.9
  41.1 22.4 %conditional.1 = (f32[384,128]{1,0:T(8,128)S(1)}, f32[384,128]{1,0:T(8,128)}, f32[384,128]{1,0:T(8,128)}, f32[384,128]{1,0:T(8,128)S(1)}, f32[3,4,128,128]{3,2,1,0:T(8,128)S(1)}, /*index=5*/f32[96,4,128]{2,1,0:T(4,128)S(1)}) conditional(s32[]{:T(128)} %convert_element_type.41, () %tuple.21, (s32[]{:T(128)}, f32[4,136,128]{2,1,0:T(8,128)S(1)}, ...), branch_computations={%region_0.1_spmd, %region_1.2_spmd} | conditional | flops 34818 | bytes 1769544 | solution.py:550
  41.1 0.1 collective-permute-start
  41.2 1.3 %collective-permute-done.corner = f32[2,136,128]{2,1,0:T(8,128)S(1)} collective-permute-done((f32[2,136,128]{2,1,0:T(8,128)S(1)}, f32[2,136,128]{2,1,0:T(8,128)S(1)}, u32[]{:S(2)}, u32[]{:S(2)}) %collective-permute-start) | collective-permute-done | bytes 139296 | tf_op jit(solution)/shard_map/cond/branch_1_fun/ppermute | solution.py:537
  42.6 3.6 %branch_1_fun.1 = (f32[384,128]{1,0:T(8,128)S(1)}, f32[384,128]{1,0:T(8,128)}, f32[384,128]{1,0:T(8,128)}, f32[384,128]{1,0:T(8,128)S(1)}, f32[96,4,128]{2,1,0:T(4,128)S(1)}, /*index=5*/f32[3,4,128,128]{3,2,1,0:T(8,128)S(1)}) custom-call(s32[4]{0:T(128)S(1)} %get-tuple-element.20.where, f32[4,5,256,128]{3,2,1,0:T(8,128)} %get-tuple-element.21.inner, ...), custom_call_target="tpu_custom_call" | custom-call | tf_op jit(solution)/shard_map/cond/branch_1_fun/pallas_call | solution.py:41
  46.2 17.3 %all_to_all.4 = f32[96,4,128]{2,1,0:T(4,128)S(1)} all-to-all(f32[96,4,128]{2,1,0:T(4,128)S(1)} %get-tuple-element.35), channel_id=1, replica_groups=mesh['grp'=4,'reg'=8,'sub'=4,'cores'=2] {'grp','sub','cores'}, dimensions={0} | all-to-all | bytes 393216 | tf_op jit(solution)/shard_map/cond/branch_1_fun/all_to_all | solution.py:541
  63.4 1.2 shard_map.98.own
  64.7 2.4 %collective-permute-start.12 = (f32[384,128]{1,0:T(8,128)}, f32[384,128]{1,0:T(8,128)S(1)}, u32[]{:S(2)}, u32[]{:S(2)}) collective-permute-start(f32[384,128]{1,0:T(8,128)} %get-tuple-element.85), channel_id=1, source_target_pairs={{0,64},{64,0},{128,192},{192,128},{1,65},{65,1},{129,193},{193,129... | collective-permute-start | bytes 589832 | tf_op jit(solution)/shard_map/ppermute | solution.py:492
  67.0 0.4 collective-permute-start.13
  67.4 1.2 collective-permute-start.14
  68.6 3.6 %collective-permute-start.11 = (f32[32,64]{1,0:T(8,128)S(1)}, f32[32,64]{1,0:T(8,128)S(1)}, u32[]{:S(2)}, u32[]{:S(2)}) collective-permute-start(f32[32,64]{1,0:T(8,128)S(1)} %get-tuple-element.94), channel_id=1, source_target_pairs={{12,0},{14,2},{8,4},{10,6},{20,8},{22,10},{16,12},{18,14},{28,16},... | collective-permute-start | bytes 24584 | tf_op jit(solution)/shard_map/ppermute | solution.py:562
  72.2 3.4 %collective-permute-start.10 = (f32[32,64]{1,0:T(8,128)S(1)}, f32[32,64]{1,0:T(8,128)S(1)}, u32[]{:S(2)}, u32[]{:S(2)}) collective-permute-start(f32[32,64]{1,0:T(8,128)S(1)} %get-tuple-element.95), channel_id=1, source_target_pairs={{0,12},{2,14},{4,8},{6,10},{8,20},{10,22},{12,16},{14,18},{16,28},... | collective-permute-start | bytes 24584 | tf_op jit(solution)/shard_map/ppermute | solution.py:561
  75.7 4.3 %collective-permute-done.10.low = f32[32,64]{1,0:T(8,128)S(1)} collective-permute-done((f32[32,64]{1,0:T(8,128)S(1)}, f32[32,64]{1,0:T(8,128)S(1)}, u32[]{:S(2)}, u32[]{:S(2)}) %collective-permute-start.10) | collective-permute-done | bytes 8224 | tf_op jit(solution)/shard_map/ppermute | solution.py:561
  80.0 3.2 %shard_map.99.refs_0_ = f32[32,32]{1,0:T(8,128)S(1)} custom-call(s32[4]{0:T(128)S(1)} %pad_add_fusion.where, f32[96,64]{1,0:T(8,128)S(1)} %shard_map.98.own, f32[32,64]{1,0:T(8,128)S(1)} %collective-permute-done.10.low, f32[32,64]{1,0:T(8,128)S(1)} %collective-permute-done.11.high), custom_call_target="tpu_custom_call" | custom-call | tf_op jit(solution)/shard_map/pallas_call | solution.py:41
  83.2 0.0 collective-permute-done.13.refs_7_
  83.2 2.9 %collective-permute-done.14.refs_8_ = f32[384,128]{1,0:T(8,128)S(1)} collective-permute-done((f32[384,128]{1,0:T(8,128)S(1)}, f32[384,128]{1,0:T(8,128)S(1)}, u32[]{:S(2)}, u32[]{:S(2)}) %collective-permute-start.14) | collective-permute-done | bytes 196640 | tf_op jit(solution)/shard_map/ppermute | solution.py:492
  86.2 1.1 shard_map.100
  87.3 0.1 collective-permute-start.16
  87.4 2.5 %collective-permute-start.17 = (f32[768,128]{1,0:T(8,128)S(1)}, f32[768,128]{1,0:T(8,128)S(1)}, u32[]{:S(2)}, u32[]{:S(2)}) collective-permute-start(f32[768,128]{1,0:T(8,128)S(1)} %get-tuple-element.91), channel_id=1, source_target_pairs={{0,128},{64,192},{128,0},{192,64},{1,129},{65,193},{129,1},{193,65... | collective-permute-start | bytes 1179656 | tf_op jit(solution)/shard_map/ppermute | solution.py:492
  89.9 1.0 collective-permute-start.15
  90.9 3.2 %shard_map.97 = f32[8,3,32,512]{3,2,1,0:T(8,128)} custom-call(s32[4]{0:T(128)S(1)} %pad_add_fusion.where, f32[4,5,256,128]{3,2,1,0:T(8,128)} %get-tuple-element.67.inner, f32[3,4,128,128]{3,2,1,0:T(8,128)S(1)} %get-tuple-element.73.outer), custom_call_target="tpu_custom_call" | custom-call | tf_op jit(solution)/shard_map/pallas_call | solution.py:41
  94.1 8.3 %collective-permute-done.16.refs_1_ = f32[768,128]{1,0:T(8,128)S(1)} collective-permute-done((f32[768,128]{1,0:T(8,128)S(1)}, f32[768,128]{1,0:T(8,128)S(1)}, u32[]{:S(2)}, u32[]{:S(2)}) %collective-permute-start.16) | collective-permute-done | bytes 393248 | tf_op jit(solution)/shard_map/ppermute | solution.py:492
  102.4 14.0 %collective-permute-done.17.refs_2_ = f32[768,128]{1,0:T(8,128)S(1)} collective-permute-done((f32[768,128]{1,0:T(8,128)S(1)}, f32[768,128]{1,0:T(8,128)S(1)}, u32[]{:S(2)}, u32[]{:S(2)}) %collective-permute-start.17) | collective-permute-done | bytes 393248 | tf_op jit(solution)/shard_map/ppermute | solution.py:492
  116.3 1.9 %shard_map.101._ = f32[8,3,32,512]{3,2,1,0:T(8,128)} custom-call(s32[4]{0:T(128)S(1)} %pad_add_fusion.where, f32[768,128]{1,0:T(8,128)S(1)} %get-tuple-element.89.refs_0_, f32[768,128]{1,0:T(8,128)S(1)} %collective-permute-done.16.refs_1_, f32[768,128]{1,0:T(8,128)S(1)} %collective-permute-done.17.refs_2_), custom_call_target="tpu_custom_call" | custom-call | tf_op jit(solution)/shard_map/pallas_call | solution.py:41
  118.2 5.7 %collective-permute-done.15.block = f32[768,128]{1,0:T(8,128)S(1)} collective-permute-done((f32[768,128]{1,0:T(8,128)S(1)}, f32[768,128]{1,0:T(8,128)S(1)}, u32[]{:S(2)}, u32[]{:S(2)}) %collective-permute-start.15) | collective-permute-done | bytes 393248 | tf_op jit(solution)/shard_map/ppermute | solution.py:492
  124.0 1.4 %shard_map.102 = f32[8,3,32,512]{3,2,1,0:T(8,128)} custom-call(s32[4]{0:T(128)S(1)} %pad_add_fusion.where, f32[768,128]{1,0:T(8,128)S(1)} %collective-permute-done.15.block, f32[8,3,32,512]{3,2,1,0:T(8,128)} %shard_map.101._), custom_call_target="tpu_custom_call", output_to_operand_aliasing={{}: (2, {})} | custom-call | tf_op jit(solution)/shard_map/pallas_call | solution.py:351
  (39 shorter events, 0.2 us)
Async XLA Ops:
  0.6 22.7 %copy-start.1 = (f32[32,512]{1,0:T(8,128)S(1)}, f32[32,512]{1,0:T(8,128)}, u32[]{:S(2)}) copy-start(f32[32,512]{1,0:T(8,128)} %seabed.3) | copy-start | bytes 196612
  0.6 22.6 %copy-start = (f32[8,3,32,512]{3,2,1,0:T(8,128)S(1)}, f32[8,3,32,512]{3,2,1,0:T(8,128)}, u32[]{:S(2)}) copy-start(f32[8,3,32,512]{3,2,1,0:T(8,128)} %trial.3) | copy-start | bytes 4718596
  0.7 15.8 %copy-start.7 = (s32[16,4]{0,1:T(4,128)S(1)}, s32[16,4]{0,1:T(4,128)}, u32[]{:S(2)}) copy-start(s32[16,4]{0,1:T(4,128)} %param.15) | copy-start | bytes 772
  0.7 15.8 %copy-start.6 = (f32[16]{0:T(128)S(1)}, f32[16]{0:T(128)}, u32[]{:S(2)}) copy-start(f32[16]{0:T(128)} %param.13) | copy-start | bytes 196
  0.7 16.0 %copy-start.3 = (s32[16,8]{0,1:T(8,128)S(1)}, s32[16,8]{0,1:T(8,128)}, u32[]{:S(2)}) copy-start(s32[16,8]{0,1:T(8,128)} %param.17) | copy-start | bytes 1540
  0.7 16.0 %copy-start.4 = (f32[16,4]{0,1:T(4,128)S(1)}, f32[16,4]{0,1:T(4,128)}, u32[]{:S(2)}) copy-start(f32[16,4]{0,1:T(4,128)} %param.16) | copy-start | bytes 772
  0.7 16.1 %copy-start.2 = (f32[16,32]{1,0:T(8,128)S(1)}, f32[16,32]{1,0:T(8,128)}, u32[]{:S(2)}) copy-start(f32[16,32]{1,0:T(8,128)} %param.14) | copy-start | bytes 6148
  0.7 16.1 %copy-start.5 = (f32[16]{0:T(128)S(1)}, f32[16]{0:T(128)}, u32[]{:S(2)}) copy-start(f32[16]{0:T(128)} %param.12) | copy-start | bytes 196
  3.5 37.5 %collective-permute-start.2 = (f32[4,136,128]{2,1,0:T(8,128)}, f32[4,136,128]{2,1,0:T(8,128)S(1)}, u32[]{:S(2)}, u32[]{:S(2)}) collective-permute-start(f32[4,136,128]{2,1,0:T(8,128)} %get-tuple-element.68), channel_id=1, source_target_pairs={{0,2},{2,4},{4,6},{6,8},{8,10},{10,12},{12,14},{14,16},{16,18},{18... | collective-permute-start | bytes 835592 | tf_op jit(solution)/shard_map/ppermute | solution.py:509
  11.7 29.3 %collective-permute-start.3 = (f32[4,136,128]{2,1,0:T(8,128)}, f32[4,136,128]{2,1,0:T(8,128)S(1)}, u32[]{:S(2)}, u32[]{:S(2)}) collective-permute-start(f32[4,136,128]{2,1,0:T(8,128)} %get-tuple-element.69), channel_id=1, source_target_pairs={{2,0},{4,2},{6,4},{8,6},{10,8},{12,10},{14,12},{16,14},{18,16},{20... | collective-permute-start | bytes 835592 | tf_op jit(solution)/shard_map/ppermute | solution.py:510
  16.3 2.1 %collective-permute-start.1 = (f32[9,3,32,128]{3,2,1,0:T(8,128)}, f32[9,3,32,128]{3,2,1,0:T(8,128)S(1)}, u32[]{:S(2)}, u32[]{:S(2)}) collective-permute-start(f32[9,3,32,128]{3,2,1,0:T(8,128)} %get-tuple-element.65), channel_id=1, source_target_pairs={{0,1},{1,0},{2,3},{3,2},{4,5},{5,4},{6,7},{7,6},{8,9},{9,8},{10,11... | collective-permute-start | bytes 1327112 | tf_op jit(solution)/shard_map/ppermute | solution.py:511
  18.4 14.6 %collective-permute-start.6 = (f32[8,128]{1,0:T(8,128)S(1)}, f32[8,128]{1,0:T(8,128)S(1)}, u32[]{:S(2)}, u32[]{:S(2)}) collective-permute-start(f32[8,128]{1,0:T(8,128)S(1)} %pad.12), channel_id=1, source_target_pairs={{0,192},{64,128},{128,64},{192,0},{1,193},{65,129},{129,65},{193,1... | collective-permute-start | bytes 12296 | tf_op jit(solution)/shard_map/ppermute | solution.py:492
  20.3 16.9 %collective-permute-start.5 = (f32[8,128]{1,0:T(8,128)S(1)}, f32[8,128]{1,0:T(8,128)S(1)}, u32[]{:S(2)}, u32[]{:S(2)}) collective-permute-start(f32[8,128]{1,0:T(8,128)S(1)} %pad.12), channel_id=1, source_target_pairs={{0,128},{64,192},{128,0},{192,64},{1,129},{65,193},{129,1},{193,65... | collective-permute-start | bytes 12296 | tf_op jit(solution)/shard_map/ppermute | solution.py:492
  21.8 15.7 %collective-permute-start.4 = (f32[8,128]{1,0:T(8,128)S(1)}, f32[8,128]{1,0:T(8,128)S(1)}, u32[]{:S(2)}, u32[]{:S(2)}) collective-permute-start(f32[8,128]{1,0:T(8,128)S(1)} %pad.12), channel_id=1, source_target_pairs={{0,64},{64,0},{128,192},{192,128},{1,65},{65,1},{129,193},{193,129... | collective-permute-start | bytes 12296 | tf_op jit(solution)/shard_map/ppermute | solution.py:492
  37.5 29.9 %collective-permute-start.7 = (f32[384,128]{1,0:T(8,128)S(1)}, f32[384,128]{1,0:T(8,128)S(1)}, u32[]{:S(2)}, u32[]{:S(2)}) collective-permute-start(f32[384,128]{1,0:T(8,128)S(1)} %get-tuple-element.79), channel_id=1, source_target_pairs={{0,64},{64,0},{128,192},{192,128},{1,65},{65,1},{129,193},{193,129... | collective-permute-start | bytes 589832 | tf_op jit(solution)/shard_map/ppermute | solution.py:492
  38.7 29.9 %collective-permute-start.8 = (f32[384,128]{1,0:T(8,128)S(1)}, f32[384,128]{1,0:T(8,128)S(1)}, u32[]{:S(2)}, u32[]{:S(2)}) collective-permute-start(f32[384,128]{1,0:T(8,128)S(1)} %get-tuple-element.80), channel_id=1, source_target_pairs={{0,128},{64,192},{128,0},{192,64},{1,129},{65,193},{129,1},{193,65... | collective-permute-start | bytes 589832 | tf_op jit(solution)/shard_map/ppermute | solution.py:492
  40.4 28.2 %collective-permute-start.9 = (f32[384,128]{1,0:T(8,128)S(1)}, f32[384,128]{1,0:T(8,128)S(1)}, u32[]{:S(2)}, u32[]{:S(2)}) collective-permute-start(f32[384,128]{1,0:T(8,128)S(1)} %get-tuple-element.81), channel_id=1, source_target_pairs={{0,192},{64,128},{128,64},{192,0},{1,193},{65,129},{129,65},{193,1... | collective-permute-start | bytes 589832 | tf_op jit(solution)/shard_map/ppermute | solution.py:492
  41.1 1.4 %collective-permute-start = (f32[2,136,128]{2,1,0:T(8,128)S(1)}, f32[2,136,128]{2,1,0:T(8,128)S(1)}, u32[]{:S(2)}, u32[]{:S(2)}) collective-permute-start(f32[2,136,128]{2,1,0:T(8,128)S(1)} %pad_maximum_fusion), channel_id=1, source_target_pairs={{0,1},{1,0},{2,3},{3,2},{4,5},{5,4},{6,7},{7,6},{8,9},{9,8},{10,11... | collective-permute-start | bytes 417800 | tf_op jit(solution)/shard_map/cond/branch_1_fun/ppermute | solution.py:537
  64.7 18.5 %collective-permute-start.12 = (f32[384,128]{1,0:T(8,128)}, f32[384,128]{1,0:T(8,128)S(1)}, u32[]{:S(2)}, u32[]{:S(2)}) collective-permute-start(f32[384,128]{1,0:T(8,128)} %get-tuple-element.85), channel_id=1, source_target_pairs={{0,64},{64,0},{128,192},{192,128},{1,65},{65,1},{129,193},{193,129... | collective-permute-start | bytes 589832 | tf_op jit(solution)/shard_map/ppermute | solution.py:492
  67.0 16.2 %collective-permute-start.13 = (f32[384,128]{1,0:T(8,128)}, f32[384,128]{1,0:T(8,128)S(1)}, u32[]{:S(2)}, u32[]{:S(2)}) collective-permute-start(f32[384,128]{1,0:T(8,128)} %get-tuple-element.86), channel_id=1, source_target_pairs={{0,128},{64,192},{128,0},{192,64},{1,129},{65,193},{129,1},{193,65... | collective-permute-start | bytes 589832 | tf_op jit(solution)/shard_map/ppermute | solution.py:492
  67.4 18.8 %collective-permute-start.14 = (f32[384,128]{1,0:T(8,128)S(1)}, f32[384,128]{1,0:T(8,128)S(1)}, u32[]{:S(2)}, u32[]{:S(2)}) collective-permute-start(f32[384,128]{1,0:T(8,128)S(1)} %get-tuple-element.87), channel_id=1, source_target_pairs={{0,192},{64,128},{128,64},{192,0},{1,193},{65,129},{129,65},{193,1... | collective-permute-start | bytes 589832 | tf_op jit(solution)/shard_map/ppermute | solution.py:492
  68.6 7.1 %collective-permute-start.11 = (f32[32,64]{1,0:T(8,128)S(1)}, f32[32,64]{1,0:T(8,128)S(1)}, u32[]{:S(2)}, u32[]{:S(2)}) collective-permute-start(f32[32,64]{1,0:T(8,128)S(1)} %get-tuple-element.94), channel_id=1, source_target_pairs={{12,0},{14,2},{8,4},{10,6},{20,8},{22,10},{16,12},{18,14},{28,16},... | collective-permute-start | bytes 24584 | tf_op jit(solution)/shard_map/ppermute | solution.py:562
  72.2 7.7 %collective-permute-start.10 = (f32[32,64]{1,0:T(8,128)S(1)}, f32[32,64]{1,0:T(8,128)S(1)}, u32[]{:S(2)}, u32[]{:S(2)}) collective-permute-start(f32[32,64]{1,0:T(8,128)S(1)} %get-tuple-element.95), channel_id=1, source_target_pairs={{0,12},{2,14},{4,8},{6,10},{8,20},{10,22},{12,16},{14,18},{16,28},... | collective-permute-start | bytes 24584 | tf_op jit(solution)/shard_map/ppermute | solution.py:561
  87.3 15.1 %collective-permute-start.16 = (f32[768,128]{1,0:T(8,128)S(1)}, f32[768,128]{1,0:T(8,128)S(1)}, u32[]{:S(2)}, u32[]{:S(2)}) collective-permute-start(f32[768,128]{1,0:T(8,128)S(1)} %get-tuple-element.90), channel_id=1, source_target_pairs={{0,64},{64,0},{128,192},{192,128},{1,65},{65,1},{129,193},{193,129... | collective-permute-start | bytes 1179656 | tf_op jit(solution)/shard_map/ppermute | solution.py:492
  87.4 28.9 %collective-permute-start.17 = (f32[768,128]{1,0:T(8,128)S(1)}, f32[768,128]{1,0:T(8,128)S(1)}, u32[]{:S(2)}, u32[]{:S(2)}) collective-permute-start(f32[768,128]{1,0:T(8,128)S(1)} %get-tuple-element.91), channel_id=1, source_target_pairs={{0,128},{64,192},{128,0},{192,64},{1,129},{65,193},{129,1},{193,65... | collective-permute-start | bytes 1179656 | tf_op jit(solution)/shard_map/ppermute | solution.py:492
  89.9 34.1 %collective-permute-start.15 = (f32[768,128]{1,0:T(8,128)S(1)}, f32[768,128]{1,0:T(8,128)S(1)}, u32[]{:S(2)}, u32[]{:S(2)}) collective-permute-start(f32[768,128]{1,0:T(8,128)S(1)} %get-tuple-element.88), channel_id=1, source_target_pairs={{0,192},{64,128},{128,64},{192,0},{1,193},{65,129},{129,65},{193,1... | collective-permute-start | bytes 1179656 | tf_op jit(solution)/shard_map/ppermute | solution.py:492

commit v4 on v3

--- a/solution.py
+++ b/solution.py
@@ -22,10 +22,11 @@
 OBS = 16
 HALF = PAD * MEM
 MIDDLE = CX * MEM - 2 * HALF
-DU, DV, DL = 6, 5, 5
+DU, DV, DL = 4, 5, 5
 STRIP = DU + DV + DL + 1
 FRICTION = 0.02
 HIGHEST = lax.Precision.HIGHEST
+EARLY, LATE = (0, 1, 3), 2
 F32 = jnp.float32
 BF16 = jnp.bfloat16
 SIDE = ("grp", "sub", "cores")
@@ -51,6 +52,14 @@
 
 def shaped(*shape, dtype=F32):
     return jax.ShapeDtypeStruct(shape, dtype)
+
+
+def up_from(group, steps):
+    return (group + steps) % GRP
+
+
+def down_from(group, steps):
+    return (group + GRP - steps) % GRP
 
 
 def aligned(value, unit):
@@ -77,19 +86,31 @@
             copies[1].wait()
         else:
             copies[2].wait()
+        base, sign = (CX - PAD, 0.5) if end else (0, -0.5)
+
+        def take(first, count):
+            return slice(PAD - first - count, PAD - first) if end else slice(first, first + count)
+
         for part in range(PARTS):
             lanes = slice(part * LANE, (part + 1) * LANE)
+            deep = bed[base : base + PAD, lanes]
             for member in range(MEM):
-                at = 0
-                for field, depth in ((1, DU), (2, DV), (0, DL)):
-                    low = PAD - depth if end else 0
-                    strips[side, part, pl.ds(at * MEM + member, depth, stride=MEM), :] = rows[
-                        member, field, low : low + depth, lanes
-                    ]
-                    at += depth
-            low, to = CX - DU if end else 0, (STRIP - 1) * MEM
+                level, east, north = (rows[member, f, :, lanes] for f in range(3))
+
+                def put(slot, count, value):
+                    to = pl.ds(slot * MEM + member, count, stride=MEM)
+                    strips[side, part, to, :] = value
+
+                flux, plus = north * deep, sign * (east * deep)
+                near, far = take(3, 2), take(4, 2)
+                put(0, DU, east[take(0, DU), :])
+                put(DU + end, DV - 1, north[take(0, DV - 1), :])
+                put(DU + (0 if end else DV - 1), 1, flux[take(DV - 1, 1), :])
+                put(DU + DV + 2 * end, DL - 2, level[take(0, DL - 2), :])
+                put(DU + DV + (0 if end else DL - 2), 2, level[near, :] + plus[far, :])
+            to = (STRIP - 1) * MEM
             strips[side, part, to : to + MEM, :] = jnp.zeros((MEM, LANE), F32)
-            strips[side, part, to : to + DU, :] = bed[low : low + DU, lanes]
+            strips[side, part, to : to + DU, :] = deep[take(0, DU), :]
         copies[4 + side].start()
     for same in range(3):
         edges[MEM, same] = bed[:, edge]
@@ -201,7 +222,7 @@
     for other in range(GRP):
         for field in range(3):
             blocks[other][field * MIDDLE : (field + 1) * MIDDLE, :] = fields[field][
-                jnp.bitwise_xor(where[0], other), HALF : CX * MEM - HALF, :
+                up_from(where[0], other), HALF : CX * MEM - HALF, :
             ]
 
 
@@ -268,6 +289,10 @@
                 fields[3][part, to : to + MEM, :] = jnp.broadcast_to(
                     piece((STRIP - 1) * MEM + row, 1), (MEM, LANE)
                 )
+            for beyond in (DU, DU + 1):
+                to = half + beyond * MEM if side else half - (beyond + 1) * MEM
+                fields[1][part, to : to + MEM, :] = jnp.zeros((MEM, LANE), F32)
+                fields[3][part, to : to + MEM, :] = jnp.full((MEM, LANE), 1.0 * (beyond == DU), F32)
     has_above = inside * where[2].astype(F32)
     has_below = inside * where[3].astype(F32)
     for step in range(STEPS):
@@ -307,7 +332,7 @@
             whole[field, part, half:, :] = bottom[field][part, :half, :]
         for other in range(GRP):
             blocks[other][field * MIDDLE : (field + 1) * MIDDLE, :] = whole[
-                field, jnp.bitwise_xor(group, other)
+                field, up_from(group, other)
             ]
 
 
@@ -328,8 +353,8 @@
 
 def unpack_body(where, *refs):
     blocks, out = refs[:-1], refs[-1]
-    for other, block in enumerate(blocks):
-        at = pl.ds(aligned(jnp.bitwise_xor(where[0], other), LANE), LANE)
+    for other, block in zip(EARLY, blocks):
+        at = pl.ds(aligned(down_from(where[0], other), LANE), LANE)
         for field in range(3):
             for member in range(MEM):
                 out[member, field, :, at] = turned_rows(block, field, member)
@@ -339,7 +364,7 @@
     for field in range(3):
         for member in range(MEM):
             held[member, field] = turned_rows(block, field, member)
-    at = pl.ds(aligned(jnp.bitwise_xor(where[0], GRP - 1), LANE), LANE)
+    at = pl.ds(aligned(down_from(where[0], LATE), LANE), LANE)
     copy = pltpu.make_async_copy(held, out.at[:, :, :, at], sem)
     copy.start()
     copy.wait()
@@ -347,7 +372,7 @@
 
 def unpack(where, blocks):
     out = shaped(MEM, 3, CX, CY)
-    early = call(unpack_body, (out,), (where, *blocks[:-1]))[0]
+    early = call(unpack_body, (out,), (where, *[blocks[s] for s in EARLY]))[0]
     return pl.pallas_call(
         unpack_last_body,
         out_shape=out,
@@ -356,7 +381,7 @@
         scratch_shapes=[pltpu.VMEM((MEM, 3, CX, LANE), F32), pltpu.SemaphoreType.DMA],
         input_output_aliases={2: 0},
         compiler_params=pltpu.CompilerParams(vmem_limit_bytes=16 * 1024 * 1024),
-    )(where, blocks[-1], early)
+    )(where, blocks[LATE], early)
 
 
 def spread_out_body(where, inner, outer, out):
@@ -379,7 +404,7 @@
     return call(spread_out_body, (shaped(MEM, 3, CX, CY),), (where, inner, outer))[0]
 
 
-def products_body(where, states, out, wanted_at):
+def products_body(where, states, out, seen_at, wanted_at):
     group = where[0]
     lane = lax.broadcasted_iota(jnp.int32, (1, LANE), 1)
 
@@ -398,22 +423,17 @@
                 turned = pltpu.roll(held, (source - part) * OBS % LANE, 1)
                 noisy[part] = jnp.where(here, turned, noisy[part])
             other = jnp.where(here, pltpu.roll(states[at + 2], source * OBS, 1), other)
-        for part in range(GRP):
-            wanted_at[block, part] = noisy[part]
-        seen = jnp.concatenate(
-            [
-                unfolded(3 * (jnp.bitwise_xor(group, s) * (SUB * 2) + block))
-                for s in range(GRP)
-            ],
-            axis=0,
-        )
-        wanted = jnp.concatenate(
-            [wanted_at[block, jnp.bitwise_xor(group, s)] for s in range(GRP)], axis=0
-        )
+        seen = [unfolded(3 * (source * (SUB * 2) + block)) for source in range(GRP)]
+        for source in range(GRP):
+            wanted_at[block, source] = noisy[source] - seen[source]
+            seen_at[block, source] = seen[source]
+        seen = [seen_at[block, down_from(group, s)] for s in range(GRP)]
+        wanted = [wanted_at[block, up_from(group, s)] for s in range(GRP)]
+        seen, wanted = jnp.concatenate(seen, axis=0), jnp.concatenate(wanted, axis=0)
         anomaly = seen - jnp.mean(seen, axis=0, keepdims=True)
         scaled = anomaly / jnp.where(lane < GRP * OBS, other[3:4, :], 1.0)
         left.append(jnp.concatenate([scaled * other[r : r + 1, :] for r in range(3)], axis=0))
-        right.append(jnp.concatenate([anomaly, wanted - seen], axis=0))
+        right.append(jnp.concatenate([anomaly, wanted], axis=0))
     out[...] = lax.dot_general(
         jnp.concatenate(left, axis=1),
         jnp.concatenate(right, axis=1),
@@ -428,7 +448,7 @@
         products_body,
         (shaped(3 * E, 2 * E),),
         (where, states),
-        [pltpu.VMEM((SUB * 2, GRP, MEM, LANE), F32)],
+        [pltpu.VMEM((SUB * 2, GRP, MEM, LANE), F32)] * 2,
     )[0]
 
 
@@ -488,9 +508,10 @@
 
 
 def exchange(blocks):
-    return [blocks[0]] + [
-        lax.ppermute(blocks[s], "grp", [(i, i ^ s) for i in range(GRP)]) for s in range(1, GRP)
-    ]
+    moved = {
+        s: lax.ppermute(blocks[s], "grp", [(i, (i + s) % GRP) for i in range(GRP)]) for s in range(1, GRP)
+    }
+    return [blocks[0]] + [moved[s] for s in range(1, GRP)]
 
 
 def on_device(

time: 126 us -> 122 us (0.968)
  the two profiles are of different devices: /device:TPU:38 before, /device:TPU:31 now
where the time goes in v4:
time: 122 us; the launch traced here: 121 us
  waiting for transfers between devices  40 us (33%)
  starting transfers between devices  35.9 us (29%)
  Pallas kernels  28 us (23%)
  blocking collectives  15.7 us (13%)
    ppermute x12, waiting for transfers between devices, exchange(): lax.ppermute(blocks[s], 'grp', [(i, (i + s) % GRP) for i in range(GRP)])  33.5 us
    pallas_call x7, Pallas kernels, call(): pl.pallas_call(body, out_shape=list(outs), in_specs=[SMEM] + [VMEM] * (le...  23.9 us
    ppermute x12, starting transfers between devices, exchange(): lax.ppermute(blocks[s], 'grp', [(i, (i + s) % GRP) for i in range(GRP)])  17.6 us
    all_to_all x1, blocking collectives, outer_rows(): return (outer, rest, lax.all_to_all(state, SIDE, 0, 0, tiled=True))  15.7 us
    ppermute x1, starting transfers between devices, on_device(): above = lax.ppermute(down, TILE, forward)  8.82 us
    ppermute x1, waiting for transfers between devices, on_device(): from_above = lax.ppermute(products[2 * E:], TILE, pairs)  4.38 us
    pallas_call x1, Pallas kernels, pack(): pl.pallas_call(pack_body, out_shape=[strip, strip, shaped(MEM + 1, 3, CX,...  2.68 us
    ppermute x1, starting transfers between devices, on_device(): from_below = lax.ppermute(products[:E], TILE, [(b, a) for a, b in pairs])  2.62 us
  transfers between devices with their start and end apart: 18, of which 8 were waited for; matrix products, arithmetic and copies ran while one was open for 0% of the time, Pallas kernels for 19%

profile of v4, /device:TPU:31, one launch (start us, length us, event | category | flops | bytes accessed | tf_op | source)
XLA Modules:
  0.0 121.2 jit_solution(17897123060439731745)
XLA Ops:
  0.6 0.0 copy-start.1
  0.6 0.0 copy-start
  0.7 0.1 pad_add_fusion.where
  0.8 2.7 %shard_map.95 = (f32[4,120,128]{2,1,0:T(8,128)}, f32[4,120,128]{2,1,0:T(8,128)}, f32[9,3,32,128]{3,2,1,0:T(8,128)}) custom-call(s32[4]{0:T(128)S(1)} %pad_add_fusion.where, f32[8,3,32,512]{3,2,1,0:T(8,128)} %trial.3, f32[32,512]{1,0:T(8,128)} %seabed.3), custom_call_target="tpu_custom_call" | custom-call | tf_op jit(solution)/shard_map/pallas_call | solution.py:127
  3.5 8.8 %collective-permute-start.2 = (f32[4,120,128]{2,1,0:T(8,128)}, f32[4,120,128]{2,1,0:T(8,128)S(1)}, u32[]{:S(2)}, u32[]{:S(2)}) collective-permute-start(f32[4,120,128]{2,1,0:T(8,128)} %get-tuple-element.68), channel_id=1, source_target_pairs={{0,2},{2,4},{4,6},{6,8},{8,10},{10,12},{12,14},{14,16},{16,18},{18... | collective-permute-start | bytes 737288 | tf_op jit(solution)/shard_map/ppermute | solution.py:530
  12.3 2.1 %collective-permute-start.3 = (f32[4,120,128]{2,1,0:T(8,128)}, f32[4,120,128]{2,1,0:T(8,128)S(1)}, u32[]{:S(2)}, u32[]{:S(2)}) collective-permute-start(f32[4,120,128]{2,1,0:T(8,128)} %get-tuple-element.69), channel_id=1, source_target_pairs={{2,0},{4,2},{6,4},{8,6},{10,8},{12,10},{14,12},{16,14},{18,16},{20... | collective-permute-start | bytes 737288 | tf_op jit(solution)/shard_map/ppermute | solution.py:531
  14.4 1.0 collective-permute-start.1
  15.5 0.1 mul.34
  15.6 0.1 mul.35
  15.7 0.1 mul.33
  15.8 0.1 add_bitcast_fusion
  15.9 1.2 collective-permute-done.1.beside
  17.1 3.8 %collective-permute-start.6 = (f32[8,128]{1,0:T(8,128)S(1)}, f32[8,128]{1,0:T(8,128)S(1)}, u32[]{:S(2)}, u32[]{:S(2)}) collective-permute-start(f32[8,128]{1,0:T(8,128)S(1)} %pad.12), channel_id=1, source_target_pairs={{0,192},{64,0},{128,64},{192,128},{1,193},{65,1},{129,65},{193,129... | collective-permute-start | bytes 12296 | tf_op jit(solution)/shard_map/ppermute | solution.py:512
  20.9 0.3 collective-permute-start.4
  21.2 0.1 copy.15
  21.3 0.1 stack_reshape.3
  21.4 9.7 %shard_map.96 = (f32[384,128]{1,0:T(8,128)S(1)}, f32[384,128]{1,0:T(8,128)S(1)}, f32[384,128]{1,0:T(8,128)S(1)}, f32[384,128]{1,0:T(8,128)S(1)}, f32[4,5,256,128]{3,2,1,0:T(8,128)}) custom-call(s32[4]{0:T(128)S(1)} %pad_add_fusion.where, f32[8,3,32,512]{3,2,1,0:T(8,128)S(1)} %copy-done, f32[32,512]{1,0:T(8,128)S(1)} %copy-done.1, ...), custom_call_target="tpu_custom_call" | custom-call | flops 10000000 | bytes 32000000 | tf_op jit(solution)/shard_map/pallas_call | solution.py:42
  31.1 3.4 %collective-permute-done.6 = f32[8,128]{1,0:T(8,128)S(1)} collective-permute-done((f32[8,128]{1,0:T(8,128)S(1)}, f32[8,128]{1,0:T(8,128)S(1)}, u32[]{:S(2)}, u32[]{:S(2)}) %collective-permute-start.6) | collective-permute-done | bytes 4128 | tf_op jit(solution)/shard_map/ppermute | solution.py:512
  34.5 1.9 %collective-permute-start.8 = (f32[384,128]{1,0:T(8,128)S(1)}, f32[384,128]{1,0:T(8,128)S(1)}, u32[]{:S(2)}, u32[]{:S(2)}) collective-permute-start(f32[384,128]{1,0:T(8,128)S(1)} %get-tuple-element.80), channel_id=1, source_target_pairs={{0,128},{64,192},{128,0},{192,64},{1,129},{65,193},{129,1},{193,65... | collective-permute-start | bytes 589832 | tf_op jit(solution)/shard_map/ppermute | solution.py:512
  36.4 1.3 %collective-permute-start.9 = (f32[384,128]{1,0:T(8,128)S(1)}, f32[384,128]{1,0:T(8,128)S(1)}, u32[]{:S(2)}, u32[]{:S(2)}) collective-permute-start(f32[384,128]{1,0:T(8,128)S(1)} %get-tuple-element.81), channel_id=1, source_target_pairs={{0,192},{64,0},{128,64},{192,128},{1,193},{65,1},{129,65},{193,129... | collective-permute-start | bytes 589832 | tf_op jit(solution)/shard_map/ppermute | solution.py:512
  37.8 0.0 collective-permute-done.3
  37.8 22.6 %conditional.1 = (f32[384,128]{1,0:T(8,128)S(1)}, f32[384,128]{1,0:T(8,128)}, f32[384,128]{1,0:T(8,128)S(1)}, f32[384,128]{1,0:T(8,128)S(1)}, f32[3,4,128,128]{3,2,1,0:T(8,128)S(1)}, /*index=5*/f32[96,4,128]{2,1,0:T(4,128)S(1)}) conditional(s32[]{:T(128)} %convert_element_type.41, () %tuple.21, (s32[]{:T(128)}, f32[4,120,128]{2,1,0:T(8,128)S(1)}, ...), branch_computations={%region_0.1_spmd, %region_1.2_spmd} | conditional | flops 30722 | bytes 1769544 | solution.py:571
  37.9 2.4 %collective-permute-start = (f32[2,120,128]{2,1,0:T(8,128)S(1)}, f32[2,120,128]{2,1,0:T(8,128)S(1)}, u32[]{:S(2)}, u32[]{:S(2)}) collective-permute-start(f32[2,120,128]{2,1,0:T(8,128)S(1)} %pad_maximum_fusion), channel_id=1, source_target_pairs={{0,1},{1,0},{2,3},{3,2},{4,5},{5,4},{6,7},{7,6},{8,9},{9,8},{10,11... | collective-permute-start | bytes 368648 | tf_op jit(solution)/shard_map/cond/branch_1_fun/ppermute | solution.py:558
  40.2 1.0 collective-permute-done.corner
  41.2 3.5 %branch_1_fun.1 = (f32[384,128]{1,0:T(8,128)S(1)}, f32[384,128]{1,0:T(8,128)}, f32[384,128]{1,0:T(8,128)S(1)}, f32[384,128]{1,0:T(8,128)S(1)}, f32[96,4,128]{2,1...) custom-call(s32[4]{0:T(128)S(1)} %get-tuple-element.20.where, f32[4,5,256,128]{3,2,1,0:T(8,128)} %get-tuple-element.21.inner, ...), custom_call_target="tpu_custom_call" | custom-call | tf_op jit(solution)/shard_map/cond/branch_1_fun/pallas_call | solution.py:42
  44.7 15.7 %all_to_all.4 = f32[96,4,128]{2,1,0:T(4,128)S(1)} all-to-all(f32[96,4,128]{2,1,0:T(4,128)S(1)} %get-tuple-element.35), channel_id=1, replica_groups=mesh['grp'=4,'reg'=8,'sub'=4,'cores'=2] {'grp','sub','cores'}, dimensions={0} | all-to-all | bytes 393216 | tf_op jit(solution)/shard_map/cond/branch_1_fun/all_to_all | solution.py:562
  60.4 1.2 %shard_map.98.own = f32[96,64]{1,0:T(8,128)S(1)} custom-call(s32[4]{0:T(128)S(1)} %pad_add_fusion.where, f32[96,4,128]{2,1,0:T(4,128)S(1)} %get-tuple-element.74.states), custom_call_target="tpu_custom_call" | custom-call | tf_op jit(solution)/shard_map/pallas_call | solution.py:42
  61.7 0.5 collective-permute-start.12
  62.2 2.2 %collective-permute-start.13 = (f32[384,128]{1,0:T(8,128)S(1)}, f32[384,128]{1,0:T(8,128)S(1)}, u32[]{:S(2)}, u32[]{:S(2)}) collective-permute-start(f32[384,128]{1,0:T(8,128)S(1)} %get-tuple-element.86), channel_id=1, source_target_pairs={{0,128},{64,192},{128,0},{192,64},{1,129},{65,193},{129,1},{193,65... | collective-permute-start | bytes 589832 | tf_op jit(solution)/shard_map/ppermute | solution.py:512
  64.4 1.1 collective-permute-start.14
  65.5 0.0 collective-permute-done.8.refs_3_
  65.5 0.0 collective-permute-done.9.refs_4_
  65.5 2.6 %collective-permute-start.11 = (f32[32,64]{1,0:T(8,128)S(1)}, f32[32,64]{1,0:T(8,128)S(1)}, u32[]{:S(2)}, u32[]{:S(2)}) collective-permute-start(f32[32,64]{1,0:T(8,128)S(1)} %get-tuple-element.94), channel_id=1, source_target_pairs={{12,0},{14,2},{8,4},{10,6},{20,8},{22,10},{16,12},{18,14},{28,16},... | collective-permute-start | bytes 24584 | tf_op jit(solution)/shard_map/ppermute | solution.py:583
  68.1 1.3 %collective-permute-start.10 = (f32[32,64]{1,0:T(8,128)S(1)}, f32[32,64]{1,0:T(8,128)S(1)}, u32[]{:S(2)}, u32[]{:S(2)}) collective-permute-start(f32[32,64]{1,0:T(8,128)S(1)} %get-tuple-element.95), channel_id=1, source_target_pairs={{0,12},{2,14},{4,8},{6,10},{8,20},{10,22},{12,16},{14,18},{16,28},... | collective-permute-start | bytes 24584 | tf_op jit(solution)/shard_map/ppermute | solution.py:582
  69.4 0.0 collective-permute-done.11.high
  69.4 4.4 %collective-permute-done.10.low = f32[32,64]{1,0:T(8,128)S(1)} collective-permute-done((f32[32,64]{1,0:T(8,128)S(1)}, f32[32,64]{1,0:T(8,128)S(1)}, u32[]{:S(2)}, u32[]{:S(2)}) %collective-permute-start.10) | collective-permute-done | bytes 8224 | tf_op jit(solution)/shard_map/ppermute | solution.py:582
  73.8 3.2 %shard_map.99.refs_0_ = f32[32,32]{1,0:T(8,128)S(1)} custom-call(s32[4]{0:T(128)S(1)} %pad_add_fusion.where, f32[96,64]{1,0:T(8,128)S(1)} %shard_map.98.own, f32[32,64]{1,0:T(8,128)S(1)} %collective-permute-done.10.low, f32[32,64]{1,0:T(8,128)S(1)} %collective-permute-done.11.high), custom_call_target="tpu_custom_call" | custom-call | tf_op jit(solution)/shard_map/pallas_call | solution.py:42
  77.1 0.6 collective-permute-done.13.refs_7_
  77.7 1.1 shard_map.100
  78.8 4.6 %collective-permute-start.16 = (f32[768,128]{1,0:T(8,128)S(1)}, f32[768,128]{1,0:T(8,128)S(1)}, u32[]{:S(2)}, u32[]{:S(2)}) collective-permute-start(f32[768,128]{1,0:T(8,128)S(1)} %get-tuple-element.90), channel_id=1, source_target_pairs={{0,64},{64,128},{128,192},{192,0},{1,65},{65,129},{129,193},{193,1... | collective-permute-start | bytes 1179656 | tf_op jit(solution)/shard_map/ppermute | solution.py:512
  83.4 1.7 %collective-permute-start.17 = (f32[768,128]{1,0:T(8,128)S(1)}, f32[768,128]{1,0:T(8,128)S(1)}, u32[]{:S(2)}, u32[]{:S(2)}) collective-permute-start(f32[768,128]{1,0:T(8,128)S(1)} %get-tuple-element.91), channel_id=1, source_target_pairs={{0,192},{64,0},{128,64},{192,128},{1,193},{65,1},{129,65},{193,129... | collective-permute-start | bytes 1179656 | tf_op jit(solution)/shard_map/ppermute | solution.py:512
  85.1 0.2 collective-permute-start.15
  85.3 3.2 %shard_map.97 = f32[8,3,32,512]{3,2,1,0:T(8,128)} custom-call(s32[4]{0:T(128)S(1)} %pad_add_fusion.where, f32[4,5,256,128]{3,2,1,0:T(8,128)} %get-tuple-element.67.inner, f32[3,4,128,128]{3,2,1,0:T(8,128)S(1)} %get-tuple-element.73.outer), custom_call_target="tpu_custom_call" | custom-call | tf_op jit(solution)/shard_map/pallas_call | solution.py:42
  88.5 5.7 %collective-permute-done.16.refs_1_ = f32[768,128]{1,0:T(8,128)S(1)} collective-permute-done((f32[768,128]{1,0:T(8,128)S(1)}, f32[768,128]{1,0:T(8,128)S(1)}, u32[]{:S(2)}, u32[]{:S(2)}) %collective-permute-start.16) | collective-permute-done | bytes 393248 | tf_op jit(solution)/shard_map/ppermute | solution.py:512
  94.2 8.4 %collective-permute-done.17.refs_2_ = f32[768,128]{1,0:T(8,128)S(1)} collective-permute-done((f32[768,128]{1,0:T(8,128)S(1)}, f32[768,128]{1,0:T(8,128)S(1)}, u32[]{:S(2)}, u32[]{:S(2)}) %collective-permute-start.17) | collective-permute-done | bytes 393248 | tf_op jit(solution)/shard_map/ppermute | solution.py:512
  102.6 1.9 %shard_map.101._ = f32[8,3,32,512]{3,2,1,0:T(8,128)} custom-call(s32[4]{0:T(128)S(1)} %pad_add_fusion.where, f32[768,128]{1,0:T(8,128)S(1)} %get-tuple-element.89.refs_0_, f32[768,128]{1,0:T(8,128)S(1)} %collective-permute-done.16.refs_1_, f32[768,128]{1,0:T(8,128)S(1)} %collective-permute-done.17.refs_2_), custom_call_target="tpu_custom_call" | custom-call | tf_op jit(solution)/shard_map/pallas_call | solution.py:42
  104.5 15.4 %collective-permute-done.15.block = f32[768,128]{1,0:T(8,128)S(1)} collective-permute-done((f32[768,128]{1,0:T(8,128)S(1)}, f32[768,128]{1,0:T(8,128)S(1)}, u32[]{:S(2)}, u32[]{:S(2)}) %collective-permute-start.15) | collective-permute-done | bytes 393248 | tf_op jit(solution)/shard_map/ppermute | solution.py:512
  119.9 1.4 %shard_map.102 = f32[8,3,32,512]{3,2,1,0:T(8,128)} custom-call(s32[4]{0:T(128)S(1)} %pad_add_fusion.where, f32[768,128]{1,0:T(8,128)S(1)} %collective-permute-done.15.block, f32[8,3,32,512]{3,2,1,0:T(8,128)} %shard_map.101._), custom_call_target="tpu_custom_call", output_to_operand_aliasing={{}: (2, {})} | custom-call | tf_op jit(solution)/shard_map/pallas_call | solution.py:376
  (39 shorter events, 0.2 us)
Async XLA Ops:
  0.6 20.7 %copy-start.1 = (f32[32,512]{1,0:T(8,128)S(1)}, f32[32,512]{1,0:T(8,128)}, u32[]{:S(2)}) copy-start(f32[32,512]{1,0:T(8,128)} %seabed.3) | copy-start | bytes 196612
  0.6 20.7 %copy-start = (f32[8,3,32,512]{3,2,1,0:T(8,128)S(1)}, f32[8,3,32,512]{3,2,1,0:T(8,128)}, u32[]{:S(2)}) copy-start(f32[8,3,32,512]{3,2,1,0:T(8,128)} %trial.3) | copy-start | bytes 4718596
  0.7 14.8 %copy-start.7 = (s32[16,4]{0,1:T(4,128)S(1)}, s32[16,4]{0,1:T(4,128)}, u32[]{:S(2)}) copy-start(s32[16,4]{0,1:T(4,128)} %param.15) | copy-start | bytes 772
  0.7 14.8 %copy-start.6 = (f32[16]{0:T(128)S(1)}, f32[16]{0:T(128)}, u32[]{:S(2)}) copy-start(f32[16]{0:T(128)} %param.13) | copy-start | bytes 196
  0.7 15.0 %copy-start.3 = (s32[16,8]{0,1:T(8,128)S(1)}, s32[16,8]{0,1:T(8,128)}, u32[]{:S(2)}) copy-start(s32[16,8]{0,1:T(8,128)} %param.17) | copy-start | bytes 1540
  0.7 15.0 %copy-start.4 = (f32[16,4]{0,1:T(4,128)S(1)}, f32[16,4]{0,1:T(4,128)}, u32[]{:S(2)}) copy-start(f32[16,4]{0,1:T(4,128)} %param.16) | copy-start | bytes 772
  0.7 15.1 %copy-start.2 = (f32[16,32]{1,0:T(8,128)S(1)}, f32[16,32]{1,0:T(8,128)}, u32[]{:S(2)}) copy-start(f32[16,32]{1,0:T(8,128)} %param.14) | copy-start | bytes 6148
  0.7 15.1 %copy-start.5 = (f32[16]{0:T(128)S(1)}, f32[16]{0:T(128)}, u32[]{:S(2)}) copy-start(f32[16]{0:T(128)} %param.12) | copy-start | bytes 196
  3.5 34.3 %collective-permute-start.2 = (f32[4,120,128]{2,1,0:T(8,128)}, f32[4,120,128]{2,1,0:T(8,128)S(1)}, u32[]{:S(2)}, u32[]{:S(2)}) collective-permute-start(f32[4,120,128]{2,1,0:T(8,128)} %get-tuple-element.68), channel_id=1, source_target_pairs={{0,2},{2,4},{4,6},{6,8},{8,10},{10,12},{12,14},{14,16},{16,18},{18... | collective-permute-start | bytes 737288 | tf_op jit(solution)/shard_map/ppermute | solution.py:530
  12.3 25.5 %collective-permute-start.3 = (f32[4,120,128]{2,1,0:T(8,128)}, f32[4,120,128]{2,1,0:T(8,128)S(1)}, u32[]{:S(2)}, u32[]{:S(2)}) collective-permute-start(f32[4,120,128]{2,1,0:T(8,128)} %get-tuple-element.69), channel_id=1, source_target_pairs={{2,0},{4,2},{6,4},{8,6},{10,8},{12,10},{14,12},{16,14},{18,16},{20... | collective-permute-start | bytes 737288 | tf_op jit(solution)/shard_map/ppermute | solution.py:531
  14.4 2.7 %collective-permute-start.1 = (f32[9,3,32,128]{3,2,1,0:T(8,128)}, f32[9,3,32,128]{3,2,1,0:T(8,128)S(1)}, u32[]{:S(2)}, u32[]{:S(2)}) collective-permute-start(f32[9,3,32,128]{3,2,1,0:T(8,128)} %get-tuple-element.65), channel_id=1, source_target_pairs={{0,1},{1,0},{2,3},{3,2},{4,5},{5,4},{6,7},{7,6},{8,9},{9,8},{10,11... | collective-permute-start | bytes 1327112 | tf_op jit(solution)/shard_map/ppermute | solution.py:532
  17.1 17.4 %collective-permute-start.6 = (f32[8,128]{1,0:T(8,128)S(1)}, f32[8,128]{1,0:T(8,128)S(1)}, u32[]{:S(2)}, u32[]{:S(2)}) collective-permute-start(f32[8,128]{1,0:T(8,128)S(1)} %pad.12), channel_id=1, source_target_pairs={{0,192},{64,0},{128,64},{192,128},{1,193},{65,1},{129,65},{193,129... | collective-permute-start | bytes 12296 | tf_op jit(solution)/shard_map/ppermute | solution.py:512
  20.9 13.6 %collective-permute-start.5 = (f32[8,128]{1,0:T(8,128)S(1)}, f32[8,128]{1,0:T(8,128)S(1)}, u32[]{:S(2)}, u32[]{:S(2)}) collective-permute-start(f32[8,128]{1,0:T(8,128)S(1)} %pad.12), channel_id=1, source_target_pairs={{0,128},{64,192},{128,0},{192,64},{1,129},{65,193},{129,1},{193,65... | collective-permute-start | bytes 12296 | tf_op jit(solution)/shard_map/ppermute | solution.py:512
  20.9 13.6 %collective-permute-start.4 = (f32[8,128]{1,0:T(8,128)S(1)}, f32[8,128]{1,0:T(8,128)S(1)}, u32[]{:S(2)}, u32[]{:S(2)}) collective-permute-start(f32[8,128]{1,0:T(8,128)S(1)} %pad.12), channel_id=1, source_target_pairs={{0,64},{64,128},{128,192},{192,0},{1,65},{65,129},{129,193},{193,1... | collective-permute-start | bytes 12296 | tf_op jit(solution)/shard_map/ppermute | solution.py:512
  34.5 29.9 %collective-permute-start.7 = (f32[384,128]{1,0:T(8,128)S(1)}, f32[384,128]{1,0:T(8,128)S(1)}, u32[]{:S(2)}, u32[]{:S(2)}) collective-permute-start(f32[384,128]{1,0:T(8,128)S(1)} %get-tuple-element.79), channel_id=1, source_target_pairs={{0,64},{64,128},{128,192},{192,0},{1,65},{65,129},{129,193},{193,1... | collective-permute-start | bytes 589832 | tf_op jit(solution)/shard_map/ppermute | solution.py:512
  34.5 31.0 %collective-permute-start.8 = (f32[384,128]{1,0:T(8,128)S(1)}, f32[384,128]{1,0:T(8,128)S(1)}, u32[]{:S(2)}, u32[]{:S(2)}) collective-permute-start(f32[384,128]{1,0:T(8,128)S(1)} %get-tuple-element.80), channel_id=1, source_target_pairs={{0,128},{64,192},{128,0},{192,64},{1,129},{65,193},{129,1},{193,65... | collective-permute-start | bytes 589832 | tf_op jit(solution)/shard_map/ppermute | solution.py:512
  36.4 29.1 %collective-permute-start.9 = (f32[384,128]{1,0:T(8,128)S(1)}, f32[384,128]{1,0:T(8,128)S(1)}, u32[]{:S(2)}, u32[]{:S(2)}) collective-permute-start(f32[384,128]{1,0:T(8,128)S(1)} %get-tuple-element.81), channel_id=1, source_target_pairs={{0,192},{64,0},{128,64},{192,128},{1,193},{65,1},{129,65},{193,129... | collective-permute-start | bytes 589832 | tf_op jit(solution)/shard_map/ppermute | solution.py:512
  37.9 3.3 %collective-permute-start = (f32[2,120,128]{2,1,0:T(8,128)S(1)}, f32[2,120,128]{2,1,0:T(8,128)S(1)}, u32[]{:S(2)}, u32[]{:S(2)}) collective-permute-start(f32[2,120,128]{2,1,0:T(8,128)S(1)} %pad_maximum_fusion), channel_id=1, source_target_pairs={{0,1},{1,0},{2,3},{3,2},{4,5},{5,4},{6,7},{7,6},{8,9},{9,8},{10,11... | collective-permute-start | bytes 368648 | tf_op jit(solution)/shard_map/cond/branch_1_fun/ppermute | solution.py:558
  61.7 15.4 %collective-permute-start.12 = (f32[384,128]{1,0:T(8,128)}, f32[384,128]{1,0:T(8,128)S(1)}, u32[]{:S(2)}, u32[]{:S(2)}) collective-permute-start(f32[384,128]{1,0:T(8,128)} %get-tuple-element.85), channel_id=1, source_target_pairs={{0,64},{64,128},{128,192},{192,0},{1,65},{65,129},{129,193},{193,1... | collective-permute-start | bytes 589832 | tf_op jit(solution)/shard_map/ppermute | solution.py:512
  62.2 15.4 %collective-permute-start.13 = (f32[384,128]{1,0:T(8,128)S(1)}, f32[384,128]{1,0:T(8,128)S(1)}, u32[]{:S(2)}, u32[]{:S(2)}) collective-permute-start(f32[384,128]{1,0:T(8,128)S(1)} %get-tuple-element.86), channel_id=1, source_target_pairs={{0,128},{64,192},{128,0},{192,64},{1,129},{65,193},{129,1},{193,65... | collective-permute-start | bytes 589832 | tf_op jit(solution)/shard_map/ppermute | solution.py:512
  64.4 13.3 %collective-permute-start.14 = (f32[384,128]{1,0:T(8,128)S(1)}, f32[384,128]{1,0:T(8,128)S(1)}, u32[]{:S(2)}, u32[]{:S(2)}) collective-permute-start(f32[384,128]{1,0:T(8,128)S(1)} %get-tuple-element.87), channel_id=1, source_target_pairs={{0,192},{64,0},{128,64},{192,128},{1,193},{65,1},{129,65},{193,129... | collective-permute-start | bytes 589832 | tf_op jit(solution)/shard_map/ppermute | solution.py:512
  65.5 3.9 %collective-permute-start.11 = (f32[32,64]{1,0:T(8,128)S(1)}, f32[32,64]{1,0:T(8,128)S(1)}, u32[]{:S(2)}, u32[]{:S(2)}) collective-permute-start(f32[32,64]{1,0:T(8,128)S(1)} %get-tuple-element.94), channel_id=1, source_target_pairs={{12,0},{14,2},{8,4},{10,6},{20,8},{22,10},{16,12},{18,14},{28,16},... | collective-permute-start | bytes 24584 | tf_op jit(solution)/shard_map/ppermute | solution.py:583
  68.1 5.7 %collective-permute-start.10 = (f32[32,64]{1,0:T(8,128)S(1)}, f32[32,64]{1,0:T(8,128)S(1)}, u32[]{:S(2)}, u32[]{:S(2)}) collective-permute-start(f32[32,64]{1,0:T(8,128)S(1)} %get-tuple-element.95), channel_id=1, source_target_pairs={{0,12},{2,14},{4,8},{6,10},{8,20},{10,22},{12,16},{14,18},{16,28},... | collective-permute-start | bytes 24584 | tf_op jit(solution)/shard_map/ppermute | solution.py:582
  78.8 15.4 %collective-permute-start.16 = (f32[768,128]{1,0:T(8,128)S(1)}, f32[768,128]{1,0:T(8,128)S(1)}, u32[]{:S(2)}, u32[]{:S(2)}) collective-permute-start(f32[768,128]{1,0:T(8,128)S(1)} %get-tuple-element.90), channel_id=1, source_target_pairs={{0,64},{64,128},{128,192},{192,0},{1,65},{65,129},{129,193},{193,1... | collective-permute-start | bytes 1179656 | tf_op jit(solution)/shard_map/ppermute | solution.py:512
  83.4 19.2 %collective-permute-start.17 = (f32[768,128]{1,0:T(8,128)S(1)}, f32[768,128]{1,0:T(8,128)S(1)}, u32[]{:S(2)}, u32[]{:S(2)}) collective-permute-start(f32[768,128]{1,0:T(8,128)S(1)} %get-tuple-element.91), channel_id=1, source_target_pairs={{0,192},{64,0},{128,64},{192,128},{1,193},{65,1},{129,65},{193,129... | collective-permute-start | bytes 1179656 | tf_op jit(solution)/shard_map/ppermute | solution.py:512
  85.1 34.8 %collective-permute-start.15 = (f32[768,128]{1,0:T(8,128)S(1)}, f32[768,128]{1,0:T(8,128)S(1)}, u32[]{:S(2)}, u32[]{:S(2)}) collective-permute-start(f32[768,128]{1,0:T(8,128)S(1)} %get-tuple-element.88), channel_id=1, source_target_pairs={{0,128},{64,192},{128,0},{192,64},{1,129},{65,193},{129,1},{193,65... | collective-permute-start | bytes 1179656 | tf_op jit(solution)/shard_map/ppermute | solution.py:512

commit v5 on v4

--- a/solution.py
+++ b/solution.py
@@ -26,7 +26,6 @@
 STRIP = DU + DV + DL + 1
 FRICTION = 0.02
 HIGHEST = lax.Precision.HIGHEST
-EARLY, LATE = (0, 1, 3), 2
 F32 = jnp.float32
 BF16 = jnp.bfloat16
 SIDE = ("grp", "sub", "cores")
@@ -347,41 +346,50 @@
     )
 
 
-def turned_rows(block, field, member):
-    return block[pl.ds(field * CX * MEM + member, CX, stride=MEM), :]
-
-
-def unpack_body(where, *refs):
-    blocks, out = refs[:-1], refs[-1]
-    for other, block in zip(EARLY, blocks):
+def unpack_middle_body(where, *refs):
+    blocks, out = refs[:GRP], refs[GRP]
+    for other, block in enumerate(blocks):
         at = pl.ds(aligned(down_from(where[0], other), LANE), LANE)
         for field in range(3):
             for member in range(MEM):
-                out[member, field, :, at] = turned_rows(block, field, member)
-
-
-def unpack_last_body(where, block, _, out, held, sem):
-    for field in range(3):
-        for member in range(MEM):
-            held[member, field] = turned_rows(block, field, member)
-    at = pl.ds(aligned(down_from(where[0], LATE), LANE), LANE)
-    copy = pltpu.make_async_copy(held, out.at[:, :, :, at], sem)
-    copy.start()
-    copy.wait()
-
-
-def unpack(where, blocks):
+                out[member, field, PAD : CX - PAD, at] = block[
+                    pl.ds(field * MIDDLE + member, CX - 2 * PAD, stride=MEM), :
+                ]
+
+
+def unpack_outer_body(where, *refs):
+    blocks, (_, out, held, sems) = refs[:GRP], refs[GRP:]
+    copies = [
+        pltpu.make_async_copy(held.at[side], out.at[:, :, rows, :], sems.at[side])
+        for side, rows in enumerate((pl.ds(0, PAD), pl.ds(CX - PAD, PAD)))
+    ]
+    for side in range(2):
+        for other, block in enumerate(blocks):
+            at = pl.ds(aligned(down_from(where[0], other), LANE), LANE)
+            for field in range(3):
+                for member in range(MEM):
+                    low = field * MIDDLE + side * HALF + member
+                    held[side, member, field, :, at] = block[pl.ds(low, PAD, stride=MEM), :]
+        copies[side].start()
+    for copy in copies:
+        copy.wait()
+
+
+def unpack(where, middle, outer):
     out = shaped(MEM, 3, CX, CY)
-    early = call(unpack_body, (out,), (where, *[blocks[s] for s in EARLY]))[0]
+    early = call(unpack_middle_body, (out,), (where, *middle), flops=10_000_000, moved=32_000_000)
     return pl.pallas_call(
-        unpack_last_body,
+        unpack_outer_body,
         out_shape=out,
-        in_specs=[SMEM, VMEM, ANY],
+        in_specs=[SMEM] + [VMEM] * GRP + [ANY],
         out_specs=ANY,
-        scratch_shapes=[pltpu.VMEM((MEM, 3, CX, LANE), F32), pltpu.SemaphoreType.DMA],
-        input_output_aliases={2: 0},
+        scratch_shapes=[
+            pltpu.VMEM((2, MEM, 3, PAD, CY), F32),
+            pltpu.SemaphoreType.DMA((2,)),
+        ],
+        input_output_aliases={1 + GRP: 0},
         compiler_params=pltpu.CompilerParams(vmem_limit_bytes=16 * 1024 * 1024),
-    )(where, blocks[LATE], early)
+    )(where, *outer, early[0])
 
 
 def spread_out_body(where, inner, outer, out):
@@ -467,14 +475,13 @@
     return call(solve_body, (shaped(E, E),), (where, own, low, high))[0]
 
 
-def increments_body(where, *refs):
-    weights, middle, edge, outs = refs[0], refs[1 : 1 + GRP], refs[1 + GRP : 1 + 2 * GRP], refs[1 + 2 * GRP :]
+def increments_body(where, weights, *refs):
+    blocks, outs = refs[:GRP], refs[GRP:]
     turned = weights[...].T
     coarse = turned.astype(BF16)
     fine = (turned - coarse.astype(F32)).astype(BF16)
     left = jnp.concatenate([coarse, coarse, fine], axis=1)
-
-    def some(blocks, low, to):
+    for low in range(0, 3 * MIDDLE, HALF):
         pieces = []
         for row in range(PAD):
             at = slice(low + row * MEM, low + (row + 1) * MEM)
@@ -487,24 +494,13 @@
         result = jnp.dot(left, right, preferred_element_type=F32)
         for row in range(PAD):
             for other in range(GRP):
-                outs[other][to + row * MEM : to + (row + 1) * MEM, :] = result[
+                outs[other][low + row * MEM : low + (row + 1) * MEM, :] = result[
                     other * MEM : (other + 1) * MEM, row * LANE : (row + 1) * LANE
                 ]
 
-    for field in range(3):
-        at, to = field * MIDDLE, field * CX * MEM
-        some(edge, at, to)
-        some(middle, at, to + HALF)
-        some(middle, at + HALF, to + 2 * HALF)
-        some(edge, at + HALF, to + 3 * HALF)
-
-
-def increments(where, weights, middle, edge):
-    return call(
-        increments_body,
-        (shaped(3 * CX * MEM, LANE),) * GRP,
-        (where, weights, *middle, *edge),
-    )
+
+def increments(where, weights, blocks):
+    return call(increments_body, (shaped(3 * MIDDLE, LANE),) * GRP, (where, weights, *blocks))
 
 
 def exchange(blocks):
@@ -571,18 +567,25 @@
     outer, rest, states = lax.cond(
         group < GRP, outer_rows, nothing, above, below, inner, known, stencils
     )
-    outer = exchange(outer)
-    propagated_trials = spread_out(where, inner, rest)
-
     pairs = [
         (r * SUB + q, (r + 1) * SUB + (q ^ 2)) for r in range(REG - 1) for q in range(SUB)
     ]
-    products = region_products(where, states)
-    products, _ = lax.optimization_barrier((products, middle[1:]))
-    from_above = lax.ppermute(products[2 * E :], TILE, pairs)
-    from_below = lax.ppermute(products[:E], TILE, [(b, a) for a, b in pairs])
-    weights = solve(where, products, from_above, from_below)
-    analysis_updates = unpack(where, exchange(increments(where, weights, middle, outer)))
+
+    def chain(states):
+        products = region_products(where, states)
+        from_above = lax.ppermute(products[2 * E :], TILE, pairs)
+        from_below = lax.ppermute(products[:E], TILE, [(b, a) for a, b in pairs])
+        return solve(where, products, from_above, from_below)
+
+    states, outer, _ = lax.optimization_barrier((states, outer, middle[1:]))
+    outer = exchange(outer)
+    propagated_trials = spread_out(where, inner, rest)
+    weights = lax.cond(group < GRP, chain, lambda states: jnp.zeros((E, E), F32), states)
+    analysis_updates = unpack(
+        where,
+        exchange(increments(where, weights, middle)),
+        exchange(increments(where, weights, outer)),
+    )
     return (propagated_trials, analysis_updates)
 
 

time: 122 us -> 120 us (0.984)
  the two profiles are of different devices: /device:TPU:31 before, /device:TPU:38 now
where the time goes in v5:
time: 120 us
  starting transfers between devices  43.5 us (36%)
  waiting for transfers between devices  29.1 us (24%)
  Pallas kernels  28.7 us (24%)
  blocking collectives  16.3 us (14%)
    pallas_call x8, Pallas kernels, call(): pl.pallas_call(body, out_shape=list(outs), in_specs=[SMEM] + [VMEM] * (le...  24.6 us
    ppermute x15, starting transfers between devices, exchange(): lax.ppermute(blocks[s], 'grp', [(i, (i + s) % GRP) for i in range(GRP)])  23.4 us
    ppermute x15, waiting for transfers between devices, exchange(): lax.ppermute(blocks[s], 'grp', [(i, (i + s) % GRP) for i in range(GRP)])  21.4 us
    all_to_all x1, blocking collectives, outer_rows(): return (outer, rest, lax.all_to_all(state, SIDE, 0, 0, tiled=True))  16.3 us
    ppermute x1, starting transfers between devices, on_device(): above = lax.ppermute(down, TILE, forward)  8.2 us
    ppermute x1, waiting for transfers between devices, chain(): from_above = lax.ppermute(products[2 * E:], TILE, pairs)  4.89 us
    ppermute x1, starting transfers between devices, on_device(): below = lax.ppermute(up, TILE, backward)  4.64 us
    ppermute x1, starting transfers between devices, chain(): from_below = lax.ppermute(products[:E], TILE, [(b, a) for a, b in pairs])  4.22 us
  transfers between devices with their start and end apart: 21, of which 10 were waited for; matrix products, arithmetic and copies ran while one was open for 1% of the time, Pallas kernels for 21%

profile of v5, /device:TPU:38, one launch (start us, length us, event | category | flops | bytes accessed | tf_op | source)
XLA Modules:
  0.0 119.6 jit_solution(2850899906313087153)
XLA Ops:
  0.7 0.1 pad_add_fusion.where
  0.8 2.7 %shard_map.95 = (f32[4,120,128]{2,1,0:T(8,128)}, f32[4,120,128]{2,1,0:T(8,128)}, f32[9,3,32,128]{3,2,1,0:T(8,128)}) custom-call(s32[4]{0:T(128)S(1)} %pad_add_fusion.where, f32[8,3,32,512]{3,2,1,0:T(8,128)} %trial.3, f32[32,512]{1,0:T(8,128)} %seabed.3), custom_call_target="tpu_custom_call" | custom-call | tf_op jit(solution)/shard_map/pallas_call | solution.py:126
  3.5 8.2 %collective-permute-start.4 = (f32[4,120,128]{2,1,0:T(8,128)}, f32[4,120,128]{2,1,0:T(8,128)S(1)}, u32[]{:S(2)}, u32[]{:S(2)}) collective-permute-start(f32[4,120,128]{2,1,0:T(8,128)} %get-tuple-element.85), channel_id=1, source_target_pairs={{0,2},{2,4},{4,6},{6,8},{8,10},{10,12},{12,14},{14,16},{16,18},{18... | collective-permute-start | bytes 737288 | tf_op jit(solution)/shard_map/ppermute | solution.py:526
  11.7 4.6 %collective-permute-start.5 = (f32[4,120,128]{2,1,0:T(8,128)}, f32[4,120,128]{2,1,0:T(8,128)S(1)}, u32[]{:S(2)}, u32[]{:S(2)}) collective-permute-start(f32[4,120,128]{2,1,0:T(8,128)} %get-tuple-element.86), channel_id=1, source_target_pairs={{2,0},{4,2},{6,4},{8,6},{10,8},{12,10},{14,12},{16,14},{18,16},{20... | collective-permute-start | bytes 737288 | tf_op jit(solution)/shard_map/ppermute | solution.py:527
  16.3 0.1 collective-permute-start.3
  16.6 0.1 mul.35
  16.7 0.1 mul.33
  16.8 0.1 add_bitcast_fusion
  16.9 1.5 %collective-permute-done.3.beside = f32[9,3,32,128]{3,2,1,0:T(8,128)S(1)} collective-permute-done((f32[9,3,32,128]{3,2,1,0:T(8,128)}, f32[9,3,32,128]{3,2,1,0:T(8,128)S(1)}, u32[]{:S(2)}, u32[]{:S(2)}) %collective-permute-start.3) | collective-permute-done | bytes 442400 | tf_op jit(solution)/shard_map/ppermute | solution.py:528
  18.4 1.0 collective-permute-start.8
  19.4 2.3 %collective-permute-start.7 = (f32[8,128]{1,0:T(8,128)S(1)}, f32[8,128]{1,0:T(8,128)S(1)}, u32[]{:S(2)}, u32[]{:S(2)}) collective-permute-start(f32[8,128]{1,0:T(8,128)S(1)} %pad.12), channel_id=1, source_target_pairs={{0,128},{64,192},{128,0},{192,64},{1,129},{65,193},{129,1},{193,65... | collective-permute-start | bytes 12296 | tf_op jit(solution)/shard_map/ppermute | solution.py:508
  21.7 2.8 %collective-permute-start.6 = (f32[8,128]{1,0:T(8,128)S(1)}, f32[8,128]{1,0:T(8,128)S(1)}, u32[]{:S(2)}, u32[]{:S(2)}) collective-permute-start(f32[8,128]{1,0:T(8,128)S(1)} %pad.12), channel_id=1, source_target_pairs={{0,64},{64,128},{128,192},{192,0},{1,65},{65,129},{129,193},{193,1... | collective-permute-start | bytes 12296 | tf_op jit(solution)/shard_map/ppermute | solution.py:508
  24.6 0.1 copy.15
  24.6 0.1 stack_reshape.3
  24.7 9.7 %shard_map.96 = (f32[384,128]{1,0:T(8,128)S(1)}, f32[384,128]{1,0:T(8,128)S(1)}, f32[384,128]{1,0:T(8,128)S(1)}, f32[384,128]{1,0:T(8,128)S(1)}, f32[4,5,256,128]{3,2,1,0:T(8,128)}) custom-call(s32[4]{0:T(128)S(1)} %pad_add_fusion.where, f32[8,3,32,512]{3,2,1,0:T(8,128)S(1)} %copy-done, f32[32,512]{1,0:T(8,128)S(1)} %copy-done.1, ...), custom_call_target="tpu_custom_call" | custom-call | flops 10000000 | bytes 32000000 | tf_op jit(solution)/shard_map/pallas_call | solution.py:41
  34.5 0.3 collective-permute-done.6
  34.8 1.5 %collective-permute-start.9 = (f32[384,128]{1,0:T(8,128)S(1)}, f32[384,128]{1,0:T(8,128)S(1)}, u32[]{:S(2)}, u32[]{:S(2)}) collective-permute-start(f32[384,128]{1,0:T(8,128)S(1)} %get-tuple-element.100), channel_id=1, source_target_pairs={{0,64},{64,128},{128,192},{192,0},{1,65},{65,129},{129,193},{193,1... | collective-permute-start | bytes 589832 | tf_op jit(solution)/shard_map/ppermute | solution.py:508
  36.3 2.0 %collective-permute-start.10 = (f32[384,128]{1,0:T(8,128)S(1)}, f32[384,128]{1,0:T(8,128)S(1)}, u32[]{:S(2)}, u32[]{:S(2)}) collective-permute-start(f32[384,128]{1,0:T(8,128)S(1)} %get-tuple-element.101), channel_id=1, source_target_pairs={{0,128},{64,192},{128,0},{192,64},{1,129},{65,193},{129,1},{193,65... | collective-permute-start | bytes 589832 | tf_op jit(solution)/shard_map/ppermute | solution.py:508
  38.3 0.9 collective-permute-start.11
  39.2 20.8 %conditional.2 = (f32[384,128]{1,0:T(8,128)S(1)}, f32[384,128]{1,0:T(8,128)S(1)}, f32[384,128]{1,0:T(8,128)S(1)}, f32[384,128]{1,0:T(8,128)S(1)}, f32[3,4,128,12...) conditional(s32[]{:T(128)} %convert_element_type.42, () %tuple.27, (s32[]{:T(128)}, f32[4,120,128]{2,1,0:T(8,128)S(1)}, ...), branch_computations={%region_0.1_spmd, %region_1.2_spmd} | conditional | flops 30722 | bytes 1769544 | solution.py:567
  39.3 0.1 collective-permute-start
  39.4 1.3 %collective-permute-done.corner = f32[2,120,128]{2,1,0:T(8,128)S(1)} collective-permute-done((f32[2,120,128]{2,1,0:T(8,128)S(1)}, f32[2,120,128]{2,1,0:T(8,128)S(1)}, u32[]{:S(2)}, u32[]{:S(2)}) %collective-permute-start) | collective-permute-done | bytes 122912 | tf_op jit(solution)/shard_map/cond/branch_1_fun/ppermute | solution.py:554
  40.7 2.9 %branch_1_fun.3 = (f32[384,128]{1,0:T(8,128)S(1)}, f32[384,128]{1,0:T(8,128)S(1)}, f32[384,128]{1,0:T(8,128)S(1)}, f32[384,128]{1,0:T(8,128)S(1)}, f32[96,4,128]...) custom-call(s32[4]{0:T(128)} %copy-done.4, f32[4,5,256,128]{3,2,1,0:T(8,128)} %get-tuple-element.28.inner, ...), custom_call_target="tpu_custom_call" | custom-call | tf_op jit(solution)/shard_map/cond/branch_1_fun/pallas_call | solution.py:41
  43.7 16.3 %all_to_all.4 = f32[96,4,128]{2,1,0:T(4,128)S(1)} all-to-all(f32[96,4,128]{2,1,0:T(4,128)S(1)} %get-tuple-element.42), channel_id=1, replica_groups=mesh['grp'=4,'reg'=8,'sub'=4,'cores'=2] {'grp','sub','cores'}, dimensions={0} | all-to-all | bytes 393216 | tf_op jit(solution)/shard_map/cond/branch_1_fun/all_to_all | solution.py:558
  60.0 1.4 %collective-permute-start.12 = (f32[384,128]{1,0:T(8,128)S(1)}, f32[384,128]{1,0:T(8,128)S(1)}, u32[]{:S(2)}, u32[]{:S(2)}) collective-permute-start(f32[384,128]{1,0:T(8,128)S(1)} %get-tuple-element.105), channel_id=1, source_target_pairs={{0,64},{64,128},{128,192},{192,0},{1,65},{65,129},{129,193},{193,1... | collective-permute-start | bytes 589832 | tf_op jit(solution)/shard_map/ppermute | solution.py:508
  61.4 2.3 %collective-permute-start.13 = (f32[384,128]{1,0:T(8,128)S(1)}, f32[384,128]{1,0:T(8,128)S(1)}, u32[]{:S(2)}, u32[]{:S(2)}) collective-permute-start(f32[384,128]{1,0:T(8,128)S(1)} %get-tuple-element.106), channel_id=1, source_target_pairs={{0,128},{64,192},{128,0},{192,64},{1,129},{65,193},{129,1},{193,65... | collective-permute-start | bytes 589832 | tf_op jit(solution)/shard_map/ppermute | solution.py:508
  63.7 1.6 %collective-permute-start.14 = (f32[384,128]{1,0:T(8,128)S(1)}, f32[384,128]{1,0:T(8,128)S(1)}, u32[]{:S(2)}, u32[]{:S(2)}) collective-permute-start(f32[384,128]{1,0:T(8,128)S(1)} %get-tuple-element.107), channel_id=1, source_target_pairs={{0,192},{64,0},{128,64},{192,128},{1,193},{65,1},{129,65},{193,129... | collective-permute-start | bytes 589832 | tf_op jit(solution)/shard_map/ppermute | solution.py:508
  65.3 16.7 %conditional.3 = (f32[32,32]{1,0:T(8,128)S(1)}) conditional(s32[]{:T(128)} %convert_element_type.42, () %tuple.30, (s32[4]{0:T(128)}, f32[96,4,128]{2,1,0:T(4,128)S(1)}) %tuple.43), branch_computations={%region_2.3_spmd, %region_3.4_spmd} | conditional | bytes 98392 | solution.py:583
  65.3 1.4 %branch_1_fun.4.own = f32[96,64]{1,0:T(8,128)S(1)} custom-call(s32[4]{0:T(128)} %get-tuple-element.43.where, f32[96,4,128]{2,1,0:T(4,128)S(1)} %get-tuple-element.44.states), custom_call_target="tpu_custom_call" | custom-call | tf_op jit(solution)/shard_map/cond/branch_1_fun/pallas_call | solution.py:41
  66.7 4.2 %collective-permute-start.2 = (f32[32,64]{1,0:T(8,128)S(1)}, f32[32,64]{1,0:T(8,128)S(1)}, u32[]{:S(2)}, u32[]{:S(2)}) collective-permute-start(f32[32,64]{1,0:T(8,128)S(1)} %get-tuple-element.117), channel_id=1, source_target_pairs={{12,0},{14,2},{8,4},{10,6},{20,8},{22,10},{16,12},{18,14},{28,16},... | collective-permute-start | bytes 24584 | tf_op jit(solution)/shard_map/cond/branch_1_fun/ppermute | solution.py:577
  70.9 2.8 %collective-permute-start.1 = (f32[32,64]{1,0:T(8,128)S(1)}, f32[32,64]{1,0:T(8,128)S(1)}, u32[]{:S(2)}, u32[]{:S(2)}) collective-permute-start(f32[32,64]{1,0:T(8,128)S(1)} %get-tuple-element.118), channel_id=1, source_target_pairs={{0,12},{2,14},{4,8},{6,10},{8,20},{10,22},{12,16},{14,18},{16,28},... | collective-permute-start | bytes 24584 | tf_op jit(solution)/shard_map/cond/branch_1_fun/ppermute | solution.py:576
  73.8 4.9 %collective-permute-done.1.low = f32[32,64]{1,0:T(8,128)S(1)} collective-permute-done((f32[32,64]{1,0:T(8,128)S(1)}, f32[32,64]{1,0:T(8,128)S(1)}, u32[]{:S(2)}, u32[]{:S(2)}) %collective-permute-start.1) | collective-permute-done | bytes 8224 | tf_op jit(solution)/shard_map/cond/branch_1_fun/ppermute | solution.py:576
  78.7 3.3 %branch_1_fun.5 = f32[32,32]{1,0:T(8,128)S(1)} custom-call(s32[4]{0:T(128)} %get-tuple-element.43.where, f32[96,64]{1,0:T(8,128)S(1)} %branch_1_fun.4.own, f32[32,64]{1,0:T(8,128)S(1)} %collective-permute-done.1.low, f32[32,64]{1,0:T(8,128)S(1)} %collective-permute-done.2.high), custom_call_target="tpu_custom_call" | custom-call | tf_op jit(solution)/shard_map/cond/branch_1_fun/pallas_call | solution.py:41
  82.0 1.1 shard_map.99
  83.1 0.8 collective-permute-start.18
  83.9 1.9 %collective-permute-start.19 = (f32[384,128]{1,0:T(8,128)S(1)}, f32[384,128]{1,0:T(8,128)S(1)}, u32[]{:S(2)}, u32[]{:S(2)}) collective-permute-start(f32[384,128]{1,0:T(8,128)S(1)} %get-tuple-element.115), channel_id=1, source_target_pairs={{0,128},{64,192},{128,0},{192,64},{1,129},{65,193},{129,1},{193,65... | collective-permute-start | bytes 589832 | tf_op jit(solution)/shard_map/ppermute | solution.py:508
  85.8 1.1 shard_map.98
  86.9 2.1 %collective-permute-start.15 = (f32[384,128]{1,0:T(8,128)S(1)}, f32[384,128]{1,0:T(8,128)S(1)}, u32[]{:S(2)}, u32[]{:S(2)}) collective-permute-start(f32[384,128]{1,0:T(8,128)S(1)} %get-tuple-element.109), channel_id=1, source_target_pairs={{0,64},{64,128},{128,192},{192,0},{1,65},{65,129},{129,193},{193,1... | collective-permute-start | bytes 589832 | tf_op jit(solution)/shard_map/ppermute | solution.py:508
  88.9 2.9 %collective-permute-start.16 = (f32[384,128]{1,0:T(8,128)S(1)}, f32[384,128]{1,0:T(8,128)S(1)}, u32[]{:S(2)}, u32[]{:S(2)}) collective-permute-start(f32[384,128]{1,0:T(8,128)S(1)} %get-tuple-element.110), channel_id=1, source_target_pairs={{0,128},{64,192},{128,0},{192,64},{1,129},{65,193},{129,1},{193,65... | collective-permute-start | bytes 589832 | tf_op jit(solution)/shard_map/ppermute | solution.py:508
  91.8 2.8 %collective-permute-done.18.refs_1_ = f32[384,128]{1,0:T(8,128)S(1)} collective-permute-done((f32[384,128]{1,0:T(8,128)S(1)}, f32[384,128]{1,0:T(8,128)S(1)}, u32[]{:S(2)}, u32[]{:S(2)}) %collective-permute-start.18) | collective-permute-done | bytes 196640 | tf_op jit(solution)/shard_map/ppermute | solution.py:508
  94.6 3.2 %shard_map.97 = f32[8,3,32,512]{3,2,1,0:T(8,128)} custom-call(s32[4]{0:T(128)S(1)} %copy-done.3, f32[4,5,256,128]{3,2,1,0:T(8,128)} %get-tuple-element.84.inner, f32[3,4,128,128]{3,2,1,0:T(8,128)S(1)} %get-tuple-element.90.outer), custom_call_target="tpu_custom_call" | custom-call | tf_op jit(solution)/shard_map/pallas_call | solution.py:41
  97.8 11.6 %collective-permute-done.19.refs_2_ = f32[384,128]{1,0:T(8,128)S(1)} collective-permute-done((f32[384,128]{1,0:T(8,128)S(1)}, f32[384,128]{1,0:T(8,128)S(1)}, u32[]{:S(2)}, u32[]{:S(2)}) %collective-permute-start.19) | collective-permute-done | bytes 196640 | tf_op jit(solution)/shard_map/ppermute | solution.py:508
  109.5 0.8 collective-permute-done.20.refs_3_
  110.3 1.8 %shard_map.100.refs_4_ = f32[8,3,32,512]{3,2,1,0:T(8,128)} custom-call(s32[4]{0:T(128)S(1)} %copy-done.3, f32[384,128]{1,0:T(8,128)S(1)} %get-tuple-element.113.refs_0_, f32[384,128]{1,0:T(8,128)S(1)} %collective-permute-done.18.refs_1_, f32[384,128]{1,0:T(8,128)S(1)} %collective-permute-done.19.refs_2_, f32[384,128]{1,0:T(8,128)S(1)} %collective-permute-done.20.refs_3_), custom_call_target="tpu_custom_call" | custom-call | flops 10000000 | bytes 32000000 | tf_op jit(solution)/shard_map/pallas_call | solution.py:41
  112.1 1.4 %collective-permute-done.15.refs_1_ = f32[384,128]{1,0:T(8,128)S(1)} collective-permute-done((f32[384,128]{1,0:T(8,128)S(1)}, f32[384,128]{1,0:T(8,128)S(1)}, u32[]{:S(2)}, u32[]{:S(2)}) %collective-permute-start.15) | collective-permute-done | bytes 196640 | tf_op jit(solution)/shard_map/ppermute | solution.py:508
  113.6 2.1 %collective-permute-done.16.refs_2_ = f32[384,128]{1,0:T(8,128)S(1)} collective-permute-done((f32[384,128]{1,0:T(8,128)S(1)}, f32[384,128]{1,0:T(8,128)S(1)}, u32[]{:S(2)}, u32[]{:S(2)}) %collective-permute-start.16) | collective-permute-done | bytes 196640 | tf_op jit(solution)/shard_map/ppermute | solution.py:508
  115.7 2.3 %collective-permute-done.17.refs_3_ = f32[384,128]{1,0:T(8,128)S(1)} collective-permute-done((f32[384,128]{1,0:T(8,128)S(1)}, f32[384,128]{1,0:T(8,128)S(1)}, u32[]{:S(2)}, u32[]{:S(2)}) %collective-permute-start.17) | collective-permute-done | bytes 196640 | tf_op jit(solution)/shard_map/ppermute | solution.py:508
  117.9 1.5 %shard_map.101 = f32[8,3,32,512]{3,2,1,0:T(8,128)} custom-call(s32[4]{0:T(128)S(1)} %copy-done.3, f32[384,128]{1,0:T(8,128)S(1)} %get-tuple-element.108.refs_0_, f32[384,128]{1,0:T(8,128)S(1)} %collective-permute-done.15.refs_1_, f32[384,128]{1,0:T(8,128)S(1)} %collective-permute-done.16.refs_2_, ...), custom_call_target="tpu_custom_call", output_to_operand_aliasing={{}: (5, {})} | custom-call | tf_op jit(solution)/shard_map/pallas_call | solution.py:381
  (61 shorter events, 0.3 us)
Async XLA Ops:
  0.6 24.1 %copy-start.1 = (f32[32,512]{1,0:T(8,128)S(1)}, f32[32,512]{1,0:T(8,128)}, u32[]{:S(2)}) copy-start(f32[32,512]{1,0:T(8,128)} %seabed.3) | copy-start | bytes 196612
  0.6 24.1 %copy-start = (f32[8,3,32,512]{3,2,1,0:T(8,128)S(1)}, f32[8,3,32,512]{3,2,1,0:T(8,128)}, u32[]{:S(2)}) copy-start(f32[8,3,32,512]{3,2,1,0:T(8,128)} %trial.3) | copy-start | bytes 4718596
  0.7 15.8 %copy-start.14 = (s32[16,4]{0,1:T(4,128)S(1)}, s32[16,4]{0,1:T(4,128)}, u32[]{:S(2)}) copy-start(s32[16,4]{0,1:T(4,128)} %param.17) | copy-start | bytes 772
  0.7 15.8 %copy-start.13 = (f32[16]{0:T(128)S(1)}, f32[16]{0:T(128)}, u32[]{:S(2)}) copy-start(f32[16]{0:T(128)} %param.15) | copy-start | bytes 196
  0.7 16.0 %copy-start.10 = (s32[16,8]{0,1:T(8,128)S(1)}, s32[16,8]{0,1:T(8,128)}, u32[]{:S(2)}) copy-start(s32[16,8]{0,1:T(8,128)} %param.19) | copy-start | bytes 1540
  0.7 16.0 %copy-start.11 = (f32[16,4]{0,1:T(4,128)S(1)}, f32[16,4]{0,1:T(4,128)}, u32[]{:S(2)}) copy-start(f32[16,4]{0,1:T(4,128)} %param.18) | copy-start | bytes 772
  0.7 16.1 %copy-start.6 = (f32[16,32]{1,0:T(8,128)S(1)}, f32[16,32]{1,0:T(8,128)}, u32[]{:S(2)}) copy-start(f32[16,32]{1,0:T(8,128)} %param.16) | copy-start | bytes 6148
  0.7 16.1 %copy-start.12 = (f32[16]{0:T(128)S(1)}, f32[16]{0:T(128)}, u32[]{:S(2)}) copy-start(f32[16]{0:T(128)} %param.14) | copy-start | bytes 196
  0.8 38.3 %copy-start.2 = (s32[4]{0:T(128)}, s32[4]{0:T(128)S(1)}, u32[]{:S(2)}) copy-start(s32[4]{0:T(128)S(1)} %pad_add_fusion.where) | copy-start | bytes 52
  3.5 35.7 %collective-permute-start.4 = (f32[4,120,128]{2,1,0:T(8,128)}, f32[4,120,128]{2,1,0:T(8,128)S(1)}, u32[]{:S(2)}, u32[]{:S(2)}) collective-permute-start(f32[4,120,128]{2,1,0:T(8,128)} %get-tuple-element.85), channel_id=1, source_target_pairs={{0,2},{2,4},{4,6},{6,8},{8,10},{10,12},{12,14},{14,16},{16,18},{18... | collective-permute-start | bytes 737288 | tf_op jit(solution)/shard_map/ppermute | solution.py:526
  11.7 27.5 %collective-permute-start.5 = (f32[4,120,128]{2,1,0:T(8,128)}, f32[4,120,128]{2,1,0:T(8,128)S(1)}, u32[]{:S(2)}, u32[]{:S(2)}) collective-permute-start(f32[4,120,128]{2,1,0:T(8,128)} %get-tuple-element.86), channel_id=1, source_target_pairs={{2,0},{4,2},{6,4},{8,6},{10,8},{12,10},{14,12},{16,14},{18,16},{20... | collective-permute-start | bytes 737288 | tf_op jit(solution)/shard_map/ppermute | solution.py:527
  16.3 2.1 %collective-permute-start.3 = (f32[9,3,32,128]{3,2,1,0:T(8,128)}, f32[9,3,32,128]{3,2,1,0:T(8,128)S(1)}, u32[]{:S(2)}, u32[]{:S(2)}) collective-permute-start(f32[9,3,32,128]{3,2,1,0:T(8,128)} %get-tuple-element.82), channel_id=1, source_target_pairs={{0,1},{1,0},{2,3},{3,2},{4,5},{5,4},{6,7},{7,6},{8,9},{9,8},{10,11... | collective-permute-start | bytes 1327112 | tf_op jit(solution)/shard_map/ppermute | solution.py:528
  18.4 16.0 %collective-permute-start.8 = (f32[8,128]{1,0:T(8,128)S(1)}, f32[8,128]{1,0:T(8,128)S(1)}, u32[]{:S(2)}, u32[]{:S(2)}) collective-permute-start(f32[8,128]{1,0:T(8,128)S(1)} %pad.12), channel_id=1, source_target_pairs={{0,192},{64,0},{128,64},{192,128},{1,193},{65,1},{129,65},{193,129... | collective-permute-start | bytes 12296 | tf_op jit(solution)/shard_map/ppermute | solution.py:508
  19.4 15.0 %collective-permute-start.7 = (f32[8,128]{1,0:T(8,128)S(1)}, f32[8,128]{1,0:T(8,128)S(1)}, u32[]{:S(2)}, u32[]{:S(2)}) collective-permute-start(f32[8,128]{1,0:T(8,128)S(1)} %pad.12), channel_id=1, source_target_pairs={{0,128},{64,192},{128,0},{192,64},{1,129},{65,193},{129,1},{193,65... | collective-permute-start | bytes 12296 | tf_op jit(solution)/shard_map/ppermute | solution.py:508
  21.7 13.0 %collective-permute-start.6 = (f32[8,128]{1,0:T(8,128)S(1)}, f32[8,128]{1,0:T(8,128)S(1)}, u32[]{:S(2)}, u32[]{:S(2)}) collective-permute-start(f32[8,128]{1,0:T(8,128)S(1)} %pad.12), channel_id=1, source_target_pairs={{0,64},{64,128},{128,192},{192,0},{1,65},{65,129},{129,193},{193,1... | collective-permute-start | bytes 12296 | tf_op jit(solution)/shard_map/ppermute | solution.py:508
  34.8 25.2 %collective-permute-start.9 = (f32[384,128]{1,0:T(8,128)S(1)}, f32[384,128]{1,0:T(8,128)S(1)}, u32[]{:S(2)}, u32[]{:S(2)}) collective-permute-start(f32[384,128]{1,0:T(8,128)S(1)} %get-tuple-element.100), channel_id=1, source_target_pairs={{0,64},{64,128},{128,192},{192,0},{1,65},{65,129},{129,193},{193,1... | collective-permute-start | bytes 589832 | tf_op jit(solution)/shard_map/ppermute | solution.py:508
  36.3 23.7 %collective-permute-start.10 = (f32[384,128]{1,0:T(8,128)S(1)}, f32[384,128]{1,0:T(8,128)S(1)}, u32[]{:S(2)}, u32[]{:S(2)}) collective-permute-start(f32[384,128]{1,0:T(8,128)S(1)} %get-tuple-element.101), channel_id=1, source_target_pairs={{0,128},{64,192},{128,0},{192,64},{1,129},{65,193},{129,1},{193,65... | collective-permute-start | bytes 589832 | tf_op jit(solution)/shard_map/ppermute | solution.py:508
  38.3 21.7 %collective-permute-start.11 = (f32[384,128]{1,0:T(8,128)S(1)}, f32[384,128]{1,0:T(8,128)S(1)}, u32[]{:S(2)}, u32[]{:S(2)}) collective-permute-start(f32[384,128]{1,0:T(8,128)S(1)} %get-tuple-element.102), channel_id=1, source_target_pairs={{0,192},{64,0},{128,64},{192,128},{1,193},{65,1},{129,65},{193,129... | collective-permute-start | bytes 589832 | tf_op jit(solution)/shard_map/ppermute | solution.py:508
  39.2 1.5 %copy-start.4 = (s32[4]{0:T(128)}, s32[4]{0:T(128)S(1)}, u32[]{:S(2)}) copy-start(s32[4]{0:T(128)S(1)} %get-tuple-element.24.where) | copy-start | bytes 52 | tf_op jit(solution)/shard_map/cond
  39.2 1.5 %copy-start.5 = (f32[8,128]{1,0:T(8,128)}, f32[8,128]{1,0:T(8,128)S(1)}, u32[]{:S(2)}) copy-start(f32[8,128]{1,0:T(8,128)S(1)} %get-tuple-element.33.rest_0_) | copy-start | bytes 12292 | tf_op jit(solution)/shard_map/cond
  39.2 1.5 %copy-start.7 = (f32[8,128]{1,0:T(8,128)}, f32[8,128]{1,0:T(8,128)S(1)}, u32[]{:S(2)}) copy-start(f32[8,128]{1,0:T(8,128)S(1)} %get-tuple-element.36.rest_3_) | copy-start | bytes 12292 | tf_op jit(solution)/shard_map/cond
  39.2 1.5 %copy-start.8 = (f32[8,128]{1,0:T(8,128)}, f32[8,128]{1,0:T(8,128)S(1)}, u32[]{:S(2)}) copy-start(f32[8,128]{1,0:T(8,128)S(1)} %get-tuple-element.35.rest_2_) | copy-start | bytes 12292 | tf_op jit(solution)/shard_map/cond
  39.2 1.5 %copy-start.9 = (f32[8,128]{1,0:T(8,128)}, f32[8,128]{1,0:T(8,128)S(1)}, u32[]{:S(2)}) copy-start(f32[8,128]{1,0:T(8,128)S(1)} %get-tuple-element.34.rest_1_) | copy-start | bytes 12292 | tf_op jit(solution)/shard_map/cond
  39.3 1.4 %collective-permute-start = (f32[2,120,128]{2,1,0:T(8,128)S(1)}, f32[2,120,128]{2,1,0:T(8,128)S(1)}, u32[]{:S(2)}, u32[]{:S(2)}) collective-permute-start(f32[2,120,128]{2,1,0:T(8,128)S(1)} %pad_maximum_fusion), channel_id=1, source_target_pairs={{0,1},{1,0},{2,3},{3,2},{4,5},{5,4},{6,7},{7,6},{8,9},{9,8},{10,11... | collective-permute-start | bytes 368648 | tf_op jit(solution)/shard_map/cond/branch_1_fun/ppermute | solution.py:554
  60.0 34.7 %copy-start.3 = (s32[4]{0:T(128)S(1)}, s32[4]{0:T(128)}, u32[]{:S(2)}) copy-start(s32[4]{0:T(128)} %copy-done.2) | copy-start | bytes 52
  60.0 25.8 %collective-permute-start.12 = (f32[384,128]{1,0:T(8,128)S(1)}, f32[384,128]{1,0:T(8,128)S(1)}, u32[]{:S(2)}, u32[]{:S(2)}) collective-permute-start(f32[384,128]{1,0:T(8,128)S(1)} %get-tuple-element.105), channel_id=1, source_target_pairs={{0,64},{64,128},{128,192},{192,0},{1,65},{65,129},{129,193},{193,1... | collective-permute-start | bytes 589832 | tf_op jit(solution)/shard_map/ppermute | solution.py:508
  61.4 24.4 %collective-permute-start.13 = (f32[384,128]{1,0:T(8,128)S(1)}, f32[384,128]{1,0:T(8,128)S(1)}, u32[]{:S(2)}, u32[]{:S(2)}) collective-permute-start(f32[384,128]{1,0:T(8,128)S(1)} %get-tuple-element.106), channel_id=1, source_target_pairs={{0,128},{64,192},{128,0},{192,64},{1,129},{65,193},{129,1},{193,65... | collective-permute-start | bytes 589832 | tf_op jit(solution)/shard_map/ppermute | solution.py:508
  63.7 22.1 %collective-permute-start.14 = (f32[384,128]{1,0:T(8,128)S(1)}, f32[384,128]{1,0:T(8,128)S(1)}, u32[]{:S(2)}, u32[]{:S(2)}) collective-permute-start(f32[384,128]{1,0:T(8,128)S(1)} %get-tuple-element.107), channel_id=1, source_target_pairs={{0,192},{64,0},{128,64},{192,128},{1,193},{65,1},{129,65},{193,129... | collective-permute-start | bytes 589832 | tf_op jit(solution)/shard_map/ppermute | solution.py:508
  66.7 7.1 %collective-permute-start.2 = (f32[32,64]{1,0:T(8,128)S(1)}, f32[32,64]{1,0:T(8,128)S(1)}, u32[]{:S(2)}, u32[]{:S(2)}) collective-permute-start(f32[32,64]{1,0:T(8,128)S(1)} %get-tuple-element.117), channel_id=1, source_target_pairs={{12,0},{14,2},{8,4},{10,6},{20,8},{22,10},{16,12},{18,14},{28,16},... | collective-permute-start | bytes 24584 | tf_op jit(solution)/shard_map/cond/branch_1_fun/ppermute | solution.py:577
  70.9 7.7 %collective-permute-start.1 = (f32[32,64]{1,0:T(8,128)S(1)}, f32[32,64]{1,0:T(8,128)S(1)}, u32[]{:S(2)}, u32[]{:S(2)}) collective-permute-start(f32[32,64]{1,0:T(8,128)S(1)} %get-tuple-element.118), channel_id=1, source_target_pairs={{0,12},{2,14},{4,8},{6,10},{8,20},{10,22},{12,16},{14,18},{16,28},... | collective-permute-start | bytes 24584 | tf_op jit(solution)/shard_map/cond/branch_1_fun/ppermute | solution.py:576
  83.1 11.5 %collective-permute-start.18 = (f32[384,128]{1,0:T(8,128)S(1)}, f32[384,128]{1,0:T(8,128)S(1)}, u32[]{:S(2)}, u32[]{:S(2)}) collective-permute-start(f32[384,128]{1,0:T(8,128)S(1)} %get-tuple-element.114), channel_id=1, source_target_pairs={{0,64},{64,128},{128,192},{192,0},{1,65},{65,129},{129,193},{193,1... | collective-permute-start | bytes 589832 | tf_op jit(solution)/shard_map/ppermute | solution.py:508
  83.9 25.6 %collective-permute-start.19 = (f32[384,128]{1,0:T(8,128)S(1)}, f32[384,128]{1,0:T(8,128)S(1)}, u32[]{:S(2)}, u32[]{:S(2)}) collective-permute-start(f32[384,128]{1,0:T(8,128)S(1)} %get-tuple-element.115), channel_id=1, source_target_pairs={{0,128},{64,192},{128,0},{192,64},{1,129},{65,193},{129,1},{193,65... | collective-permute-start | bytes 589832 | tf_op jit(solution)/shard_map/ppermute | solution.py:508
  85.8 24.5 %collective-permute-start.20 = (f32[384,128]{1,0:T(8,128)S(1)}, f32[384,128]{1,0:T(8,128)S(1)}, u32[]{:S(2)}, u32[]{:S(2)}) collective-permute-start(f32[384,128]{1,0:T(8,128)S(1)} %get-tuple-element.116), channel_id=1, source_target_pairs={{0,192},{64,0},{128,64},{192,128},{1,193},{65,1},{129,65},{193,129... | collective-permute-start | bytes 589832 | tf_op jit(solution)/shard_map/ppermute | solution.py:508
  86.9 26.7 %collective-permute-start.15 = (f32[384,128]{1,0:T(8,128)S(1)}, f32[384,128]{1,0:T(8,128)S(1)}, u32[]{:S(2)}, u32[]{:S(2)}) collective-permute-start(f32[384,128]{1,0:T(8,128)S(1)} %get-tuple-element.109), channel_id=1, source_target_pairs={{0,64},{64,128},{128,192},{192,0},{1,65},{65,129},{129,193},{193,1... | collective-permute-start | bytes 589832 | tf_op jit(solution)/shard_map/ppermute | solution.py:508
  88.9 26.7 %collective-permute-start.16 = (f32[384,128]{1,0:T(8,128)S(1)}, f32[384,128]{1,0:T(8,128)S(1)}, u32[]{:S(2)}, u32[]{:S(2)}) collective-permute-start(f32[384,128]{1,0:T(8,128)S(1)} %get-tuple-element.110), channel_id=1, source_target_pairs={{0,128},{64,192},{128,0},{192,64},{1,129},{65,193},{129,1},{193,65... | collective-permute-start | bytes 589832 | tf_op jit(solution)/shard_map/ppermute | solution.py:508
  94.6 23.3 %collective-permute-start.17 = (f32[384,128]{1,0:T(8,128)S(1)}, f32[384,128]{1,0:T(8,128)S(1)}, u32[]{:S(2)}, u32[]{:S(2)}) collective-permute-start(f32[384,128]{1,0:T(8,128)S(1)} %get-tuple-element.111), channel_id=1, source_target_pairs={{0,192},{64,0},{128,64},{192,128},{1,193},{65,1},{129,65},{193,129... | collective-permute-start | bytes 589832 | tf_op jit(solution)/shard_map/ppermute | solution.py:508

commit v6 on v5

--- a/solution.py
+++ b/solution.py
@@ -412,7 +412,7 @@
     return call(spread_out_body, (shaped(MEM, 3, CX, CY),), (where, inner, outer))[0]
 
 
-def products_body(where, states, out, seen_at, wanted_at):
+def products_body(where, states, own, send, seen_at, wanted_at):
     group = where[0]
     lane = lax.broadcasted_iota(jnp.int32, (1, LANE), 1)
 
@@ -442,26 +442,28 @@
         scaled = anomaly / jnp.where(lane < GRP * OBS, other[3:4, :], 1.0)
         left.append(jnp.concatenate([scaled * other[r : r + 1, :] for r in range(3)], axis=0))
         right.append(jnp.concatenate([anomaly, wanted], axis=0))
-    out[...] = lax.dot_general(
+    products = lax.dot_general(
         jnp.concatenate(left, axis=1),
         jnp.concatenate(right, axis=1),
         (((1,), (1,)), ((), ())),
         precision=HIGHEST,
         preferred_element_type=F32,
     )
+    own[...] = products[E : 2 * E, :]
+    send[...] = jnp.where(where[1] == 0, products[2 * E :, :], products[:E, :])
 
 
 def region_products(where, states):
     return call(
         products_body,
-        (shaped(3 * E, 2 * E),),
+        (shaped(E, 2 * E),) * 2,
         (where, states),
         [pltpu.VMEM((SUB * 2, GRP, MEM, LANE), F32)] * 2,
-    )[0]
+    )
 
 
 def solve_body(where, own, low, high, out):
-    total = own[E : 2 * E, :] + low[...] + high[...]
+    total = own[...] + low[...] + high[...]
     row = lax.broadcasted_iota(jnp.int32, (E, 2 * E), 0)
     lane = lax.broadcasted_iota(jnp.int32, (E, 2 * E), 1)
     system = total + jnp.where(row == lane, E - 1.0, 0.0)
@@ -570,12 +572,13 @@
     pairs = [
         (r * SUB + q, (r + 1) * SUB + (q ^ 2)) for r in range(REG - 1) for q in range(SUB)
     ]
+    pairs = [(2 * a, 2 * b) for a, b in pairs] + [(2 * b + 1, 2 * a + 1) for a, b in pairs]
 
     def chain(states):
-        products = region_products(where, states)
-        from_above = lax.ppermute(products[2 * E :], TILE, pairs)
-        from_below = lax.ppermute(products[:E], TILE, [(b, a) for a, b in pairs])
-        return solve(where, products, from_above, from_below)
+        own, send = region_products(where, states)
+        came = lax.ppermute(send, ("reg", "sub", "cores"), pairs)
+        swapped = lax.ppermute(came, "cores", [(0, 1), (1, 0)])
+        return solve(where, own, came, swapped)
 
     states, outer, _ = lax.optimization_barrier((states, outer, middle[1:]))
     outer = exchange(outer)

time: 120 us -> 119 us (level)
  starting transfers between devices: 43.5 us -> 42.1 us
    ppermute x2, starting transfers between devices: 7.05 us -> 3.95 us  [the longest x1 3.95 us: chain(): came = lax.ppermute(send, ('reg', 'sub', 'cores'), pairs)]
    ppermute x15, starting transfers between devices: 23.4 us -> 25.1 us  [exchange(): lax.ppermute(blocks[s], 'grp', [(i, (i + s) % GRP) for i in range(GRP)])]
  transfers between devices with their start and end apart: 21 -> 21, of which waited for: 10 -> 9; matrix products, arithmetic and copies ran while one was open for 1% -> 1% of each run, Pallas kernels for 21% -> 20%
where the time goes in v6:
time: 119 us
  starting transfers between devices  42.1 us (35%)
  waiting for transfers between devices  30.3 us (25%)
  Pallas kernels  28.2 us (24%)
  blocking collectives  16.4 us (14%)
    ppermute x15, starting transfers between devices, exchange(): lax.ppermute(blocks[s], 'grp', [(i, (i + s) % GRP) for i in range(GRP)])  25.1 us
    pallas_call x8, Pallas kernels, call(): pl.pallas_call(body, out_shape=list(outs), in_specs=[SMEM] + [VMEM] * (le...  24 us
    ppermute x15, waiting for transfers between devices, exchange(): lax.ppermute(blocks[s], 'grp', [(i, (i + s) % GRP) for i in range(GRP)])  22.5 us
    all_to_all x1, blocking collectives, outer_rows(): return (outer, rest, lax.all_to_all(state, SIDE, 0, 0, tiled=True))  16.4 us
    ppermute x1, starting transfers between devices, on_device(): above = lax.ppermute(down, TILE, forward)  8.2 us
    ppermute x1, starting transfers between devices, on_device(): below = lax.ppermute(up, TILE, backward)  4.64 us
    ppermute x1, starting transfers between devices, chain(): came = lax.ppermute(send, ('reg', 'sub', 'cores'), pairs)  3.95 us
    ppermute x1, waiting for transfers between devices, chain(): came = lax.ppermute(send, ('reg', 'sub', 'cores'), pairs)  3.78 us
  transfers between devices with their start and end apart: 21, of which 9 were waited for; matrix products, arithmetic and copies ran while one was open for 1% of the time, Pallas kernels for 20%

profile of v6, /device:TPU:38, one launch (start us, length us, event | category | flops | bytes accessed | tf_op | source)
XLA Modules:
  0.0 118.9 jit_solution(3146557820062956138)
XLA Ops:
  0.7 0.1 pad_add_fusion.where
  0.8 2.7 %shard_map.95 = (f32[4,120,128]{2,1,0:T(8,128)}, f32[4,120,128]{2,1,0:T(8,128)}, f32[9,3,32,128]{3,2,1,0:T(8,128)}) custom-call(s32[4]{0:T(128)S(1)} %pad_add_fusion.where, f32[8,3,32,512]{3,2,1,0:T(8,128)} %trial.3, f32[32,512]{1,0:T(8,128)} %seabed.3), custom_call_target="tpu_custom_call" | custom-call | tf_op jit(solution)/shard_map/pallas_call | solution.py:126
  3.5 8.2 %collective-permute-start.4 = (f32[4,120,128]{2,1,0:T(8,128)}, f32[4,120,128]{2,1,0:T(8,128)S(1)}, u32[]{:S(2)}, u32[]{:S(2)}) collective-permute-start(f32[4,120,128]{2,1,0:T(8,128)} %get-tuple-element.87), channel_id=1, source_target_pairs={{0,2},{2,4},{4,6},{6,8},{8,10},{10,12},{12,14},{14,16},{16,18},{18... | collective-permute-start | bytes 737288 | tf_op jit(solution)/shard_map/ppermute | solution.py:528
  11.7 4.6 %collective-permute-start.5 = (f32[4,120,128]{2,1,0:T(8,128)}, f32[4,120,128]{2,1,0:T(8,128)S(1)}, u32[]{:S(2)}, u32[]{:S(2)}) collective-permute-start(f32[4,120,128]{2,1,0:T(8,128)} %get-tuple-element.88), channel_id=1, source_target_pairs={{2,0},{4,2},{6,4},{8,6},{10,8},{12,10},{14,12},{16,14},{18,16},{20... | collective-permute-start | bytes 737288 | tf_op jit(solution)/shard_map/ppermute | solution.py:529
  16.3 0.1 collective-permute-start.3
  16.5 0.1 mul.34
  16.6 0.1 mul.35
  16.7 0.1 mul.33
  16.8 0.1 add_bitcast_fusion
  16.9 1.5 %collective-permute-done.3.beside = f32[9,3,32,128]{3,2,1,0:T(8,128)S(1)} collective-permute-done((f32[9,3,32,128]{3,2,1,0:T(8,128)}, f32[9,3,32,128]{3,2,1,0:T(8,128)S(1)}, u32[]{:S(2)}, u32[]{:S(2)}) %collective-permute-start.3) | collective-permute-done | bytes 442400 | tf_op jit(solution)/shard_map/ppermute | solution.py:530
  18.4 1.0 collective-permute-start.8
  19.4 2.3 %collective-permute-start.7 = (f32[8,128]{1,0:T(8,128)S(1)}, f32[8,128]{1,0:T(8,128)S(1)}, u32[]{:S(2)}, u32[]{:S(2)}) collective-permute-start(f32[8,128]{1,0:T(8,128)S(1)} %pad.12), channel_id=1, source_target_pairs={{0,128},{64,192},{128,0},{192,64},{1,129},{65,193},{129,1},{193,65... | collective-permute-start | bytes 12296 | tf_op jit(solution)/shard_map/ppermute | solution.py:510
  21.7 2.8 %collective-permute-start.6 = (f32[8,128]{1,0:T(8,128)S(1)}, f32[8,128]{1,0:T(8,128)S(1)}, u32[]{:S(2)}, u32[]{:S(2)}) collective-permute-start(f32[8,128]{1,0:T(8,128)S(1)} %pad.12), channel_id=1, source_target_pairs={{0,64},{64,128},{128,192},{192,0},{1,65},{65,129},{129,193},{193,1... | collective-permute-start | bytes 12296 | tf_op jit(solution)/shard_map/ppermute | solution.py:510
  24.6 0.1 copy.15
  24.6 0.1 stack_reshape.3
  24.7 9.7 %shard_map.96 = (f32[384,128]{1,0:T(8,128)S(1)}, f32[384,128]{1,0:T(8,128)S(1)}, f32[384,128]{1,0:T(8,128)S(1)}, f32[384,128]{1,0:T(8,128)S(1)}, f32[4,5,256,128]{3,2,1,0:T(8,128)}) custom-call(s32[4]{0:T(128)S(1)} %pad_add_fusion.where, f32[8,3,32,512]{3,2,1,0:T(8,128)S(1)} %copy-done, f32[32,512]{1,0:T(8,128)S(1)} %copy-done.1, ...), custom_call_target="tpu_custom_call" | custom-call | flops 10000000 | bytes 32000000 | tf_op jit(solution)/shard_map/pallas_call | solution.py:41
  34.5 0.3 collective-permute-done.6
  34.7 1.5 %collective-permute-start.9 = (f32[384,128]{1,0:T(8,128)S(1)}, f32[384,128]{1,0:T(8,128)S(1)}, u32[]{:S(2)}, u32[]{:S(2)}) collective-permute-start(f32[384,128]{1,0:T(8,128)S(1)} %get-tuple-element.102), channel_id=1, source_target_pairs={{0,64},{64,128},{128,192},{192,0},{1,65},{65,129},{129,193},{193,1... | collective-permute-start | bytes 589832 | tf_op jit(solution)/shard_map/ppermute | solution.py:510
  36.3 2.0 %collective-permute-start.10 = (f32[384,128]{1,0:T(8,128)S(1)}, f32[384,128]{1,0:T(8,128)S(1)}, u32[]{:S(2)}, u32[]{:S(2)}) collective-permute-start(f32[384,128]{1,0:T(8,128)S(1)} %get-tuple-element.103), channel_id=1, source_target_pairs={{0,128},{64,192},{128,0},{192,64},{1,129},{65,193},{129,1},{193,65... | collective-permute-start | bytes 589832 | tf_op jit(solution)/shard_map/ppermute | solution.py:510
  38.3 0.9 collective-permute-start.11
  39.2 20.8 %conditional.2 = (f32[384,128]{1,0:T(8,128)S(1)}, f32[384,128]{1,0:T(8,128)S(1)}, f32[384,128]{1,0:T(8,128)S(1)}, f32[384,128]{1,0:T(8,128)S(1)}, f32[3,4,128,12...) conditional(s32[]{:T(128)} %convert_element_type.42, () %tuple.27, (s32[]{:T(128)}, f32[4,120,128]{2,1,0:T(8,128)S(1)}, ...), branch_computations={%region_0.1_spmd, %region_1.2_spmd} | conditional | flops 30722 | bytes 1769544 | solution.py:569
  39.2 0.1 collective-permute-start.2
  39.3 1.3 %collective-permute-done.2.corner = f32[2,120,128]{2,1,0:T(8,128)S(1)} collective-permute-done((f32[2,120,128]{2,1,0:T(8,128)S(1)}, f32[2,120,128]{2,1,0:T(8,128)S(1)}, u32[]{:S(2)}, u32[]{:S(2)}) %collective-permute-start.2) | collective-permute-done | bytes 122912 | tf_op jit(solution)/shard_map/cond/branch_1_fun/ppermute | solution.py:556
  40.6 2.9 %branch_1_fun.3 = (f32[384,128]{1,0:T(8,128)S(1)}, f32[384,128]{1,0:T(8,128)S(1)}, f32[384,128]{1,0:T(8,128)S(1)}, f32[384,128]{1,0:T(8,128)S(1)}, f32[96,4,128]...) custom-call(s32[4]{0:T(128)S(1)} %get-tuple-element.24.where, f32[4,5,256,128]{3,2,1,0:T(8,128)} %get-tuple-element.28.inner, ...), custom_call_target="tpu_custom_call" | custom-call | tf_op jit(solution)/shard_map/cond/branch_1_fun/pallas_call | solution.py:41
  43.5 16.4 %all_to_all.4 = f32[96,4,128]{2,1,0:T(4,128)S(1)} all-to-all(f32[96,4,128]{2,1,0:T(4,128)S(1)} %get-tuple-element.42), channel_id=1, replica_groups=mesh['grp'=4,'reg'=8,'sub'=4,'cores'=2] {'grp','sub','cores'}, dimensions={0} | all-to-all | bytes 393216 | tf_op jit(solution)/shard_map/cond/branch_1_fun/all_to_all | solution.py:560
  60.0 1.5 %collective-permute-start.12 = (f32[384,128]{1,0:T(8,128)S(1)}, f32[384,128]{1,0:T(8,128)S(1)}, u32[]{:S(2)}, u32[]{:S(2)}) collective-permute-start(f32[384,128]{1,0:T(8,128)S(1)} %get-tuple-element.107), channel_id=1, source_target_pairs={{0,64},{64,128},{128,192},{192,0},{1,65},{65,129},{129,193},{193,1... | collective-permute-start | bytes 589832 | tf_op jit(solution)/shard_map/ppermute | solution.py:510
  61.5 2.2 %collective-permute-start.13 = (f32[384,128]{1,0:T(8,128)S(1)}, f32[384,128]{1,0:T(8,128)S(1)}, u32[]{:S(2)}, u32[]{:S(2)}) collective-permute-start(f32[384,128]{1,0:T(8,128)S(1)} %get-tuple-element.108), channel_id=1, source_target_pairs={{0,128},{64,192},{128,0},{192,64},{1,129},{65,193},{129,1},{193,65... | collective-permute-start | bytes 589832 | tf_op jit(solution)/shard_map/ppermute | solution.py:510
  63.6 1.7 %collective-permute-start.14 = (f32[384,128]{1,0:T(8,128)S(1)}, f32[384,128]{1,0:T(8,128)S(1)}, u32[]{:S(2)}, u32[]{:S(2)}) collective-permute-start(f32[384,128]{1,0:T(8,128)S(1)} %get-tuple-element.109), channel_id=1, source_target_pairs={{0,192},{64,0},{128,64},{192,128},{1,193},{65,1},{129,65},{193,129... | collective-permute-start | bytes 589832 | tf_op jit(solution)/shard_map/ppermute | solution.py:510
  65.3 13.4 %conditional.3 = (f32[32,32]{1,0:T(8,128)S(1)}) conditional(s32[]{:T(128)} %convert_element_type.42, () %tuple.30, (s32[4]{0:T(128)S(1)}, f32[96,4,128]{2,1,0:T(4,128)S(1)}) %tuple.33), branch_computations={%region_2.3_spmd, %region_3.4_spmd} | conditional | bytes 65624 | solution.py:586
  65.3 1.2 %branch_1_fun.4 = (f32[32,64]{1,0:T(8,128)S(1)}, f32[32,64]{1,0:T(8,128)S(1)}) custom-call(s32[4]{0:T(128)S(1)} %get-tuple-element.43.where, f32[96,4,128]{2,1,0:T(4,128)S(1)} %get-tuple-element.44.states), custom_call_target="tpu_custom_call" | custom-call | tf_op jit(solution)/shard_map/cond/branch_1_fun/pallas_call | solution.py:41
  66.6 4.0 %collective-permute-start = (f32[32,64]{1,0:T(8,128)S(1)}, f32[32,64]{1,0:T(8,128)S(1)}, u32[]{:S(2)}, u32[]{:S(2)}) collective-permute-start(f32[32,64]{1,0:T(8,128)S(1)} %get-tuple-element.46), channel_id=1, source_target_pairs={{0,12},{2,14},{4,8},{6,10},{8,20},{10,22},{12,16},{14,18},{16,28},... | collective-permute-start | bytes 24584 | tf_op jit(solution)/shard_map/cond/branch_1_fun/ppermute | solution.py:579
  70.5 3.8 %collective-permute-done.low = f32[32,64]{1,0:T(8,128)S(1)} collective-permute-done((f32[32,64]{1,0:T(8,128)S(1)}, f32[32,64]{1,0:T(8,128)S(1)}, u32[]{:S(2)}, u32[]{:S(2)}) %collective-permute-start) | collective-permute-done | bytes 8224 | tf_op jit(solution)/shard_map/cond/branch_1_fun/ppermute | solution.py:579
  74.3 1.2 collective-permute-done.1.high
  75.5 3.2 %branch_1_fun.5 = f32[32,32]{1,0:T(8,128)S(1)} custom-call(s32[4]{0:T(128)S(1)} %get-tuple-element.43.where, f32[32,64]{1,0:T(8,128)S(1)} %get-tuple-element.45.own, f32[32,64]{1,0:T(8,128)S(1)} %collective-permute-done.low, f32[32,64]{1,0:T(8,128)S(1)} %collective-permute-done.1.high), custom_call_target="tpu_custom_call" | custom-call | tf_op jit(solution)/shard_map/cond/branch_1_fun/pallas_call | solution.py:41
  78.7 1.0 shard_map.99
  79.7 0.4 collective-permute-start.18
  80.1 2.5 %collective-permute-start.19 = (f32[384,128]{1,0:T(8,128)S(1)}, f32[384,128]{1,0:T(8,128)S(1)}, u32[]{:S(2)}, u32[]{:S(2)}) collective-permute-start(f32[384,128]{1,0:T(8,128)S(1)} %get-tuple-element.117), channel_id=1, source_target_pairs={{0,128},{64,192},{128,0},{192,64},{1,129},{65,193},{129,1},{193,65... | collective-permute-start | bytes 589832 | tf_op jit(solution)/shard_map/ppermute | solution.py:510
  82.7 1.0 shard_map.98
  83.7 2.1 %collective-permute-start.15 = (f32[384,128]{1,0:T(8,128)S(1)}, f32[384,128]{1,0:T(8,128)S(1)}, u32[]{:S(2)}, u32[]{:S(2)}) collective-permute-start(f32[384,128]{1,0:T(8,128)S(1)} %get-tuple-element.111), channel_id=1, source_target_pairs={{0,64},{64,128},{128,192},{192,0},{1,65},{65,129},{129,193},{193,1... | collective-permute-start | bytes 589832 | tf_op jit(solution)/shard_map/ppermute | solution.py:510
  85.8 2.2 %collective-permute-start.16 = (f32[384,128]{1,0:T(8,128)S(1)}, f32[384,128]{1,0:T(8,128)S(1)}, u32[]{:S(2)}, u32[]{:S(2)}) collective-permute-start(f32[384,128]{1,0:T(8,128)S(1)} %get-tuple-element.112), channel_id=1, source_target_pairs={{0,128},{64,192},{128,0},{192,64},{1,129},{65,193},{129,1},{193,65... | collective-permute-start | bytes 589832 | tf_op jit(solution)/shard_map/ppermute | solution.py:510
  87.9 2.1 %collective-permute-start.17 = (f32[384,128]{1,0:T(8,128)S(1)}, f32[384,128]{1,0:T(8,128)S(1)}, u32[]{:S(2)}, u32[]{:S(2)}) collective-permute-start(f32[384,128]{1,0:T(8,128)S(1)} %get-tuple-element.113), channel_id=1, source_target_pairs={{0,192},{64,0},{128,64},{192,128},{1,193},{65,1},{129,65},{193,129... | collective-permute-start | bytes 589832 | tf_op jit(solution)/shard_map/ppermute | solution.py:510
  90.0 3.2 %shard_map.97 = f32[8,3,32,512]{3,2,1,0:T(8,128)} custom-call(s32[4]{0:T(128)S(1)} %pad_add_fusion.where, f32[4,5,256,128]{3,2,1,0:T(8,128)} %get-tuple-element.86.inner, f32[3,4,128,128]{3,2,1,0:T(8,128)S(1)} %get-tuple-element.92.outer), custom_call_target="tpu_custom_call" | custom-call | tf_op jit(solution)/shard_map/pallas_call | solution.py:41
  93.2 4.8 %collective-permute-done.19.refs_2_ = f32[384,128]{1,0:T(8,128)S(1)} collective-permute-done((f32[384,128]{1,0:T(8,128)S(1)}, f32[384,128]{1,0:T(8,128)S(1)}, u32[]{:S(2)}, u32[]{:S(2)}) %collective-permute-start.19) | collective-permute-done | bytes 196640 | tf_op jit(solution)/shard_map/ppermute | solution.py:510
  98.0 10.9 %collective-permute-done.20.refs_3_ = f32[384,128]{1,0:T(8,128)S(1)} collective-permute-done((f32[384,128]{1,0:T(8,128)S(1)}, f32[384,128]{1,0:T(8,128)S(1)}, u32[]{:S(2)}, u32[]{:S(2)}) %collective-permute-start.20) | collective-permute-done | bytes 196640 | tf_op jit(solution)/shard_map/ppermute | solution.py:510
  108.9 1.8 %shard_map.100.refs_4_ = f32[8,3,32,512]{3,2,1,0:T(8,128)} custom-call(s32[4]{0:T(128)S(1)} %pad_add_fusion.where, f32[384,128]{1,0:T(8,128)S(1)} %get-tuple-element.115.refs_0_, f32[384,128]{1,0:T(8,128)S(1)} %collective-permute-done.18.refs_1_, f32[384,128]{1,0:T(8,128)S(1)} %collective-permute-done.19.refs_2_, f32[384,128]{1,0:T(8,128)S(1)} %collective-permute-done.20.refs_3_), custom_call_target="tpu_custom_call" | custom-call | flops 10000000 | bytes 32000000 | tf_op jit(solution)/shard_map/pallas_call | solution.py:41
  110.7 3.4 %collective-permute-done.16.refs_2_ = f32[384,128]{1,0:T(8,128)S(1)} collective-permute-done((f32[384,128]{1,0:T(8,128)S(1)}, f32[384,128]{1,0:T(8,128)S(1)}, u32[]{:S(2)}, u32[]{:S(2)}) %collective-permute-start.16) | collective-permute-done | bytes 196640 | tf_op jit(solution)/shard_map/ppermute | solution.py:510
  114.1 3.1 %collective-permute-done.17.refs_3_ = f32[384,128]{1,0:T(8,128)S(1)} collective-permute-done((f32[384,128]{1,0:T(8,128)S(1)}, f32[384,128]{1,0:T(8,128)S(1)}, u32[]{:S(2)}, u32[]{:S(2)}) %collective-permute-start.17) | collective-permute-done | bytes 196640 | tf_op jit(solution)/shard_map/ppermute | solution.py:510
  117.2 1.5 %shard_map.101 = f32[8,3,32,512]{3,2,1,0:T(8,128)} custom-call(s32[4]{0:T(128)S(1)} %pad_add_fusion.where, f32[384,128]{1,0:T(8,128)S(1)} %get-tuple-element.110.refs_0_, f32[384,128]{1,0:T(8,128)S(1)} %collective-permute-done.15.refs_1_, f32[384,128]{1,0:T(8,128)S(1)} %collective-permute-done.16.refs_2_, ...), custom_call_target="tpu_custom_call", output_to_operand_aliasing={{}: (5, {})} | custom-call | tf_op jit(solution)/shard_map/pallas_call | solution.py:381
  (46 shorter events, 0.2 us)
Async XLA Ops:
  0.6 24.1 %copy-start.1 = (f32[32,512]{1,0:T(8,128)S(1)}, f32[32,512]{1,0:T(8,128)}, u32[]{:S(2)}) copy-start(f32[32,512]{1,0:T(8,128)} %seabed.3) | copy-start | bytes 196612
  0.6 24.1 %copy-start = (f32[8,3,32,512]{3,2,1,0:T(8,128)S(1)}, f32[8,3,32,512]{3,2,1,0:T(8,128)}, u32[]{:S(2)}) copy-start(f32[8,3,32,512]{3,2,1,0:T(8,128)} %trial.3) | copy-start | bytes 4718596
  0.7 15.8 %copy-start.7 = (s32[16,4]{0,1:T(4,128)S(1)}, s32[16,4]{0,1:T(4,128)}, u32[]{:S(2)}) copy-start(s32[16,4]{0,1:T(4,128)} %param.17) | copy-start | bytes 772
  0.7 15.8 %copy-start.6 = (f32[16]{0:T(128)S(1)}, f32[16]{0:T(128)}, u32[]{:S(2)}) copy-start(f32[16]{0:T(128)} %param.15) | copy-start | bytes 196
  0.7 16.0 %copy-start.3 = (s32[16,8]{0,1:T(8,128)S(1)}, s32[16,8]{0,1:T(8,128)}, u32[]{:S(2)}) copy-start(s32[16,8]{0,1:T(8,128)} %param.19) | copy-start | bytes 1540
  0.7 16.0 %copy-start.4 = (f32[16,4]{0,1:T(4,128)S(1)}, f32[16,4]{0,1:T(4,128)}, u32[]{:S(2)}) copy-start(f32[16,4]{0,1:T(4,128)} %param.18) | copy-start | bytes 772
  0.7 16.1 %copy-start.2 = (f32[16,32]{1,0:T(8,128)S(1)}, f32[16,32]{1,0:T(8,128)}, u32[]{:S(2)}) copy-start(f32[16,32]{1,0:T(8,128)} %param.16) | copy-start | bytes 6148
  0.7 16.1 %copy-start.5 = (f32[16]{0:T(128)S(1)}, f32[16]{0:T(128)}, u32[]{:S(2)}) copy-start(f32[16]{0:T(128)} %param.14) | copy-start | bytes 196
  3.5 35.7 %collective-permute-start.4 = (f32[4,120,128]{2,1,0:T(8,128)}, f32[4,120,128]{2,1,0:T(8,128)S(1)}, u32[]{:S(2)}, u32[]{:S(2)}) collective-permute-start(f32[4,120,128]{2,1,0:T(8,128)} %get-tuple-element.87), channel_id=1, source_target_pairs={{0,2},{2,4},{4,6},{6,8},{8,10},{10,12},{12,14},{14,16},{16,18},{18... | collective-permute-start | bytes 737288 | tf_op jit(solution)/shard_map/ppermute | solution.py:528
  11.7 27.5 %collective-permute-start.5 = (f32[4,120,128]{2,1,0:T(8,128)}, f32[4,120,128]{2,1,0:T(8,128)S(1)}, u32[]{:S(2)}, u32[]{:S(2)}) collective-permute-start(f32[4,120,128]{2,1,0:T(8,128)} %get-tuple-element.88), channel_id=1, source_target_pairs={{2,0},{4,2},{6,4},{8,6},{10,8},{12,10},{14,12},{16,14},{18,16},{20... | collective-permute-start | bytes 737288 | tf_op jit(solution)/shard_map/ppermute | solution.py:529
  16.3 2.1 %collective-permute-start.3 = (f32[9,3,32,128]{3,2,1,0:T(8,128)}, f32[9,3,32,128]{3,2,1,0:T(8,128)S(1)}, u32[]{:S(2)}, u32[]{:S(2)}) collective-permute-start(f32[9,3,32,128]{3,2,1,0:T(8,128)} %get-tuple-element.84), channel_id=1, source_target_pairs={{0,1},{1,0},{2,3},{3,2},{4,5},{5,4},{6,7},{7,6},{8,9},{9,8},{10,11... | collective-permute-start | bytes 1327112 | tf_op jit(solution)/shard_map/ppermute | solution.py:530
  18.4 16.0 %collective-permute-start.8 = (f32[8,128]{1,0:T(8,128)S(1)}, f32[8,128]{1,0:T(8,128)S(1)}, u32[]{:S(2)}, u32[]{:S(2)}) collective-permute-start(f32[8,128]{1,0:T(8,128)S(1)} %pad.12), channel_id=1, source_target_pairs={{0,192},{64,0},{128,64},{192,128},{1,193},{65,1},{129,65},{193,129... | collective-permute-start | bytes 12296 | tf_op jit(solution)/shard_map/ppermute | solution.py:510
  19.4 15.0 %collective-permute-start.7 = (f32[8,128]{1,0:T(8,128)S(1)}, f32[8,128]{1,0:T(8,128)S(1)}, u32[]{:S(2)}, u32[]{:S(2)}) collective-permute-start(f32[8,128]{1,0:T(8,128)S(1)} %pad.12), channel_id=1, source_target_pairs={{0,128},{64,192},{128,0},{192,64},{1,129},{65,193},{129,1},{193,65... | collective-permute-start | bytes 12296 | tf_op jit(solution)/shard_map/ppermute | solution.py:510
  21.7 13.0 %collective-permute-start.6 = (f32[8,128]{1,0:T(8,128)S(1)}, f32[8,128]{1,0:T(8,128)S(1)}, u32[]{:S(2)}, u32[]{:S(2)}) collective-permute-start(f32[8,128]{1,0:T(8,128)S(1)} %pad.12), channel_id=1, source_target_pairs={{0,64},{64,128},{128,192},{192,0},{1,65},{65,129},{129,193},{193,1... | collective-permute-start | bytes 12296 | tf_op jit(solution)/shard_map/ppermute | solution.py:510
  34.7 25.2 %collective-permute-start.9 = (f32[384,128]{1,0:T(8,128)S(1)}, f32[384,128]{1,0:T(8,128)S(1)}, u32[]{:S(2)}, u32[]{:S(2)}) collective-permute-start(f32[384,128]{1,0:T(8,128)S(1)} %get-tuple-element.102), channel_id=1, source_target_pairs={{0,64},{64,128},{128,192},{192,0},{1,65},{65,129},{129,193},{193,1... | collective-permute-start | bytes 589832 | tf_op jit(solution)/shard_map/ppermute | solution.py:510
  36.3 23.7 %collective-permute-start.10 = (f32[384,128]{1,0:T(8,128)S(1)}, f32[384,128]{1,0:T(8,128)S(1)}, u32[]{:S(2)}, u32[]{:S(2)}) collective-permute-start(f32[384,128]{1,0:T(8,128)S(1)} %get-tuple-element.103), channel_id=1, source_target_pairs={{0,128},{64,192},{128,0},{192,64},{1,129},{65,193},{129,1},{193,65... | collective-permute-start | bytes 589832 | tf_op jit(solution)/shard_map/ppermute | solution.py:510
  38.3 21.7 %collective-permute-start.11 = (f32[384,128]{1,0:T(8,128)S(1)}, f32[384,128]{1,0:T(8,128)S(1)}, u32[]{:S(2)}, u32[]{:S(2)}) collective-permute-start(f32[384,128]{1,0:T(8,128)S(1)} %get-tuple-element.104), channel_id=1, source_target_pairs={{0,192},{64,0},{128,64},{192,128},{1,193},{65,1},{129,65},{193,129... | collective-permute-start | bytes 589832 | tf_op jit(solution)/shard_map/ppermute | solution.py:510
  39.2 1.4 %collective-permute-start.2 = (f32[2,120,128]{2,1,0:T(8,128)S(1)}, f32[2,120,128]{2,1,0:T(8,128)S(1)}, u32[]{:S(2)}, u32[]{:S(2)}) collective-permute-start(f32[2,120,128]{2,1,0:T(8,128)S(1)} %pad_maximum_fusion), channel_id=1, source_target_pairs={{0,1},{1,0},{2,3},{3,2},{4,5},{5,4},{6,7},{7,6},{8,9},{9,8},{10,11... | collective-permute-start | bytes 368648 | tf_op jit(solution)/shard_map/cond/branch_1_fun/ppermute | solution.py:556
  60.0 22.7 %collective-permute-start.12 = (f32[384,128]{1,0:T(8,128)S(1)}, f32[384,128]{1,0:T(8,128)S(1)}, u32[]{:S(2)}, u32[]{:S(2)}) collective-permute-start(f32[384,128]{1,0:T(8,128)S(1)} %get-tuple-element.107), channel_id=1, source_target_pairs={{0,64},{64,128},{128,192},{192,0},{1,65},{65,129},{129,193},{193,1... | collective-permute-start | bytes 589832 | tf_op jit(solution)/shard_map/ppermute | solution.py:510
  61.5 21.2 %collective-permute-start.13 = (f32[384,128]{1,0:T(8,128)S(1)}, f32[384,128]{1,0:T(8,128)S(1)}, u32[]{:S(2)}, u32[]{:S(2)}) collective-permute-start(f32[384,128]{1,0:T(8,128)S(1)} %get-tuple-element.108), channel_id=1, source_target_pairs={{0,128},{64,192},{128,0},{192,64},{1,129},{65,193},{129,1},{193,65... | collective-permute-start | bytes 589832 | tf_op jit(solution)/shard_map/ppermute | solution.py:510
  63.6 19.0 %collective-permute-start.14 = (f32[384,128]{1,0:T(8,128)S(1)}, f32[384,128]{1,0:T(8,128)S(1)}, u32[]{:S(2)}, u32[]{:S(2)}) collective-permute-start(f32[384,128]{1,0:T(8,128)S(1)} %get-tuple-element.109), channel_id=1, source_target_pairs={{0,192},{64,0},{128,64},{192,128},{1,193},{65,1},{129,65},{193,129... | collective-permute-start | bytes 589832 | tf_op jit(solution)/shard_map/ppermute | solution.py:510
  66.6 7.7 %collective-permute-start = (f32[32,64]{1,0:T(8,128)S(1)}, f32[32,64]{1,0:T(8,128)S(1)}, u32[]{:S(2)}, u32[]{:S(2)}) collective-permute-start(f32[32,64]{1,0:T(8,128)S(1)} %get-tuple-element.46), channel_id=1, source_target_pairs={{0,12},{2,14},{4,8},{6,10},{8,20},{10,22},{12,16},{14,18},{16,28},... | collective-permute-start | bytes 24584 | tf_op jit(solution)/shard_map/cond/branch_1_fun/ppermute | solution.py:579
  74.3 1.2 collective-permute-start.1
  79.7 8.2 %collective-permute-start.18 = (f32[384,128]{1,0:T(8,128)S(1)}, f32[384,128]{1,0:T(8,128)S(1)}, u32[]{:S(2)}, u32[]{:S(2)}) collective-permute-start(f32[384,128]{1,0:T(8,128)S(1)} %get-tuple-element.116), channel_id=1, source_target_pairs={{0,64},{64,128},{128,192},{192,0},{1,65},{65,129},{129,193},{193,1... | collective-permute-start | bytes 589832 | tf_op jit(solution)/shard_map/ppermute | solution.py:510
  80.1 17.8 %collective-permute-start.19 = (f32[384,128]{1,0:T(8,128)S(1)}, f32[384,128]{1,0:T(8,128)S(1)}, u32[]{:S(2)}, u32[]{:S(2)}) collective-permute-start(f32[384,128]{1,0:T(8,128)S(1)} %get-tuple-element.117), channel_id=1, source_target_pairs={{0,128},{64,192},{128,0},{192,64},{1,129},{65,193},{129,1},{193,65... | collective-permute-start | bytes 589832 | tf_op jit(solution)/shard_map/ppermute | solution.py:510
  82.7 26.2 %collective-permute-start.20 = (f32[384,128]{1,0:T(8,128)S(1)}, f32[384,128]{1,0:T(8,128)S(1)}, u32[]{:S(2)}, u32[]{:S(2)}) collective-permute-start(f32[384,128]{1,0:T(8,128)S(1)} %get-tuple-element.118), channel_id=1, source_target_pairs={{0,192},{64,0},{128,64},{192,128},{1,193},{65,1},{129,65},{193,129... | collective-permute-start | bytes 589832 | tf_op jit(solution)/shard_map/ppermute | solution.py:510
  83.7 27.0 %collective-permute-start.15 = (f32[384,128]{1,0:T(8,128)S(1)}, f32[384,128]{1,0:T(8,128)S(1)}, u32[]{:S(2)}, u32[]{:S(2)}) collective-permute-start(f32[384,128]{1,0:T(8,128)S(1)} %get-tuple-element.111), channel_id=1, source_target_pairs={{0,64},{64,128},{128,192},{192,0},{1,65},{65,129},{129,193},{193,1... | collective-permute-start | bytes 589832 | tf_op jit(solution)/shard_map/ppermute | solution.py:510
  85.8 28.4 %collective-permute-start.16 = (f32[384,128]{1,0:T(8,128)S(1)}, f32[384,128]{1,0:T(8,128)S(1)}, u32[]{:S(2)}, u32[]{:S(2)}) collective-permute-start(f32[384,128]{1,0:T(8,128)S(1)} %get-tuple-element.112), channel_id=1, source_target_pairs={{0,128},{64,192},{128,0},{192,64},{1,129},{65,193},{129,1},{193,65... | collective-permute-start | bytes 589832 | tf_op jit(solution)/shard_map/ppermute | solution.py:510
  87.9 29.3 %collective-permute-start.17 = (f32[384,128]{1,0:T(8,128)S(1)}, f32[384,128]{1,0:T(8,128)S(1)}, u32[]{:S(2)}, u32[]{:S(2)}) collective-permute-start(f32[384,128]{1,0:T(8,128)S(1)} %get-tuple-element.113), channel_id=1, source_target_pairs={{0,192},{64,0},{128,64},{192,128},{1,193},{65,1},{129,65},{193,129... | collective-permute-start | bytes 589832 | tf_op jit(solution)/shard_map/ppermute | solution.py:510

commit v7 on v6

--- a/solution.py
+++ b/solution.py
@@ -357,39 +357,46 @@
                 ]
 
 
-def unpack_outer_body(where, *refs):
-    blocks, (_, out, held, sems) = refs[:GRP], refs[GRP:]
-    copies = [
-        pltpu.make_async_copy(held.at[side], out.at[:, :, rows, :], sems.at[side])
-        for side, rows in enumerate((pl.ds(0, PAD), pl.ds(CX - PAD, PAD)))
-    ]
-    for side in range(2):
-        for other, block in enumerate(blocks):
-            at = pl.ds(aligned(down_from(where[0], other), LANE), LANE)
+def unpack_outer_body(some, where, *refs):
+    blocks, (_, out, held, sems) = refs[: len(some)], refs[len(some) :]
+    copies = []
+    for at, (other, block) in enumerate(zip(some, blocks)):
+        lanes = pl.ds(aligned(down_from(where[0], other), LANE), LANE)
+        for side, rows in enumerate((pl.ds(0, PAD), pl.ds(CX - PAD, PAD))):
             for field in range(3):
                 for member in range(MEM):
                     low = field * MIDDLE + side * HALF + member
-                    held[side, member, field, :, at] = block[pl.ds(low, PAD, stride=MEM), :]
-        copies[side].start()
+                    held[at, side, member, field] = block[pl.ds(low, PAD, stride=MEM), :]
+            copies.append(
+                pltpu.make_async_copy(
+                    held.at[at, side], out.at[:, :, rows, lanes], sems.at[2 * at + side]
+                )
+            )
+            copies[-1].start()
     for copy in copies:
         copy.wait()
+
+
+def unpack_outer(where, some, blocks, given):
+    return pl.pallas_call(
+        functools.partial(unpack_outer_body, some),
+        out_shape=shaped(MEM, 3, CX, CY),
+        in_specs=[SMEM] + [VMEM] * len(some) + [ANY],
+        out_specs=ANY,
+        scratch_shapes=[
+            pltpu.VMEM((len(some), 2, MEM, 3, PAD, LANE), F32),
+            pltpu.SemaphoreType.DMA((2 * len(some),)),
+        ],
+        input_output_aliases={1 + len(some): 0},
+        compiler_params=pltpu.CompilerParams(vmem_limit_bytes=16 * 1024 * 1024),
+    )(where, *[blocks[s] for s in some], given)
 
 
 def unpack(where, middle, outer):
     out = shaped(MEM, 3, CX, CY)
     early = call(unpack_middle_body, (out,), (where, *middle), flops=10_000_000, moved=32_000_000)
-    return pl.pallas_call(
-        unpack_outer_body,
-        out_shape=out,
-        in_specs=[SMEM] + [VMEM] * GRP + [ANY],
-        out_specs=ANY,
-        scratch_shapes=[
-            pltpu.VMEM((2, MEM, 3, PAD, CY), F32),
-            pltpu.SemaphoreType.DMA((2,)),
-        ],
-        input_output_aliases={1 + GRP: 0},
-        compiler_params=pltpu.CompilerParams(vmem_limit_bytes=16 * 1024 * 1024),
-    )(where, *outer, early[0])
+    early = unpack_outer(where, (0, 1), outer, early[0])
+    return unpack_outer(where, (2, 3), outer, early)
 
 
 def spread_out_body(where, inner, outer, out):

time: 119 us -> 119 us (level)
  waiting for transfers between devices: 30.3 us -> 28.9 us
  Pallas kernels: 28.2 us -> 29.4 us
    ppermute x15, waiting for transfers between devices: 22.5 us -> 21.2 us  [exchange(): lax.ppermute(blocks[s], 'grp', [(i, (i + s) % GRP) for i in range(GRP)])]
    pallas_call x1 -> x2, Pallas kernels: 1.51 us -> 2.67 us  [unpack_outer(): pl.pallas_call(functools.partial(unpack_outer_body, some), out_shape=shap...]
  transfers between devices with their start and end apart: 21 -> 21, of which waited for: 9 -> 9; matrix products, arithmetic and copies ran while one was open for 1% -> 1% of each run, Pallas kernels for 20% -> 21%
where the time goes in v7:
time: 119 us
  starting transfers between devices  42.1 us (35%)
  Pallas kernels  29.4 us (25%)
  waiting for transfers between devices  28.9 us (24%)
  blocking collectives  16.4 us (14%)
    ppermute x15, starting transfers between devices, exchange(): lax.ppermute(blocks[s], 'grp', [(i, (i + s) % GRP) for i in range(GRP)])  25.1 us
    pallas_call x8, Pallas kernels, call(): pl.pallas_call(body, out_shape=list(outs), in_specs=[SMEM] + [VMEM] * (le...  24 us
    ppermute x15, waiting for transfers between devices, exchange(): lax.ppermute(blocks[s], 'grp', [(i, (i + s) % GRP) for i in range(GRP)])  21.2 us
    all_to_all x1, blocking collectives, outer_rows(): return (outer, rest, lax.all_to_all(state, SIDE, 0, 0, tiled=True))  16.4 us
    ppermute x1, starting transfers between devices, on_device(): above = lax.ppermute(down, TILE, forward)  8.2 us
    ppermute x1, starting transfers between devices, on_device(): below = lax.ppermute(up, TILE, backward)  4.64 us
    ppermute x1, starting transfers between devices, chain(): came = lax.ppermute(send, ('reg', 'sub', 'cores'), pairs)  3.95 us
    ppermute x1, waiting for transfers between devices, chain(): came = lax.ppermute(send, ('reg', 'sub', 'cores'), pairs)  3.78 us
  transfers between devices with their start and end apart: 21, of which 9 were waited for; matrix products, arithmetic and copies ran while one was open for 1% of the time, Pallas kernels for 21%

profile of v7, /device:TPU:38, one launch (start us, length us, event | category | flops | bytes accessed | tf_op | source)
XLA Modules:
  0.0 118.7 jit_solution(12174542857866262130)
XLA Ops:
  0.7 0.1 pad_add_fusion.where
  0.8 2.7 %shard_map.95 = (f32[4,120,128]{2,1,0:T(8,128)}, f32[4,120,128]{2,1,0:T(8,128)}, f32[9,3,32,128]{3,2,1,0:T(8,128)}) custom-call(s32[4]{0:T(128)S(1)} %pad_add_fusion.where, f32[8,3,32,512]{3,2,1,0:T(8,128)} %trial.3, f32[32,512]{1,0:T(8,128)} %seabed.3), custom_call_target="tpu_custom_call" | custom-call | tf_op jit(solution)/shard_map/pallas_call | solution.py:126
  3.5 8.2 %collective-permute-start.4 = (f32[4,120,128]{2,1,0:T(8,128)}, f32[4,120,128]{2,1,0:T(8,128)S(1)}, u32[]{:S(2)}, u32[]{:S(2)}) collective-permute-start(f32[4,120,128]{2,1,0:T(8,128)} %get-tuple-element.87), channel_id=1, source_target_pairs={{0,2},{2,4},{4,6},{6,8},{8,10},{10,12},{12,14},{14,16},{16,18},{18... | collective-permute-start | bytes 737288 | tf_op jit(solution)/shard_map/ppermute | solution.py:535
  11.7 4.6 %collective-permute-start.5 = (f32[4,120,128]{2,1,0:T(8,128)}, f32[4,120,128]{2,1,0:T(8,128)S(1)}, u32[]{:S(2)}, u32[]{:S(2)}) collective-permute-start(f32[4,120,128]{2,1,0:T(8,128)} %get-tuple-element.88), channel_id=1, source_target_pairs={{2,0},{4,2},{6,4},{8,6},{10,8},{12,10},{14,12},{16,14},{18,16},{20... | collective-permute-start | bytes 737288 | tf_op jit(solution)/shard_map/ppermute | solution.py:536
  16.3 0.1 collective-permute-start.3
  16.6 0.1 mul.35
  16.7 0.1 mul.33
  16.8 0.1 add_bitcast_fusion
  16.9 1.5 %collective-permute-done.3.beside = f32[9,3,32,128]{3,2,1,0:T(8,128)S(1)} collective-permute-done((f32[9,3,32,128]{3,2,1,0:T(8,128)}, f32[9,3,32,128]{3,2,1,0:T(8,128)S(1)}, u32[]{:S(2)}, u32[]{:S(2)}) %collective-permute-start.3) | collective-permute-done | bytes 442400 | tf_op jit(solution)/shard_map/ppermute | solution.py:537
  18.4 1.0 collective-permute-start.8
  19.4 2.3 %collective-permute-start.7 = (f32[8,128]{1,0:T(8,128)S(1)}, f32[8,128]{1,0:T(8,128)S(1)}, u32[]{:S(2)}, u32[]{:S(2)}) collective-permute-start(f32[8,128]{1,0:T(8,128)S(1)} %pad.12), channel_id=1, source_target_pairs={{0,128},{64,192},{128,0},{192,64},{1,129},{65,193},{129,1},{193,65... | collective-permute-start | bytes 12296 | tf_op jit(solution)/shard_map/ppermute | solution.py:517
  21.7 2.8 %collective-permute-start.6 = (f32[8,128]{1,0:T(8,128)S(1)}, f32[8,128]{1,0:T(8,128)S(1)}, u32[]{:S(2)}, u32[]{:S(2)}) collective-permute-start(f32[8,128]{1,0:T(8,128)S(1)} %pad.12), channel_id=1, source_target_pairs={{0,64},{64,128},{128,192},{192,0},{1,65},{65,129},{129,193},{193,1... | collective-permute-start | bytes 12296 | tf_op jit(solution)/shard_map/ppermute | solution.py:517
  24.6 0.1 copy.16
  24.6 0.1 stack_reshape.3
  24.7 9.7 %shard_map.96 = (f32[384,128]{1,0:T(8,128)S(1)}, f32[384,128]{1,0:T(8,128)S(1)}, f32[384,128]{1,0:T(8,128)S(1)}, f32[384,128]{1,0:T(8,128)S(1)}, f32[4,5,256,128]{3,2,1,0:T(8,128)}) custom-call(s32[4]{0:T(128)S(1)} %pad_add_fusion.where, f32[8,3,32,512]{3,2,1,0:T(8,128)S(1)} %copy-done, f32[32,512]{1,0:T(8,128)S(1)} %copy-done.1, ...), custom_call_target="tpu_custom_call" | custom-call | flops 10000000 | bytes 32000000 | tf_op jit(solution)/shard_map/pallas_call | solution.py:41
  34.5 0.3 collective-permute-done.6
  34.7 1.5 %collective-permute-start.9 = (f32[384,128]{1,0:T(8,128)S(1)}, f32[384,128]{1,0:T(8,128)S(1)}, u32[]{:S(2)}, u32[]{:S(2)}) collective-permute-start(f32[384,128]{1,0:T(8,128)S(1)} %get-tuple-element.102), channel_id=1, source_target_pairs={{0,64},{64,128},{128,192},{192,0},{1,65},{65,129},{129,193},{193,1... | collective-permute-start | bytes 589832 | tf_op jit(solution)/shard_map/ppermute | solution.py:517
  36.3 2.0 %collective-permute-start.10 = (f32[384,128]{1,0:T(8,128)S(1)}, f32[384,128]{1,0:T(8,128)S(1)}, u32[]{:S(2)}, u32[]{:S(2)}) collective-permute-start(f32[384,128]{1,0:T(8,128)S(1)} %get-tuple-element.103), channel_id=1, source_target_pairs={{0,128},{64,192},{128,0},{192,64},{1,129},{65,193},{129,1},{193,65... | collective-permute-start | bytes 589832 | tf_op jit(solution)/shard_map/ppermute | solution.py:517
  38.3 0.9 collective-permute-start.11
  39.2 20.8 %conditional.2 = (f32[384,128]{1,0:T(8,128)S(1)}, f32[384,128]{1,0:T(8,128)S(1)}, f32[384,128]{1,0:T(8,128)S(1)}, f32[384,128]{1,0:T(8,128)S(1)}, f32[3,4,128,12...) conditional(s32[]{:T(128)} %convert_element_type.42, () %tuple.27, (s32[]{:T(128)}, f32[4,120,128]{2,1,0:T(8,128)S(1)}, ...), branch_computations={%region_0.1_spmd, %region_1.2_spmd} | conditional | flops 30722 | bytes 1769544 | solution.py:576
  39.2 0.1 collective-permute-start.2
  39.3 1.3 %collective-permute-done.2.corner = f32[2,120,128]{2,1,0:T(8,128)S(1)} collective-permute-done((f32[2,120,128]{2,1,0:T(8,128)S(1)}, f32[2,120,128]{2,1,0:T(8,128)S(1)}, u32[]{:S(2)}, u32[]{:S(2)}) %collective-permute-start.2) | collective-permute-done | bytes 122912 | tf_op jit(solution)/shard_map/cond/branch_1_fun/ppermute | solution.py:563
  40.6 2.9 %branch_1_fun.3 = (f32[384,128]{1,0:T(8,128)S(1)}, f32[384,128]{1,0:T(8,128)S(1)}, f32[384,128]{1,0:T(8,128)S(1)}, f32[384,128]{1,0:T(8,128)S(1)}, f32[96,4,128]...) custom-call(s32[4]{0:T(128)S(1)} %get-tuple-element.24.where, f32[4,5,256,128]{3,2,1,0:T(8,128)} %get-tuple-element.28.inner, ...), custom_call_target="tpu_custom_call" | custom-call | tf_op jit(solution)/shard_map/cond/branch_1_fun/pallas_call | solution.py:41
  43.5 16.4 %all_to_all.4 = f32[96,4,128]{2,1,0:T(4,128)S(1)} all-to-all(f32[96,4,128]{2,1,0:T(4,128)S(1)} %get-tuple-element.42), channel_id=1, replica_groups=mesh['grp'=4,'reg'=8,'sub'=4,'cores'=2] {'grp','sub','cores'}, dimensions={0} | all-to-all | bytes 393216 | tf_op jit(solution)/shard_map/cond/branch_1_fun/all_to_all | solution.py:567
  60.0 1.5 %collective-permute-start.12 = (f32[384,128]{1,0:T(8,128)S(1)}, f32[384,128]{1,0:T(8,128)S(1)}, u32[]{:S(2)}, u32[]{:S(2)}) collective-permute-start(f32[384,128]{1,0:T(8,128)S(1)} %get-tuple-element.107), channel_id=1, source_target_pairs={{0,64},{64,128},{128,192},{192,0},{1,65},{65,129},{129,193},{193,1... | collective-permute-start | bytes 589832 | tf_op jit(solution)/shard_map/ppermute | solution.py:517
  61.5 2.2 %collective-permute-start.13 = (f32[384,128]{1,0:T(8,128)S(1)}, f32[384,128]{1,0:T(8,128)S(1)}, u32[]{:S(2)}, u32[]{:S(2)}) collective-permute-start(f32[384,128]{1,0:T(8,128)S(1)} %get-tuple-element.108), channel_id=1, source_target_pairs={{0,128},{64,192},{128,0},{192,64},{1,129},{65,193},{129,1},{193,65... | collective-permute-start | bytes 589832 | tf_op jit(solution)/shard_map/ppermute | solution.py:517
  63.6 1.7 %collective-permute-start.14 = (f32[384,128]{1,0:T(8,128)S(1)}, f32[384,128]{1,0:T(8,128)S(1)}, u32[]{:S(2)}, u32[]{:S(2)}) collective-permute-start(f32[384,128]{1,0:T(8,128)S(1)} %get-tuple-element.109), channel_id=1, source_target_pairs={{0,192},{64,0},{128,64},{192,128},{1,193},{65,1},{129,65},{193,129... | collective-permute-start | bytes 589832 | tf_op jit(solution)/shard_map/ppermute | solution.py:517
  65.3 13.4 %conditional.3 = (f32[32,32]{1,0:T(8,128)S(1)}) conditional(s32[]{:T(128)} %convert_element_type.42, () %tuple.30, (s32[4]{0:T(128)S(1)}, f32[96,4,128]{2,1,0:T(4,128)S(1)}) %tuple.33), branch_computations={%region_2.3_spmd, %region_3.4_spmd} | conditional | bytes 65624 | solution.py:593
  65.3 1.2 %branch_1_fun.4 = (f32[32,64]{1,0:T(8,128)S(1)}, f32[32,64]{1,0:T(8,128)S(1)}) custom-call(s32[4]{0:T(128)S(1)} %get-tuple-element.43.where, f32[96,4,128]{2,1,0:T(4,128)S(1)} %get-tuple-element.44.states), custom_call_target="tpu_custom_call" | custom-call | tf_op jit(solution)/shard_map/cond/branch_1_fun/pallas_call | solution.py:41
  66.6 4.0 %collective-permute-start = (f32[32,64]{1,0:T(8,128)S(1)}, f32[32,64]{1,0:T(8,128)S(1)}, u32[]{:S(2)}, u32[]{:S(2)}) collective-permute-start(f32[32,64]{1,0:T(8,128)S(1)} %get-tuple-element.46), channel_id=1, source_target_pairs={{0,12},{2,14},{4,8},{6,10},{8,20},{10,22},{12,16},{14,18},{16,28},... | collective-permute-start | bytes 24584 | tf_op jit(solution)/shard_map/cond/branch_1_fun/ppermute | solution.py:586
  70.5 3.8 %collective-permute-done.low = f32[32,64]{1,0:T(8,128)S(1)} collective-permute-done((f32[32,64]{1,0:T(8,128)S(1)}, f32[32,64]{1,0:T(8,128)S(1)}, u32[]{:S(2)}, u32[]{:S(2)}) %collective-permute-start) | collective-permute-done | bytes 8224 | tf_op jit(solution)/shard_map/cond/branch_1_fun/ppermute | solution.py:586
  74.3 1.2 collective-permute-done.1.high
  75.5 3.2 %branch_1_fun.5 = f32[32,32]{1,0:T(8,128)S(1)} custom-call(s32[4]{0:T(128)S(1)} %get-tuple-element.43.where, f32[32,64]{1,0:T(8,128)S(1)} %get-tuple-element.45.own, f32[32,64]{1,0:T(8,128)S(1)} %collective-permute-done.low, f32[32,64]{1,0:T(8,128)S(1)} %collective-permute-done.1.high), custom_call_target="tpu_custom_call" | custom-call | tf_op jit(solution)/shard_map/cond/branch_1_fun/pallas_call | solution.py:41
  78.7 1.0 shard_map.99
  79.7 0.4 collective-permute-start.18
  80.1 2.5 %collective-permute-start.19 = (f32[384,128]{1,0:T(8,128)S(1)}, f32[384,128]{1,0:T(8,128)S(1)}, u32[]{:S(2)}, u32[]{:S(2)}) collective-permute-start(f32[384,128]{1,0:T(8,128)S(1)} %get-tuple-element.117), channel_id=1, source_target_pairs={{0,128},{64,192},{128,0},{192,64},{1,129},{65,193},{129,1},{193,65... | collective-permute-start | bytes 589832 | tf_op jit(solution)/shard_map/ppermute | solution.py:517
  82.7 1.0 shard_map.98
  83.7 2.1 %collective-permute-start.17 = (f32[384,128]{1,0:T(8,128)S(1)}, f32[384,128]{1,0:T(8,128)S(1)}, u32[]{:S(2)}, u32[]{:S(2)}) collective-permute-start(f32[384,128]{1,0:T(8,128)S(1)} %get-tuple-element.113), channel_id=1, source_target_pairs={{0,64},{64,128},{128,192},{192,0},{1,65},{65,129},{129,193},{193,1... | collective-permute-start | bytes 589832 | tf_op jit(solution)/shard_map/ppermute | solution.py:517
  85.8 2.2 %collective-permute-start.15 = (f32[384,128]{1,0:T(8,128)S(1)}, f32[384,128]{1,0:T(8,128)S(1)}, u32[]{:S(2)}, u32[]{:S(2)}) collective-permute-start(f32[384,128]{1,0:T(8,128)S(1)} %get-tuple-element.110), channel_id=1, source_target_pairs={{0,128},{64,192},{128,0},{192,64},{1,129},{65,193},{129,1},{193,65... | collective-permute-start | bytes 589832 | tf_op jit(solution)/shard_map/ppermute | solution.py:517
  87.9 2.1 %collective-permute-start.16 = (f32[384,128]{1,0:T(8,128)S(1)}, f32[384,128]{1,0:T(8,128)S(1)}, u32[]{:S(2)}, u32[]{:S(2)}) collective-permute-start(f32[384,128]{1,0:T(8,128)S(1)} %get-tuple-element.111), channel_id=1, source_target_pairs={{0,192},{64,0},{128,64},{192,128},{1,193},{65,1},{129,65},{193,129... | collective-permute-start | bytes 589832 | tf_op jit(solution)/shard_map/ppermute | solution.py:517
  90.0 3.2 %shard_map.97 = f32[8,3,32,512]{3,2,1,0:T(8,128)} custom-call(s32[4]{0:T(128)S(1)} %pad_add_fusion.where, f32[4,5,256,128]{3,2,1,0:T(8,128)} %get-tuple-element.86.inner, f32[3,4,128,128]{3,2,1,0:T(8,128)S(1)} %get-tuple-element.92.outer), custom_call_target="tpu_custom_call" | custom-call | tf_op jit(solution)/shard_map/pallas_call | solution.py:41
  93.2 4.8 %collective-permute-done.19.refs_2_ = f32[384,128]{1,0:T(8,128)S(1)} collective-permute-done((f32[384,128]{1,0:T(8,128)S(1)}, f32[384,128]{1,0:T(8,128)S(1)}, u32[]{:S(2)}, u32[]{:S(2)}) %collective-permute-start.19) | collective-permute-done | bytes 196640 | tf_op jit(solution)/shard_map/ppermute | solution.py:517
  98.0 10.9 %collective-permute-done.20.refs_3_ = f32[384,128]{1,0:T(8,128)S(1)} collective-permute-done((f32[384,128]{1,0:T(8,128)S(1)}, f32[384,128]{1,0:T(8,128)S(1)}, u32[]{:S(2)}, u32[]{:S(2)}) %collective-permute-start.20) | collective-permute-done | bytes 196640 | tf_op jit(solution)/shard_map/ppermute | solution.py:517
  108.9 1.8 %shard_map.100.refs_2_ = f32[8,3,32,512]{3,2,1,0:T(8,128)} custom-call(s32[4]{0:T(128)S(1)} %pad_add_fusion.where, f32[384,128]{1,0:T(8,128)S(1)} %get-tuple-element.115.refs_0_, f32[384,128]{1,0:T(8,128)S(1)} %collective-permute-done.18.refs_1_, f32[384,128]{1,0:T(8,128)S(1)} %collective-permute-done.19.refs_2_, f32[384,128]{1,0:T(8,128)S(1)} %collective-permute-done.20.refs_3_), custom_call_target="tpu_custom_call" | custom-call | flops 10000000 | bytes 32000000 | tf_op jit(solution)/shard_map/pallas_call | solution.py:41
  110.7 1.3 %shard_map.101.refs_2_ = f32[8,3,32,512]{3,2,1,0:T(8,128)} custom-call(s32[4]{0:T(128)S(1)} %pad_add_fusion.where, f32[384,128]{1,0:T(8,128)S(1)} %get-tuple-element.112.refs_0_, f32[384,128]{1,0:T(8,128)S(1)} %collective-permute-done.17.refs_1_, f32[8,3,32,512]{3,2,1,0:T(8,128)} %shard_map.100.refs_2_), custom_call_target="tpu_custom_call", output_to_operand_aliasing={{}: (3, {})} | custom-call | tf_op jit(solution)/shard_map/pallas_call | solution.py:381
  112.1 2.1 %collective-permute-done.15.refs_0_ = f32[384,128]{1,0:T(8,128)S(1)} collective-permute-done((f32[384,128]{1,0:T(8,128)S(1)}, f32[384,128]{1,0:T(8,128)S(1)}, u32[]{:S(2)}, u32[]{:S(2)}) %collective-permute-start.15) | collective-permute-done | bytes 196640 | tf_op jit(solution)/shard_map/ppermute | solution.py:517
  114.1 3.1 %collective-permute-done.16.refs_1_ = f32[384,128]{1,0:T(8,128)S(1)} collective-permute-done((f32[384,128]{1,0:T(8,128)S(1)}, f32[384,128]{1,0:T(8,128)S(1)}, u32[]{:S(2)}, u32[]{:S(2)}) %collective-permute-start.16) | collective-permute-done | bytes 196640 | tf_op jit(solution)/shard_map/ppermute | solution.py:517
  117.2 1.3 %shard_map.102 = f32[8,3,32,512]{3,2,1,0:T(8,128)} custom-call(s32[4]{0:T(128)S(1)} %pad_add_fusion.where, f32[384,128]{1,0:T(8,128)S(1)} %collective-permute-done.15.refs_0_, f32[384,128]{1,0:T(8,128)S(1)} %collective-permute-done.16.refs_1_, f32[8,3,32,512]{3,2,1,0:T(8,128)} %shard_map.101.refs_2_), custom_call_target="tpu_custom_call", output_to_operand_aliasing={{}: (3, {})} | custom-call | tf_op jit(solution)/shard_map/pallas_call | solution.py:381
  (47 shorter events, 0.3 us)
Async XLA Ops:
  0.6 24.1 %copy-start.1 = (f32[32,512]{1,0:T(8,128)S(1)}, f32[32,512]{1,0:T(8,128)}, u32[]{:S(2)}) copy-start(f32[32,512]{1,0:T(8,128)} %seabed.3) | copy-start | bytes 196612
  0.6 24.1 %copy-start = (f32[8,3,32,512]{3,2,1,0:T(8,128)S(1)}, f32[8,3,32,512]{3,2,1,0:T(8,128)}, u32[]{:S(2)}) copy-start(f32[8,3,32,512]{3,2,1,0:T(8,128)} %trial.3) | copy-start | bytes 4718596
  0.7 15.8 %copy-start.7 = (s32[16,4]{0,1:T(4,128)S(1)}, s32[16,4]{0,1:T(4,128)}, u32[]{:S(2)}) copy-start(s32[16,4]{0,1:T(4,128)} %param.17) | copy-start | bytes 772
  0.7 15.8 %copy-start.6 = (f32[16]{0:T(128)S(1)}, f32[16]{0:T(128)}, u32[]{:S(2)}) copy-start(f32[16]{0:T(128)} %param.15) | copy-start | bytes 196
  0.7 16.0 %copy-start.3 = (s32[16,8]{0,1:T(8,128)S(1)}, s32[16,8]{0,1:T(8,128)}, u32[]{:S(2)}) copy-start(s32[16,8]{0,1:T(8,128)} %param.19) | copy-start | bytes 1540
  0.7 16.0 %copy-start.4 = (f32[16,4]{0,1:T(4,128)S(1)}, f32[16,4]{0,1:T(4,128)}, u32[]{:S(2)}) copy-start(f32[16,4]{0,1:T(4,128)} %param.18) | copy-start | bytes 772
  0.7 16.1 %copy-start.2 = (f32[16,32]{1,0:T(8,128)S(1)}, f32[16,32]{1,0:T(8,128)}, u32[]{:S(2)}) copy-start(f32[16,32]{1,0:T(8,128)} %param.16) | copy-start | bytes 6148
  0.7 16.1 %copy-start.5 = (f32[16]{0:T(128)S(1)}, f32[16]{0:T(128)}, u32[]{:S(2)}) copy-start(f32[16]{0:T(128)} %param.14) | copy-start | bytes 196
  3.5 35.7 %collective-permute-start.4 = (f32[4,120,128]{2,1,0:T(8,128)}, f32[4,120,128]{2,1,0:T(8,128)S(1)}, u32[]{:S(2)}, u32[]{:S(2)}) collective-permute-start(f32[4,120,128]{2,1,0:T(8,128)} %get-tuple-element.87), channel_id=1, source_target_pairs={{0,2},{2,4},{4,6},{6,8},{8,10},{10,12},{12,14},{14,16},{16,18},{18... | collective-permute-start | bytes 737288 | tf_op jit(solution)/shard_map/ppermute | solution.py:535
  11.7 27.5 %collective-permute-start.5 = (f32[4,120,128]{2,1,0:T(8,128)}, f32[4,120,128]{2,1,0:T(8,128)S(1)}, u32[]{:S(2)}, u32[]{:S(2)}) collective-permute-start(f32[4,120,128]{2,1,0:T(8,128)} %get-tuple-element.88), channel_id=1, source_target_pairs={{2,0},{4,2},{6,4},{8,6},{10,8},{12,10},{14,12},{16,14},{18,16},{20... | collective-permute-start | bytes 737288 | tf_op jit(solution)/shard_map/ppermute | solution.py:536
  16.3 2.1 %collective-permute-start.3 = (f32[9,3,32,128]{3,2,1,0:T(8,128)}, f32[9,3,32,128]{3,2,1,0:T(8,128)S(1)}, u32[]{:S(2)}, u32[]{:S(2)}) collective-permute-start(f32[9,3,32,128]{3,2,1,0:T(8,128)} %get-tuple-element.84), channel_id=1, source_target_pairs={{0,1},{1,0},{2,3},{3,2},{4,5},{5,4},{6,7},{7,6},{8,9},{9,8},{10,11... | collective-permute-start | bytes 1327112 | tf_op jit(solution)/shard_map/ppermute | solution.py:537
  18.4 16.0 %collective-permute-start.8 = (f32[8,128]{1,0:T(8,128)S(1)}, f32[8,128]{1,0:T(8,128)S(1)}, u32[]{:S(2)}, u32[]{:S(2)}) collective-permute-start(f32[8,128]{1,0:T(8,128)S(1)} %pad.12), channel_id=1, source_target_pairs={{0,192},{64,0},{128,64},{192,128},{1,193},{65,1},{129,65},{193,129... | collective-permute-start | bytes 12296 | tf_op jit(solution)/shard_map/ppermute | solution.py:517
  19.4 15.0 %collective-permute-start.7 = (f32[8,128]{1,0:T(8,128)S(1)}, f32[8,128]{1,0:T(8,128)S(1)}, u32[]{:S(2)}, u32[]{:S(2)}) collective-permute-start(f32[8,128]{1,0:T(8,128)S(1)} %pad.12), channel_id=1, source_target_pairs={{0,128},{64,192},{128,0},{192,64},{1,129},{65,193},{129,1},{193,65... | collective-permute-start | bytes 12296 | tf_op jit(solution)/shard_map/ppermute | solution.py:517
  21.7 13.0 %collective-permute-start.6 = (f32[8,128]{1,0:T(8,128)S(1)}, f32[8,128]{1,0:T(8,128)S(1)}, u32[]{:S(2)}, u32[]{:S(2)}) collective-permute-start(f32[8,128]{1,0:T(8,128)S(1)} %pad.12), channel_id=1, source_target_pairs={{0,64},{64,128},{128,192},{192,0},{1,65},{65,129},{129,193},{193,1... | collective-permute-start | bytes 12296 | tf_op jit(solution)/shard_map/ppermute | solution.py:517
  34.7 25.2 %collective-permute-start.9 = (f32[384,128]{1,0:T(8,128)S(1)}, f32[384,128]{1,0:T(8,128)S(1)}, u32[]{:S(2)}, u32[]{:S(2)}) collective-permute-start(f32[384,128]{1,0:T(8,128)S(1)} %get-tuple-element.102), channel_id=1, source_target_pairs={{0,64},{64,128},{128,192},{192,0},{1,65},{65,129},{129,193},{193,1... | collective-permute-start | bytes 589832 | tf_op jit(solution)/shard_map/ppermute | solution.py:517
  36.3 23.7 %collective-permute-start.10 = (f32[384,128]{1,0:T(8,128)S(1)}, f32[384,128]{1,0:T(8,128)S(1)}, u32[]{:S(2)}, u32[]{:S(2)}) collective-permute-start(f32[384,128]{1,0:T(8,128)S(1)} %get-tuple-element.103), channel_id=1, source_target_pairs={{0,128},{64,192},{128,0},{192,64},{1,129},{65,193},{129,1},{193,65... | collective-permute-start | bytes 589832 | tf_op jit(solution)/shard_map/ppermute | solution.py:517
  38.3 21.7 %collective-permute-start.11 = (f32[384,128]{1,0:T(8,128)S(1)}, f32[384,128]{1,0:T(8,128)S(1)}, u32[]{:S(2)}, u32[]{:S(2)}) collective-permute-start(f32[384,128]{1,0:T(8,128)S(1)} %get-tuple-element.104), channel_id=1, source_target_pairs={{0,192},{64,0},{128,64},{192,128},{1,193},{65,1},{129,65},{193,129... | collective-permute-start | bytes 589832 | tf_op jit(solution)/shard_map/ppermute | solution.py:517
  39.2 1.4 %collective-permute-start.2 = (f32[2,120,128]{2,1,0:T(8,128)S(1)}, f32[2,120,128]{2,1,0:T(8,128)S(1)}, u32[]{:S(2)}, u32[]{:S(2)}) collective-permute-start(f32[2,120,128]{2,1,0:T(8,128)S(1)} %pad_maximum_fusion), channel_id=1, source_target_pairs={{0,1},{1,0},{2,3},{3,2},{4,5},{5,4},{6,7},{7,6},{8,9},{9,8},{10,11... | collective-permute-start | bytes 368648 | tf_op jit(solution)/shard_map/cond/branch_1_fun/ppermute | solution.py:563
  60.0 22.7 %collective-permute-start.12 = (f32[384,128]{1,0:T(8,128)S(1)}, f32[384,128]{1,0:T(8,128)S(1)}, u32[]{:S(2)}, u32[]{:S(2)}) collective-permute-start(f32[384,128]{1,0:T(8,128)S(1)} %get-tuple-element.107), channel_id=1, source_target_pairs={{0,64},{64,128},{128,192},{192,0},{1,65},{65,129},{129,193},{193,1... | collective-permute-start | bytes 589832 | tf_op jit(solution)/shard_map/ppermute | solution.py:517
  61.5 21.2 %collective-permute-start.13 = (f32[384,128]{1,0:T(8,128)S(1)}, f32[384,128]{1,0:T(8,128)S(1)}, u32[]{:S(2)}, u32[]{:S(2)}) collective-permute-start(f32[384,128]{1,0:T(8,128)S(1)} %get-tuple-element.108), channel_id=1, source_target_pairs={{0,128},{64,192},{128,0},{192,64},{1,129},{65,193},{129,1},{193,65... | collective-permute-start | bytes 589832 | tf_op jit(solution)/shard_map/ppermute | solution.py:517
  63.6 19.0 %collective-permute-start.14 = (f32[384,128]{1,0:T(8,128)S(1)}, f32[384,128]{1,0:T(8,128)S(1)}, u32[]{:S(2)}, u32[]{:S(2)}) collective-permute-start(f32[384,128]{1,0:T(8,128)S(1)} %get-tuple-element.109), channel_id=1, source_target_pairs={{0,192},{64,0},{128,64},{192,128},{1,193},{65,1},{129,65},{193,129... | collective-permute-start | bytes 589832 | tf_op jit(solution)/shard_map/ppermute | solution.py:517
  66.6 7.7 %collective-permute-start = (f32[32,64]{1,0:T(8,128)S(1)}, f32[32,64]{1,0:T(8,128)S(1)}, u32[]{:S(2)}, u32[]{:S(2)}) collective-permute-start(f32[32,64]{1,0:T(8,128)S(1)} %get-tuple-element.46), channel_id=1, source_target_pairs={{0,12},{2,14},{4,8},{6,10},{8,20},{10,22},{12,16},{14,18},{16,28},... | collective-permute-start | bytes 24584 | tf_op jit(solution)/shard_map/cond/branch_1_fun/ppermute | solution.py:586
  74.3 1.2 collective-permute-start.1
  79.7 8.2 %collective-permute-start.18 = (f32[384,128]{1,0:T(8,128)S(1)}, f32[384,128]{1,0:T(8,128)S(1)}, u32[]{:S(2)}, u32[]{:S(2)}) collective-permute-start(f32[384,128]{1,0:T(8,128)S(1)} %get-tuple-element.116), channel_id=1, source_target_pairs={{0,64},{64,128},{128,192},{192,0},{1,65},{65,129},{129,193},{193,1... | collective-permute-start | bytes 589832 | tf_op jit(solution)/shard_map/ppermute | solution.py:517
  80.1 17.8 %collective-permute-start.19 = (f32[384,128]{1,0:T(8,128)S(1)}, f32[384,128]{1,0:T(8,128)S(1)}, u32[]{:S(2)}, u32[]{:S(2)}) collective-permute-start(f32[384,128]{1,0:T(8,128)S(1)} %get-tuple-element.117), channel_id=1, source_target_pairs={{0,128},{64,192},{128,0},{192,64},{1,129},{65,193},{129,1},{193,65... | collective-permute-start | bytes 589832 | tf_op jit(solution)/shard_map/ppermute | solution.py:517
  82.7 26.2 %collective-permute-start.20 = (f32[384,128]{1,0:T(8,128)S(1)}, f32[384,128]{1,0:T(8,128)S(1)}, u32[]{:S(2)}, u32[]{:S(2)}) collective-permute-start(f32[384,128]{1,0:T(8,128)S(1)} %get-tuple-element.118), channel_id=1, source_target_pairs={{0,192},{64,0},{128,64},{192,128},{1,193},{65,1},{129,65},{193,129... | collective-permute-start | bytes 589832 | tf_op jit(solution)/shard_map/ppermute | solution.py:517
  83.7 27.0 %collective-permute-start.17 = (f32[384,128]{1,0:T(8,128)S(1)}, f32[384,128]{1,0:T(8,128)S(1)}, u32[]{:S(2)}, u32[]{:S(2)}) collective-permute-start(f32[384,128]{1,0:T(8,128)S(1)} %get-tuple-element.113), channel_id=1, source_target_pairs={{0,64},{64,128},{128,192},{192,0},{1,65},{65,129},{129,193},{193,1... | collective-permute-start | bytes 589832 | tf_op jit(solution)/shard_map/ppermute | solution.py:517
  85.8 28.4 %collective-permute-start.15 = (f32[384,128]{1,0:T(8,128)S(1)}, f32[384,128]{1,0:T(8,128)S(1)}, u32[]{:S(2)}, u32[]{:S(2)}) collective-permute-start(f32[384,128]{1,0:T(8,128)S(1)} %get-tuple-element.110), channel_id=1, source_target_pairs={{0,128},{64,192},{128,0},{192,64},{1,129},{65,193},{129,1},{193,65... | collective-permute-start | bytes 589832 | tf_op jit(solution)/shard_map/ppermute | solution.py:517
  87.9 29.3 %collective-permute-start.16 = (f32[384,128]{1,0:T(8,128)S(1)}, f32[384,128]{1,0:T(8,128)S(1)}, u32[]{:S(2)}, u32[]{:S(2)}) collective-permute-start(f32[384,128]{1,0:T(8,128)S(1)} %get-tuple-element.111), channel_id=1, source_target_pairs={{0,192},{64,0},{128,64},{192,128},{1,193},{65,1},{129,65},{193,129... | collective-permute-start | bytes 589832 | tf_op jit(solution)/shard_map/ppermute | solution.py:517

commit v8 on v7

--- a/solution.py
+++ b/solution.py
@@ -248,8 +248,10 @@
     left = levels - first.astype(F32)
     second = left.astype(BF16)
     third = (left - second.astype(F32)).astype(BF16)
-    dot = functools.partial(jnp.dot, preferred_element_type=F32)
-    picked = dot(first, pick) + dot(second, pick) + dot(third, pick)
+    parts = jnp.concatenate([first, second, third], axis=1)
+    picked = jnp.dot(
+        parts, jnp.concatenate([pick] * 3, axis=0), preferred_element_type=F32
+    )
     total = jnp.zeros((MEM, LANE), F32)
     for at in range(CX):
         here = jnp.where(row == at, stencils[1:2, :], 0.0)

time: 119 us -> 119 us (level)
  no operation moved by 1% of the time
where the time goes in v8:
time: 119 us
  starting transfers between devices  42.1 us (35%)
  Pallas kernels  29.4 us (25%)
  waiting for transfers between devices  28.9 us (24%)
  blocking collectives  16.4 us (14%)
    ppermute x15, starting transfers between devices, exchange(): lax.ppermute(blocks[s], 'grp', [(i, (i + s) % GRP) for i in range(GRP)])  25.1 us
    pallas_call x8, Pallas kernels, call(): pl.pallas_call(body, out_shape=list(outs), in_specs=[SMEM] + [VMEM] * (le...  24.1 us
    ppermute x15, waiting for transfers between devices, exchange(): lax.ppermute(blocks[s], 'grp', [(i, (i + s) % GRP) for i in range(GRP)])  21.2 us
    all_to_all x1, blocking collectives, outer_rows(): return (outer, rest, lax.all_to_all(state, SIDE, 0, 0, tiled=True))  16.4 us
    ppermute x1, starting transfers between devices, on_device(): above = lax.ppermute(down, TILE, forward)  8.2 us
    ppermute x1, starting transfers between devices, on_device(): below = lax.ppermute(up, TILE, backward)  4.64 us
    ppermute x1, starting transfers between devices, chain(): came = lax.ppermute(send, ('reg', 'sub', 'cores'), pairs)  3.95 us
    ppermute x1, waiting for transfers between devices, chain(): came = lax.ppermute(send, ('reg', 'sub', 'cores'), pairs)  3.78 us
  transfers between devices with their start and end apart: 21, of which 9 were waited for; matrix products, arithmetic and copies ran while one was open for 1% of the time, Pallas kernels for 21%

profile of v8, /device:TPU:38, one launch (start us, length us, event | category | flops | bytes accessed | tf_op | source)
XLA Modules:
  0.0 118.7 jit_solution(4451187210620856731)
XLA Ops:
  0.7 0.1 pad_add_fusion.where
  0.8 2.7 %shard_map.95 = (f32[4,120,128]{2,1,0:T(8,128)}, f32[4,120,128]{2,1,0:T(8,128)}, f32[9,3,32,128]{3,2,1,0:T(8,128)}) custom-call(s32[4]{0:T(128)S(1)} %pad_add_fusion.where, f32[8,3,32,512]{3,2,1,0:T(8,128)} %trial.3, f32[32,512]{1,0:T(8,128)} %seabed.3), custom_call_target="tpu_custom_call" | custom-call | tf_op jit(solution)/shard_map/pallas_call | solution.py:126
  3.5 8.2 %collective-permute-start.4 = (f32[4,120,128]{2,1,0:T(8,128)}, f32[4,120,128]{2,1,0:T(8,128)S(1)}, u32[]{:S(2)}, u32[]{:S(2)}) collective-permute-start(f32[4,120,128]{2,1,0:T(8,128)} %get-tuple-element.87), channel_id=1, source_target_pairs={{0,2},{2,4},{4,6},{6,8},{8,10},{10,12},{12,14},{14,16},{16,18},{18... | collective-permute-start | bytes 737288 | tf_op jit(solution)/shard_map/ppermute | solution.py:537
  11.7 4.6 %collective-permute-start.5 = (f32[4,120,128]{2,1,0:T(8,128)}, f32[4,120,128]{2,1,0:T(8,128)S(1)}, u32[]{:S(2)}, u32[]{:S(2)}) collective-permute-start(f32[4,120,128]{2,1,0:T(8,128)} %get-tuple-element.88), channel_id=1, source_target_pairs={{2,0},{4,2},{6,4},{8,6},{10,8},{12,10},{14,12},{16,14},{18,16},{20... | collective-permute-start | bytes 737288 | tf_op jit(solution)/shard_map/ppermute | solution.py:538
  16.3 0.1 collective-permute-start.3
  16.6 0.1 mul.35
  16.7 0.1 mul.33
  16.8 0.1 add_bitcast_fusion
  16.9 1.5 %collective-permute-done.3.beside = f32[9,3,32,128]{3,2,1,0:T(8,128)S(1)} collective-permute-done((f32[9,3,32,128]{3,2,1,0:T(8,128)}, f32[9,3,32,128]{3,2,1,0:T(8,128)S(1)}, u32[]{:S(2)}, u32[]{:S(2)}) %collective-permute-start.3) | collective-permute-done | bytes 442400 | tf_op jit(solution)/shard_map/ppermute | solution.py:539
  18.4 1.0 collective-permute-start.8
  19.4 2.3 %collective-permute-start.7 = (f32[8,128]{1,0:T(8,128)S(1)}, f32[8,128]{1,0:T(8,128)S(1)}, u32[]{:S(2)}, u32[]{:S(2)}) collective-permute-start(f32[8,128]{1,0:T(8,128)S(1)} %pad.12), channel_id=1, source_target_pairs={{0,128},{64,192},{128,0},{192,64},{1,129},{65,193},{129,1},{193,65... | collective-permute-start | bytes 12296 | tf_op jit(solution)/shard_map/ppermute | solution.py:519
  21.7 2.8 %collective-permute-start.6 = (f32[8,128]{1,0:T(8,128)S(1)}, f32[8,128]{1,0:T(8,128)S(1)}, u32[]{:S(2)}, u32[]{:S(2)}) collective-permute-start(f32[8,128]{1,0:T(8,128)S(1)} %pad.12), channel_id=1, source_target_pairs={{0,64},{64,128},{128,192},{192,0},{1,65},{65,129},{129,193},{193,1... | collective-permute-start | bytes 12296 | tf_op jit(solution)/shard_map/ppermute | solution.py:519
  24.6 0.1 copy.16
  24.6 0.1 stack_reshape.3
  24.7 9.7 %shard_map.96 = (f32[384,128]{1,0:T(8,128)S(1)}, f32[384,128]{1,0:T(8,128)S(1)}, f32[384,128]{1,0:T(8,128)S(1)}, f32[384,128]{1,0:T(8,128)S(1)}, f32[4,5,256,128]{3,2,1,0:T(8,128)}) custom-call(s32[4]{0:T(128)S(1)} %pad_add_fusion.where, f32[8,3,32,512]{3,2,1,0:T(8,128)S(1)} %copy-done, f32[32,512]{1,0:T(8,128)S(1)} %copy-done.1, ...), custom_call_target="tpu_custom_call" | custom-call | flops 10000000 | bytes 32000000 | tf_op jit(solution)/shard_map/pallas_call | solution.py:41
  34.5 0.3 collective-permute-done.6
  34.7 1.5 %collective-permute-start.9 = (f32[384,128]{1,0:T(8,128)S(1)}, f32[384,128]{1,0:T(8,128)S(1)}, u32[]{:S(2)}, u32[]{:S(2)}) collective-permute-start(f32[384,128]{1,0:T(8,128)S(1)} %get-tuple-element.102), channel_id=1, source_target_pairs={{0,64},{64,128},{128,192},{192,0},{1,65},{65,129},{129,193},{193,1... | collective-permute-start | bytes 589832 | tf_op jit(solution)/shard_map/ppermute | solution.py:519
  36.3 2.0 %collective-permute-start.10 = (f32[384,128]{1,0:T(8,128)S(1)}, f32[384,128]{1,0:T(8,128)S(1)}, u32[]{:S(2)}, u32[]{:S(2)}) collective-permute-start(f32[384,128]{1,0:T(8,128)S(1)} %get-tuple-element.103), channel_id=1, source_target_pairs={{0,128},{64,192},{128,0},{192,64},{1,129},{65,193},{129,1},{193,65... | collective-permute-start | bytes 589832 | tf_op jit(solution)/shard_map/ppermute | solution.py:519
  38.3 0.9 collective-permute-start.11
  39.2 20.8 %conditional.2 = (f32[384,128]{1,0:T(8,128)S(1)}, f32[384,128]{1,0:T(8,128)S(1)}, f32[384,128]{1,0:T(8,128)S(1)}, f32[384,128]{1,0:T(8,128)S(1)}, f32[3,4,128,12...) conditional(s32[]{:T(128)} %convert_element_type.42, () %tuple.27, (s32[]{:T(128)}, f32[4,120,128]{2,1,0:T(8,128)S(1)}, ...), branch_computations={%region_0.1_spmd, %region_1.2_spmd} | conditional | flops 30722 | bytes 1769544 | solution.py:578
  39.2 0.1 collective-permute-start.2
  39.3 1.3 %collective-permute-done.2.corner = f32[2,120,128]{2,1,0:T(8,128)S(1)} collective-permute-done((f32[2,120,128]{2,1,0:T(8,128)S(1)}, f32[2,120,128]{2,1,0:T(8,128)S(1)}, u32[]{:S(2)}, u32[]{:S(2)}) %collective-permute-start.2) | collective-permute-done | bytes 122912 | tf_op jit(solution)/shard_map/cond/branch_1_fun/ppermute | solution.py:565
  40.6 2.9 %branch_1_fun.3 = (f32[384,128]{1,0:T(8,128)S(1)}, f32[384,128]{1,0:T(8,128)S(1)}, f32[384,128]{1,0:T(8,128)S(1)}, f32[384,128]{1,0:T(8,128)S(1)}, f32[96,4,128]...) custom-call(s32[4]{0:T(128)S(1)} %get-tuple-element.24.where, f32[4,5,256,128]{3,2,1,0:T(8,128)} %get-tuple-element.28.inner, ...), custom_call_target="tpu_custom_call" | custom-call | tf_op jit(solution)/shard_map/cond/branch_1_fun/pallas_call | solution.py:41
  43.6 16.4 %all_to_all.4 = f32[96,4,128]{2,1,0:T(4,128)S(1)} all-to-all(f32[96,4,128]{2,1,0:T(4,128)S(1)} %get-tuple-element.42), channel_id=1, replica_groups=mesh['grp'=4,'reg'=8,'sub'=4,'cores'=2] {'grp','sub','cores'}, dimensions={0} | all-to-all | bytes 393216 | tf_op jit(solution)/shard_map/cond/branch_1_fun/all_to_all | solution.py:569
  60.0 1.5 %collective-permute-start.12 = (f32[384,128]{1,0:T(8,128)S(1)}, f32[384,128]{1,0:T(8,128)S(1)}, u32[]{:S(2)}, u32[]{:S(2)}) collective-permute-start(f32[384,128]{1,0:T(8,128)S(1)} %get-tuple-element.107), channel_id=1, source_target_pairs={{0,64},{64,128},{128,192},{192,0},{1,65},{65,129},{129,193},{193,1... | collective-permute-start | bytes 589832 | tf_op jit(solution)/shard_map/ppermute | solution.py:519
  61.5 2.2 %collective-permute-start.13 = (f32[384,128]{1,0:T(8,128)S(1)}, f32[384,128]{1,0:T(8,128)S(1)}, u32[]{:S(2)}, u32[]{:S(2)}) collective-permute-start(f32[384,128]{1,0:T(8,128)S(1)} %get-tuple-element.108), channel_id=1, source_target_pairs={{0,128},{64,192},{128,0},{192,64},{1,129},{65,193},{129,1},{193,65... | collective-permute-start | bytes 589832 | tf_op jit(solution)/shard_map/ppermute | solution.py:519
  63.6 1.7 %collective-permute-start.14 = (f32[384,128]{1,0:T(8,128)S(1)}, f32[384,128]{1,0:T(8,128)S(1)}, u32[]{:S(2)}, u32[]{:S(2)}) collective-permute-start(f32[384,128]{1,0:T(8,128)S(1)} %get-tuple-element.109), channel_id=1, source_target_pairs={{0,192},{64,0},{128,64},{192,128},{1,193},{65,1},{129,65},{193,129... | collective-permute-start | bytes 589832 | tf_op jit(solution)/shard_map/ppermute | solution.py:519
  65.3 13.4 %conditional.3 = (f32[32,32]{1,0:T(8,128)S(1)}) conditional(s32[]{:T(128)} %convert_element_type.42, () %tuple.30, (s32[4]{0:T(128)S(1)}, f32[96,4,128]{2,1,0:T(4,128)S(1)}) %tuple.33), branch_computations={%region_2.3_spmd, %region_3.4_spmd} | conditional | bytes 65624 | solution.py:595
  65.3 1.2 %branch_1_fun.4 = (f32[32,64]{1,0:T(8,128)S(1)}, f32[32,64]{1,0:T(8,128)S(1)}) custom-call(s32[4]{0:T(128)S(1)} %get-tuple-element.43.where, f32[96,4,128]{2,1,0:T(4,128)S(1)} %get-tuple-element.44.states), custom_call_target="tpu_custom_call" | custom-call | tf_op jit(solution)/shard_map/cond/branch_1_fun/pallas_call | solution.py:41
  66.6 4.0 %collective-permute-start = (f32[32,64]{1,0:T(8,128)S(1)}, f32[32,64]{1,0:T(8,128)S(1)}, u32[]{:S(2)}, u32[]{:S(2)}) collective-permute-start(f32[32,64]{1,0:T(8,128)S(1)} %get-tuple-element.46), channel_id=1, source_target_pairs={{0,12},{2,14},{4,8},{6,10},{8,20},{10,22},{12,16},{14,18},{16,28},... | collective-permute-start | bytes 24584 | tf_op jit(solution)/shard_map/cond/branch_1_fun/ppermute | solution.py:588
  70.5 3.8 %collective-permute-done.low = f32[32,64]{1,0:T(8,128)S(1)} collective-permute-done((f32[32,64]{1,0:T(8,128)S(1)}, f32[32,64]{1,0:T(8,128)S(1)}, u32[]{:S(2)}, u32[]{:S(2)}) %collective-permute-start) | collective-permute-done | bytes 8224 | tf_op jit(solution)/shard_map/cond/branch_1_fun/ppermute | solution.py:588
  74.3 1.2 collective-permute-done.1.high
  75.5 3.2 %branch_1_fun.5 = f32[32,32]{1,0:T(8,128)S(1)} custom-call(s32[4]{0:T(128)S(1)} %get-tuple-element.43.where, f32[32,64]{1,0:T(8,128)S(1)} %get-tuple-element.45.own, f32[32,64]{1,0:T(8,128)S(1)} %collective-permute-done.low, f32[32,64]{1,0:T(8,128)S(1)} %collective-permute-done.1.high), custom_call_target="tpu_custom_call" | custom-call | tf_op jit(solution)/shard_map/cond/branch_1_fun/pallas_call | solution.py:41
  78.7 1.0 shard_map.99
  79.7 0.4 collective-permute-start.18
  80.1 2.5 %collective-permute-start.19 = (f32[384,128]{1,0:T(8,128)S(1)}, f32[384,128]{1,0:T(8,128)S(1)}, u32[]{:S(2)}, u32[]{:S(2)}) collective-permute-start(f32[384,128]{1,0:T(8,128)S(1)} %get-tuple-element.117), channel_id=1, source_target_pairs={{0,128},{64,192},{128,0},{192,64},{1,129},{65,193},{129,1},{193,65... | collective-permute-start | bytes 589832 | tf_op jit(solution)/shard_map/ppermute | solution.py:519
  82.7 1.0 shard_map.98
  83.7 2.1 %collective-permute-start.17 = (f32[384,128]{1,0:T(8,128)S(1)}, f32[384,128]{1,0:T(8,128)S(1)}, u32[]{:S(2)}, u32[]{:S(2)}) collective-permute-start(f32[384,128]{1,0:T(8,128)S(1)} %get-tuple-element.113), channel_id=1, source_target_pairs={{0,64},{64,128},{128,192},{192,0},{1,65},{65,129},{129,193},{193,1... | collective-permute-start | bytes 589832 | tf_op jit(solution)/shard_map/ppermute | solution.py:519
  85.8 2.2 %collective-permute-start.15 = (f32[384,128]{1,0:T(8,128)S(1)}, f32[384,128]{1,0:T(8,128)S(1)}, u32[]{:S(2)}, u32[]{:S(2)}) collective-permute-start(f32[384,128]{1,0:T(8,128)S(1)} %get-tuple-element.110), channel_id=1, source_target_pairs={{0,128},{64,192},{128,0},{192,64},{1,129},{65,193},{129,1},{193,65... | collective-permute-start | bytes 589832 | tf_op jit(solution)/shard_map/ppermute | solution.py:519
  87.9 2.1 %collective-permute-start.16 = (f32[384,128]{1,0:T(8,128)S(1)}, f32[384,128]{1,0:T(8,128)S(1)}, u32[]{:S(2)}, u32[]{:S(2)}) collective-permute-start(f32[384,128]{1,0:T(8,128)S(1)} %get-tuple-element.111), channel_id=1, source_target_pairs={{0,192},{64,0},{128,64},{192,128},{1,193},{65,1},{129,65},{193,129... | collective-permute-start | bytes 589832 | tf_op jit(solution)/shard_map/ppermute | solution.py:519
  90.0 3.2 %shard_map.97 = f32[8,3,32,512]{3,2,1,0:T(8,128)} custom-call(s32[4]{0:T(128)S(1)} %pad_add_fusion.where, f32[4,5,256,128]{3,2,1,0:T(8,128)} %get-tuple-element.86.inner, f32[3,4,128,128]{3,2,1,0:T(8,128)S(1)} %get-tuple-element.92.outer), custom_call_target="tpu_custom_call" | custom-call | tf_op jit(solution)/shard_map/pallas_call | solution.py:41
  93.2 4.8 %collective-permute-done.19.refs_2_ = f32[384,128]{1,0:T(8,128)S(1)} collective-permute-done((f32[384,128]{1,0:T(8,128)S(1)}, f32[384,128]{1,0:T(8,128)S(1)}, u32[]{:S(2)}, u32[]{:S(2)}) %collective-permute-start.19) | collective-permute-done | bytes 196640 | tf_op jit(solution)/shard_map/ppermute | solution.py:519
  98.0 10.9 %collective-permute-done.20.refs_3_ = f32[384,128]{1,0:T(8,128)S(1)} collective-permute-done((f32[384,128]{1,0:T(8,128)S(1)}, f32[384,128]{1,0:T(8,128)S(1)}, u32[]{:S(2)}, u32[]{:S(2)}) %collective-permute-start.20) | collective-permute-done | bytes 196640 | tf_op jit(solution)/shard_map/ppermute | solution.py:519
  108.9 1.8 %shard_map.100.refs_2_ = f32[8,3,32,512]{3,2,1,0:T(8,128)} custom-call(s32[4]{0:T(128)S(1)} %pad_add_fusion.where, f32[384,128]{1,0:T(8,128)S(1)} %get-tuple-element.115.refs_0_, f32[384,128]{1,0:T(8,128)S(1)} %collective-permute-done.18.refs_1_, f32[384,128]{1,0:T(8,128)S(1)} %collective-permute-done.19.refs_2_, f32[384,128]{1,0:T(8,128)S(1)} %collective-permute-done.20.refs_3_), custom_call_target="tpu_custom_call" | custom-call | flops 10000000 | bytes 32000000 | tf_op jit(solution)/shard_map/pallas_call | solution.py:41
  110.7 1.3 %shard_map.101.refs_2_ = f32[8,3,32,512]{3,2,1,0:T(8,128)} custom-call(s32[4]{0:T(128)S(1)} %pad_add_fusion.where, f32[384,128]{1,0:T(8,128)S(1)} %get-tuple-element.112.refs_0_, f32[384,128]{1,0:T(8,128)S(1)} %collective-permute-done.17.refs_1_, f32[8,3,32,512]{3,2,1,0:T(8,128)} %shard_map.100.refs_2_), custom_call_target="tpu_custom_call", output_to_operand_aliasing={{}: (3, {})} | custom-call | tf_op jit(solution)/shard_map/pallas_call | solution.py:383
  112.1 2.1 %collective-permute-done.15.refs_0_ = f32[384,128]{1,0:T(8,128)S(1)} collective-permute-done((f32[384,128]{1,0:T(8,128)S(1)}, f32[384,128]{1,0:T(8,128)S(1)}, u32[]{:S(2)}, u32[]{:S(2)}) %collective-permute-start.15) | collective-permute-done | bytes 196640 | tf_op jit(solution)/shard_map/ppermute | solution.py:519
  114.1 3.1 %collective-permute-done.16.refs_1_ = f32[384,128]{1,0:T(8,128)S(1)} collective-permute-done((f32[384,128]{1,0:T(8,128)S(1)}, f32[384,128]{1,0:T(8,128)S(1)}, u32[]{:S(2)}, u32[]{:S(2)}) %collective-permute-start.16) | collective-permute-done | bytes 196640 | tf_op jit(solution)/shard_map/ppermute | solution.py:519
  117.2 1.3 %shard_map.102 = f32[8,3,32,512]{3,2,1,0:T(8,128)} custom-call(s32[4]{0:T(128)S(1)} %pad_add_fusion.where, f32[384,128]{1,0:T(8,128)S(1)} %collective-permute-done.15.refs_0_, f32[384,128]{1,0:T(8,128)S(1)} %collective-permute-done.16.refs_1_, f32[8,3,32,512]{3,2,1,0:T(8,128)} %shard_map.101.refs_2_), custom_call_target="tpu_custom_call", output_to_operand_aliasing={{}: (3, {})} | custom-call | tf_op jit(solution)/shard_map/pallas_call | solution.py:383
  (47 shorter events, 0.3 us)
Async XLA Ops:
  0.6 24.1 %copy-start.1 = (f32[32,512]{1,0:T(8,128)S(1)}, f32[32,512]{1,0:T(8,128)}, u32[]{:S(2)}) copy-start(f32[32,512]{1,0:T(8,128)} %seabed.3) | copy-start | bytes 196612
  0.6 24.1 %copy-start = (f32[8,3,32,512]{3,2,1,0:T(8,128)S(1)}, f32[8,3,32,512]{3,2,1,0:T(8,128)}, u32[]{:S(2)}) copy-start(f32[8,3,32,512]{3,2,1,0:T(8,128)} %trial.3) | copy-start | bytes 4718596
  0.7 15.8 %copy-start.7 = (s32[16,4]{0,1:T(4,128)S(1)}, s32[16,4]{0,1:T(4,128)}, u32[]{:S(2)}) copy-start(s32[16,4]{0,1:T(4,128)} %param.17) | copy-start | bytes 772
  0.7 15.8 %copy-start.6 = (f32[16]{0:T(128)S(1)}, f32[16]{0:T(128)}, u32[]{:S(2)}) copy-start(f32[16]{0:T(128)} %param.15) | copy-start | bytes 196
  0.7 16.0 %copy-start.3 = (s32[16,8]{0,1:T(8,128)S(1)}, s32[16,8]{0,1:T(8,128)}, u32[]{:S(2)}) copy-start(s32[16,8]{0,1:T(8,128)} %param.19) | copy-start | bytes 1540
  0.7 16.0 %copy-start.4 = (f32[16,4]{0,1:T(4,128)S(1)}, f32[16,4]{0,1:T(4,128)}, u32[]{:S(2)}) copy-start(f32[16,4]{0,1:T(4,128)} %param.18) | copy-start | bytes 772
  0.7 16.1 %copy-start.2 = (f32[16,32]{1,0:T(8,128)S(1)}, f32[16,32]{1,0:T(8,128)}, u32[]{:S(2)}) copy-start(f32[16,32]{1,0:T(8,128)} %param.16) | copy-start | bytes 6148
  0.7 16.1 %copy-start.5 = (f32[16]{0:T(128)S(1)}, f32[16]{0:T(128)}, u32[]{:S(2)}) copy-start(f32[16]{0:T(128)} %param.14) | copy-start | bytes 196
  3.5 35.7 %collective-permute-start.4 = (f32[4,120,128]{2,1,0:T(8,128)}, f32[4,120,128]{2,1,0:T(8,128)S(1)}, u32[]{:S(2)}, u32[]{:S(2)}) collective-permute-start(f32[4,120,128]{2,1,0:T(8,128)} %get-tuple-element.87), channel_id=1, source_target_pairs={{0,2},{2,4},{4,6},{6,8},{8,10},{10,12},{12,14},{14,16},{16,18},{18... | collective-permute-start | bytes 737288 | tf_op jit(solution)/shard_map/ppermute | solution.py:537
  11.7 27.5 %collective-permute-start.5 = (f32[4,120,128]{2,1,0:T(8,128)}, f32[4,120,128]{2,1,0:T(8,128)S(1)}, u32[]{:S(2)}, u32[]{:S(2)}) collective-permute-start(f32[4,120,128]{2,1,0:T(8,128)} %get-tuple-element.88), channel_id=1, source_target_pairs={{2,0},{4,2},{6,4},{8,6},{10,8},{12,10},{14,12},{16,14},{18,16},{20... | collective-permute-start | bytes 737288 | tf_op jit(solution)/shard_map/ppermute | solution.py:538
  16.3 2.1 %collective-permute-start.3 = (f32[9,3,32,128]{3,2,1,0:T(8,128)}, f32[9,3,32,128]{3,2,1,0:T(8,128)S(1)}, u32[]{:S(2)}, u32[]{:S(2)}) collective-permute-start(f32[9,3,32,128]{3,2,1,0:T(8,128)} %get-tuple-element.84), channel_id=1, source_target_pairs={{0,1},{1,0},{2,3},{3,2},{4,5},{5,4},{6,7},{7,6},{8,9},{9,8},{10,11... | collective-permute-start | bytes 1327112 | tf_op jit(solution)/shard_map/ppermute | solution.py:539
  18.4 16.0 %collective-permute-start.8 = (f32[8,128]{1,0:T(8,128)S(1)}, f32[8,128]{1,0:T(8,128)S(1)}, u32[]{:S(2)}, u32[]{:S(2)}) collective-permute-start(f32[8,128]{1,0:T(8,128)S(1)} %pad.12), channel_id=1, source_target_pairs={{0,192},{64,0},{128,64},{192,128},{1,193},{65,1},{129,65},{193,129... | collective-permute-start | bytes 12296 | tf_op jit(solution)/shard_map/ppermute | solution.py:519
  19.4 15.0 %collective-permute-start.7 = (f32[8,128]{1,0:T(8,128)S(1)}, f32[8,128]{1,0:T(8,128)S(1)}, u32[]{:S(2)}, u32[]{:S(2)}) collective-permute-start(f32[8,128]{1,0:T(8,128)S(1)} %pad.12), channel_id=1, source_target_pairs={{0,128},{64,192},{128,0},{192,64},{1,129},{65,193},{129,1},{193,65... | collective-permute-start | bytes 12296 | tf_op jit(solution)/shard_map/ppermute | solution.py:519
  21.7 13.0 %collective-permute-start.6 = (f32[8,128]{1,0:T(8,128)S(1)}, f32[8,128]{1,0:T(8,128)S(1)}, u32[]{:S(2)}, u32[]{:S(2)}) collective-permute-start(f32[8,128]{1,0:T(8,128)S(1)} %pad.12), channel_id=1, source_target_pairs={{0,64},{64,128},{128,192},{192,0},{1,65},{65,129},{129,193},{193,1... | collective-permute-start | bytes 12296 | tf_op jit(solution)/shard_map/ppermute | solution.py:519
  34.7 25.2 %collective-permute-start.9 = (f32[384,128]{1,0:T(8,128)S(1)}, f32[384,128]{1,0:T(8,128)S(1)}, u32[]{:S(2)}, u32[]{:S(2)}) collective-permute-start(f32[384,128]{1,0:T(8,128)S(1)} %get-tuple-element.102), channel_id=1, source_target_pairs={{0,64},{64,128},{128,192},{192,0},{1,65},{65,129},{129,193},{193,1... | collective-permute-start | bytes 589832 | tf_op jit(solution)/shard_map/ppermute | solution.py:519
  36.3 23.7 %collective-permute-start.10 = (f32[384,128]{1,0:T(8,128)S(1)}, f32[384,128]{1,0:T(8,128)S(1)}, u32[]{:S(2)}, u32[]{:S(2)}) collective-permute-start(f32[384,128]{1,0:T(8,128)S(1)} %get-tuple-element.103), channel_id=1, source_target_pairs={{0,128},{64,192},{128,0},{192,64},{1,129},{65,193},{129,1},{193,65... | collective-permute-start | bytes 589832 | tf_op jit(solution)/shard_map/ppermute | solution.py:519
  38.3 21.7 %collective-permute-start.11 = (f32[384,128]{1,0:T(8,128)S(1)}, f32[384,128]{1,0:T(8,128)S(1)}, u32[]{:S(2)}, u32[]{:S(2)}) collective-permute-start(f32[384,128]{1,0:T(8,128)S(1)} %get-tuple-element.104), channel_id=1, source_target_pairs={{0,192},{64,0},{128,64},{192,128},{1,193},{65,1},{129,65},{193,129... | collective-permute-start | bytes 589832 | tf_op jit(solution)/shard_map/ppermute | solution.py:519
  39.2 1.4 %collective-permute-start.2 = (f32[2,120,128]{2,1,0:T(8,128)S(1)}, f32[2,120,128]{2,1,0:T(8,128)S(1)}, u32[]{:S(2)}, u32[]{:S(2)}) collective-permute-start(f32[2,120,128]{2,1,0:T(8,128)S(1)} %pad_maximum_fusion), channel_id=1, source_target_pairs={{0,1},{1,0},{2,3},{3,2},{4,5},{5,4},{6,7},{7,6},{8,9},{9,8},{10,11... | collective-permute-start | bytes 368648 | tf_op jit(solution)/shard_map/cond/branch_1_fun/ppermute | solution.py:565
  60.0 22.7 %collective-permute-start.12 = (f32[384,128]{1,0:T(8,128)S(1)}, f32[384,128]{1,0:T(8,128)S(1)}, u32[]{:S(2)}, u32[]{:S(2)}) collective-permute-start(f32[384,128]{1,0:T(8,128)S(1)} %get-tuple-element.107), channel_id=1, source_target_pairs={{0,64},{64,128},{128,192},{192,0},{1,65},{65,129},{129,193},{193,1... | collective-permute-start | bytes 589832 | tf_op jit(solution)/shard_map/ppermute | solution.py:519
  61.5 21.2 %collective-permute-start.13 = (f32[384,128]{1,0:T(8,128)S(1)}, f32[384,128]{1,0:T(8,128)S(1)}, u32[]{:S(2)}, u32[]{:S(2)}) collective-permute-start(f32[384,128]{1,0:T(8,128)S(1)} %get-tuple-element.108), channel_id=1, source_target_pairs={{0,128},{64,192},{128,0},{192,64},{1,129},{65,193},{129,1},{193,65... | collective-permute-start | bytes 589832 | tf_op jit(solution)/shard_map/ppermute | solution.py:519
  63.6 19.0 %collective-permute-start.14 = (f32[384,128]{1,0:T(8,128)S(1)}, f32[384,128]{1,0:T(8,128)S(1)}, u32[]{:S(2)}, u32[]{:S(2)}) collective-permute-start(f32[384,128]{1,0:T(8,128)S(1)} %get-tuple-element.109), channel_id=1, source_target_pairs={{0,192},{64,0},{128,64},{192,128},{1,193},{65,1},{129,65},{193,129... | collective-permute-start | bytes 589832 | tf_op jit(solution)/shard_map/ppermute | solution.py:519
  66.6 7.7 %collective-permute-start = (f32[32,64]{1,0:T(8,128)S(1)}, f32[32,64]{1,0:T(8,128)S(1)}, u32[]{:S(2)}, u32[]{:S(2)}) collective-permute-start(f32[32,64]{1,0:T(8,128)S(1)} %get-tuple-element.46), channel_id=1, source_target_pairs={{0,12},{2,14},{4,8},{6,10},{8,20},{10,22},{12,16},{14,18},{16,28},... | collective-permute-start | bytes 24584 | tf_op jit(solution)/shard_map/cond/branch_1_fun/ppermute | solution.py:588
  74.3 1.2 collective-permute-start.1
  79.7 8.2 %collective-permute-start.18 = (f32[384,128]{1,0:T(8,128)S(1)}, f32[384,128]{1,0:T(8,128)S(1)}, u32[]{:S(2)}, u32[]{:S(2)}) collective-permute-start(f32[384,128]{1,0:T(8,128)S(1)} %get-tuple-element.116), channel_id=1, source_target_pairs={{0,64},{64,128},{128,192},{192,0},{1,65},{65,129},{129,193},{193,1... | collective-permute-start | bytes 589832 | tf_op jit(solution)/shard_map/ppermute | solution.py:519
  80.1 17.8 %collective-permute-start.19 = (f32[384,128]{1,0:T(8,128)S(1)}, f32[384,128]{1,0:T(8,128)S(1)}, u32[]{:S(2)}, u32[]{:S(2)}) collective-permute-start(f32[384,128]{1,0:T(8,128)S(1)} %get-tuple-element.117), channel_id=1, source_target_pairs={{0,128},{64,192},{128,0},{192,64},{1,129},{65,193},{129,1},{193,65... | collective-permute-start | bytes 589832 | tf_op jit(solution)/shard_map/ppermute | solution.py:519
  82.7 26.2 %collective-permute-start.20 = (f32[384,128]{1,0:T(8,128)S(1)}, f32[384,128]{1,0:T(8,128)S(1)}, u32[]{:S(2)}, u32[]{:S(2)}) collective-permute-start(f32[384,128]{1,0:T(8,128)S(1)} %get-tuple-element.118), channel_id=1, source_target_pairs={{0,192},{64,0},{128,64},{192,128},{1,193},{65,1},{129,65},{193,129... | collective-permute-start | bytes 589832 | tf_op jit(solution)/shard_map/ppermute | solution.py:519
  83.7 27.0 %collective-permute-start.17 = (f32[384,128]{1,0:T(8,128)S(1)}, f32[384,128]{1,0:T(8,128)S(1)}, u32[]{:S(2)}, u32[]{:S(2)}) collective-permute-start(f32[384,128]{1,0:T(8,128)S(1)} %get-tuple-element.113), channel_id=1, source_target_pairs={{0,64},{64,128},{128,192},{192,0},{1,65},{65,129},{129,193},{193,1... | collective-permute-start | bytes 589832 | tf_op jit(solution)/shard_map/ppermute | solution.py:519
  85.8 28.4 %collective-permute-start.15 = (f32[384,128]{1,0:T(8,128)S(1)}, f32[384,128]{1,0:T(8,128)S(1)}, u32[]{:S(2)}, u32[]{:S(2)}) collective-permute-start(f32[384,128]{1,0:T(8,128)S(1)} %get-tuple-element.110), channel_id=1, source_target_pairs={{0,128},{64,192},{128,0},{192,64},{1,129},{65,193},{129,1},{193,65... | collective-permute-start | bytes 589832 | tf_op jit(solution)/shard_map/ppermute | solution.py:519
  87.9 29.3 %collective-permute-start.16 = (f32[384,128]{1,0:T(8,128)S(1)}, f32[384,128]{1,0:T(8,128)S(1)}, u32[]{:S(2)}, u32[]{:S(2)}) collective-permute-start(f32[384,128]{1,0:T(8,128)S(1)} %get-tuple-element.111), channel_id=1, source_target_pairs={{0,192},{64,0},{128,64},{192,128},{1,193},{65,1},{129,65},{193,129... | collective-permute-start | bytes 589832 | tf_op jit(solution)/shard_map/ppermute | solution.py:519
